TPU v7x, 32 devices: a whole 2x2x4 slice. The times are simulated.
32 devices in a mesh: ctx: 8 (over y, x, core), fsdp: 4 (over z).
Axes of the slice: x: 2, y: 2, z: 4, core: 2. Of those that a mesh axis runs over, the one named last changes fastest.
Arguments:
- tokens: bfloat16 [4, 1024, 1280], P('fsdp', 'ctx'), may hold values from -6 to 6
- documents: int32 [4, 1024], P('fsdp', 'ctx'), may hold values from 0 to 1, as said below
- routes: int32 [4, 1024, 7], P('fsdp', 'ctx'), may hold values from 0 to 15, all different within a row
- priority: int32 [4, 8, 128], P('fsdp', 'ctx'), may hold values from 0 to 127, each once within a row
- attention_gain: bfloat16 [1280], P('fsdp'), may hold values from 0.5 to 1.5
- query_weight: bfloat16 [1280, 1280], P('fsdp'), may hold values from -0.25 to 0.25
- key_weight: bfloat16 [1280, 1280], P('fsdp'), may hold values from -0.25 to 0.25
- value_weight: bfloat16 [1280, 1280], P('fsdp'), may hold values from -0.15625 to 0.15625
- output_weight: bfloat16 [1280, 1280], P('fsdp'), may hold values from -1.25 to 1.25
- feedforward_gain: bfloat16 [1280], P('fsdp'), may hold values from 0.5 to 1.5
- router_weight: bfloat16 [1280, 16], P('fsdp'), may hold values from -0.078125 to 0.078125
- shared_gate: bfloat16 [1280, 896], P('fsdp'), may hold values from -0.15625 to 0.15625
- shared_up: bfloat16 [1280, 896], P('fsdp'), may hold values from -0.15625 to 0.15625
- shared_down: bfloat16 [896, 1280], P('fsdp'), may hold values from -0.1875 to 0.1875
- expert_gate: bfloat16 [16, 1280, 896], P('ctx', 'fsdp'), may hold values from -0.15625 to 0.15625
- expert_up: bfloat16 [16, 1280, 896], P('ctx', 'fsdp'), may hold values from -0.15625 to 0.15625
- expert_down: bfloat16 [16, 896, 1280], P('ctx', 'fsdp'), may hold values from -2 to 2
- cotangent: bfloat16 [4, 1024, 1280], P('fsdp', 'ctx'), may hold values from -6 to 6
Outputs:
- output: bfloat16 [4, 1024, 1280], P('fsdp', 'ctx')
- grad_tokens: bfloat16 [4, 1024, 1280], P('fsdp', 'ctx')
- grad_attention_gain: float32 [1280], P('fsdp')
- grad_query_weight: float32 [1280, 1280], P('fsdp')
- grad_key_weight: float32 [1280, 1280], P('fsdp')
- grad_value_weight: float32 [1280, 1280], P('fsdp')
- grad_output_weight: float32 [1280, 1280], P('fsdp')
- grad_feedforward_gain: float32 [1280], P('fsdp')
- grad_router_weight: float32 [1280, 16], P('fsdp')
- grad_shared_gate: float32 [1280, 896], P('fsdp')
- grad_shared_up: float32 [1280, 896], P('fsdp')
- grad_shared_down: float32 [896, 1280], P('fsdp')
- grad_expert_gate: float32 [16, 1280, 896], P('ctx', 'fsdp')
- grad_expert_up: float32 [16, 1280, 896], P('ctx', 'fsdp')
- grad_expert_down: float32 [16, 896, 1280], P('ctx', 'fsdp')
Inputs may be any that keep to these rules, and one draw needn't show every extreme that they name: In each packed sequence the documents are 0 up to a boundary and 1 after it, both present; one of the two lies within the first or the last 128 positions. `routes`: each token names 7 different experts. `priority`: each block of 128 tokens holds every number once.
All inputs are finite; a program needn't handle non-finite values.
Results may differ from a plain program's by a relative error of at most 0.025.
Values may be sent and summed in bfloat16 or wider, within the bound.
A program may use at most 320 MiB of HBM per device.

v0:
```python
import math

import jax
import jax.numpy as jnp
from jax import lax
from jax.sharding import PartitionSpec as P

D = 1280
HEADS = 10
HEAD_DIM = 128
TOPK = 7
EXP_DEV = 2


epsilon = 1e-06
theta_base = 10000.0
negative = -1e30
highest = lax.Precision.HIGHEST


def rotary_tables(positions, half_dim):
    frequency = theta_base ** (-jnp.arange(half_dim, dtype=jnp.float32) / half_dim)
    angles = positions.astype(jnp.float32)[:, None] * frequency[None, :]
    return (jnp.cos(angles)[:, None, :], jnp.sin(angles)[:, None, :])


def rotate(values, cosine, sine):
    half_dim = values.shape[-1] // 2
    leading = values[..., :half_dim]
    trailing = values[..., half_dim:]
    return jnp.concatenate(
        [leading * cosine - trailing * sine, trailing * cosine + leading * sine], axis=-1
    )


def unrotate(values, cosine, sine):
    half_dim = values.shape[-1] // 2
    leading = values[..., :half_dim]
    trailing = values[..., half_dim:]
    return jnp.concatenate(
        [leading * cosine + trailing * sine, trailing * cosine - leading * sine], axis=-1
    )


def blockwise(count, visit, initial):
    rows_each = math.gcd(count, 512)

    def advance(progress, number):
        return (visit(progress, number * rows_each, rows_each), None)

    final, ignored = lax.scan(advance, initial, jnp.arange(count // rows_each, dtype=jnp.int32))
    return final


def allowed_mask(query_pos, query_docs, key_pos, key_docs):
    return (key_pos[None, :] <= query_pos[:, None]) & (key_docs[None, :] == query_docs[:, None])


def rms_factor(values):
    return lax.rsqrt(jnp.mean(values * values, axis=-1, keepdims=True) + epsilon)


def silu_parts(values):
    sigma = jax.nn.sigmoid(values)
    return (values * sigma, sigma * (1.0 + values * (1.0 - sigma)))


def unchanged(progress):
    return progress


def per_device(
    tokens,
    documents,
    routes,
    priority,
    attention_gain,
    query_weight,
    key_weight,
    value_weight,
    output_weight,
    feedforward_gain,
    router_weight,
    shared_gate,
    shared_up,
    shared_down,
    expert_gate,
    expert_up,
    expert_down,
    cotangent,
):
    gathered = (
        lax.all_gather(attention_gain, "fsdp", axis=0, tiled=True),
        lax.all_gather(query_weight, "fsdp", axis=0, tiled=True),
        lax.all_gather(key_weight, "fsdp", axis=0, tiled=True),
        lax.all_gather(value_weight, "fsdp", axis=0, tiled=True),
        lax.all_gather(output_weight, "fsdp", axis=0, tiled=True),
        lax.all_gather(feedforward_gain, "fsdp", axis=0, tiled=True),
        lax.all_gather(router_weight, "fsdp", axis=0, tiled=True),
        lax.all_gather(shared_gate, "fsdp", axis=0, tiled=True),
        lax.all_gather(shared_up, "fsdp", axis=0, tiled=True),
        lax.all_gather(shared_down, "fsdp", axis=0, tiled=True),
        lax.all_gather(expert_gate, "fsdp", axis=1, tiled=True),
        lax.all_gather(expert_up, "fsdp", axis=1, tiled=True),
        lax.all_gather(expert_down, "fsdp", axis=1, tiled=True),
    )
    (
        gain_one,
        w_query,
        w_key,
        w_value,
        w_output,
        gain_two,
        w_router,
        w_shared_gate,
        w_shared_up,
        w_shared_down,
        w_expert_gate,
        w_expert_up,
        w_expert_down,
    ) = gathered
    groups = lax.axis_size("ctx")
    length = tokens.shape[1]
    row_length = length * groups
    experts = EXP_DEV * groups
    capacity = 9 * length * TOPK // (8 * experts)
    inner_width = HEADS * HEAD_DIM
    score_scale = HEAD_DIM ** (-0.5)
    spare_slot = experts * capacity
    first_here = lax.axis_index("ctx") * length
    positions = first_here + jnp.arange(length, dtype=jnp.int32)
    last_here = first_here + length - 1
    doc_here = documents[0].astype(jnp.float32)
    doc_wire = documents[0].astype(jnp.bfloat16)
    inputs = tokens[0].astype(jnp.float32)
    upstream_low = cotangent[0]
    upstream = upstream_low.astype(jnp.float32)
    factor_one = rms_factor(inputs)
    normed_one = inputs * factor_one
    gain_one_wide = gain_one.astype(jnp.float32)
    attn_input = (normed_one * gain_one_wide).astype(jnp.bfloat16)
    query_pre = jnp.dot(attn_input, w_query, preferred_element_type=jnp.float32).reshape(
        length, HEADS, HEAD_DIM
    )
    key_pre = jnp.dot(attn_input, w_key, preferred_element_type=jnp.float32).reshape(
        length, HEADS, HEAD_DIM
    )
    cosine, sine = rotary_tables(positions, HEAD_DIM // 2)
    queries = rotate(query_pre, cosine, sine).astype(jnp.bfloat16)
    key_rows = rotate(key_pre, cosine, sine).astype(jnp.bfloat16)
    value_rows = (
        jnp.dot(attn_input, w_value, preferred_element_type=jnp.float32)
        .astype(jnp.bfloat16)
        .reshape(length, HEADS, HEAD_DIM)
    )
    initial = (
        jnp.zeros((HEADS, length, HEAD_DIM), jnp.float32),
        jnp.full((HEADS, length), negative, jnp.float32),
        jnp.zeros((HEADS, length), jnp.float32),
    )
    key_all = lax.all_gather(key_rows, "ctx", axis=0, tiled=True)
    value_all = lax.all_gather(value_rows, "ctx", axis=0, tiled=True)
    docs_all = lax.all_gather(doc_wire, "ctx", axis=0, tiled=True)

    def visit(progress, within, rows_now):

        def compute(progress):
            accum, highest_seen, totals = progress
            key_block = lax.dynamic_slice_in_dim(key_all, within, rows_now, 0)
            value_block = lax.dynamic_slice_in_dim(value_all, within, rows_now, 0)
            docs_block = lax.dynamic_slice_in_dim(docs_all, within, rows_now, 0).astype(jnp.float32)
            key_pos = within + jnp.arange(rows_now, dtype=jnp.int32)
            allowed = allowed_mask(positions, doc_here, key_pos, docs_block)[None]
            scores = jnp.einsum(
                "qhd,khd->hqk", queries, key_block, preferred_element_type=jnp.float32
            )
            scores = jnp.where(allowed, scores * score_scale, negative)
            newest = jnp.maximum(highest_seen, jnp.max(scores, axis=-1))
            shrink = jnp.exp(highest_seen - newest)
            shares = jnp.exp(scores - newest[..., None]) * allowed
            totals = totals * shrink + jnp.sum(shares, axis=-1)
            accum = accum * shrink[..., None] + jnp.einsum(
                "hqk,khd->hqd",
                shares.astype(jnp.bfloat16),
                value_block,
                preferred_element_type=jnp.float32,
            )
            return (accum, newest, totals)

        return lax.cond(within > last_here, unchanged, compute, progress)

    accum, highest_seen, totals = blockwise(key_all.shape[0], visit, initial)
    attended = accum / totals[..., None]
    log_total = highest_seen + jnp.log(totals)
    mixed_rows = (
        jnp.transpose(attended, (1, 0, 2)).reshape(length, inner_width).astype(jnp.bfloat16)
    )
    hidden = inputs + jnp.dot(mixed_rows, w_output, preferred_element_type=jnp.float32)
    factor_two = rms_factor(hidden)
    normed_two = hidden * factor_two
    gain_two_wide = gain_two.astype(jnp.float32)
    moe_input = (normed_two * gain_two_wide).astype(jnp.bfloat16)
    moe_wide = moe_input.astype(jnp.float32)
    router_wide = w_router.astype(jnp.float32)
    gate_probs = jax.nn.softmax(jnp.dot(moe_wide, router_wide, precision=highest), axis=-1)
    route_now = routes[0]
    order_now = priority[0, 0]
    onehot = (route_now[:, :, None] == jnp.arange(experts, dtype=jnp.int32)).astype(jnp.float32)
    counts = jnp.sum(onehot, axis=1)
    earlier = (order_now[None, :] < order_now[:, None]).astype(jnp.bfloat16)
    before = jnp.dot(earlier, counts.astype(jnp.bfloat16), preferred_element_type=jnp.float32)
    ranking = jnp.sum(onehot * before[:, None, :], axis=-1).astype(jnp.int32)
    kept_mask = ranking < capacity
    slot_index = jnp.where(
        kept_mask,
        route_now % EXP_DEV * (groups * capacity) + route_now // EXP_DEV * capacity + ranking,
        spare_slot,
    )
    chosen = jnp.sum(onehot * gate_probs[:, None, :], axis=-1)
    weight = jnp.where(kept_mask, chosen, 0.0)
    flat_slots = slot_index.reshape(-1)
    copies = jnp.broadcast_to(moe_input[:, None, :], (length, TOPK, D)).reshape(length * TOPK, D)
    outgoing = jnp.zeros((spare_slot + 1, D), jnp.bfloat16).at[flat_slots].set(copies)[:spare_slot]
    arrived = lax.all_to_all(
        outgoing.reshape(EXP_DEV, groups, capacity, D),
        "ctx",
        split_axis=1,
        concat_axis=1,
        tiled=True,
    ).reshape(EXP_DEV, groups * capacity, D)
    gate_act = jnp.einsum(
        "erd,edf->erf", arrived, w_expert_gate, preferred_element_type=jnp.float32
    )
    up_act = jnp.einsum("erd,edf->erf", arrived, w_expert_up, preferred_element_type=jnp.float32)
    silu_gate, slope_gate = silu_parts(gate_act)
    expert_hidden = (silu_gate * up_act).astype(jnp.bfloat16)
    expert_out = jnp.einsum(
        "erf,efd->erd", expert_hidden, w_expert_down, preferred_element_type=jnp.float32
    ).astype(jnp.bfloat16)
    returned = lax.all_to_all(
        expert_out.reshape(EXP_DEV, groups, capacity, D),
        "ctx",
        split_axis=1,
        concat_axis=1,
        tiled=True,
    ).reshape(spare_slot, D)
    returned = jnp.concatenate([returned, jnp.zeros((1, D), jnp.bfloat16)], axis=0)
    picked = returned[slot_index]
    routed = jnp.sum(weight[..., None] * picked, axis=1)
    shared_gate_act = jnp.dot(moe_input, w_shared_gate, preferred_element_type=jnp.float32)
    shared_up_act = jnp.dot(moe_input, w_shared_up, preferred_element_type=jnp.float32)
    silu_shared, slope_shared = silu_parts(shared_gate_act)
    shared_hidden = (silu_shared * shared_up_act).astype(jnp.bfloat16)
    shared_out = jnp.dot(shared_hidden, w_shared_down, preferred_element_type=jnp.float32)
    output_rows = (hidden + shared_out + routed).astype(jnp.bfloat16)
    grad_shared_down = jnp.dot(shared_hidden.T, upstream_low, preferred_element_type=jnp.float32)
    grad_shared_hidden = jnp.dot(upstream_low, w_shared_down.T, preferred_element_type=jnp.float32)
    grad_shared_gate_act = (grad_shared_hidden * shared_up_act * slope_shared).astype(jnp.bfloat16)
    grad_shared_up_act = (grad_shared_hidden * silu_shared).astype(jnp.bfloat16)
    grad_shared_gate = jnp.dot(
        moe_input.T, grad_shared_gate_act, preferred_element_type=jnp.float32
    )
    grad_shared_up = jnp.dot(moe_input.T, grad_shared_up_act, preferred_element_type=jnp.float32)
    grad_moe = jnp.dot(
        grad_shared_gate_act, w_shared_gate.T, preferred_element_type=jnp.float32
    ) + jnp.dot(grad_shared_up_act, w_shared_up.T, preferred_element_type=jnp.float32)
    grad_copies = (
        (weight[..., None] * upstream[:, None, :]).astype(jnp.bfloat16).reshape(length * TOPK, D)
    )
    grad_weight = jnp.sum(picked.astype(jnp.float32) * upstream[:, None, :], axis=-1)
    grad_outgoing = (
        jnp.zeros((spare_slot + 1, D), jnp.bfloat16).at[flat_slots].set(grad_copies)[:spare_slot]
    )
    grad_arrived = lax.all_to_all(
        grad_outgoing.reshape(EXP_DEV, groups, capacity, D),
        "ctx",
        split_axis=1,
        concat_axis=1,
        tiled=True,
    ).reshape(EXP_DEV, groups * capacity, D)
    grad_expert_hidden = jnp.einsum(
        "erd,efd->erf", grad_arrived, w_expert_down, preferred_element_type=jnp.float32
    )
    grad_expert_down = jnp.einsum(
        "erf,erd->efd", expert_hidden, grad_arrived, preferred_element_type=jnp.float32
    )
    grad_gate_act = (grad_expert_hidden * up_act * slope_gate).astype(jnp.bfloat16)
    grad_up_act = (grad_expert_hidden * silu_gate).astype(jnp.bfloat16)
    grad_expert_gate = jnp.einsum(
        "erd,erf->edf", arrived, grad_gate_act, preferred_element_type=jnp.float32
    )
    grad_expert_up = jnp.einsum(
        "erd,erf->edf", arrived, grad_up_act, preferred_element_type=jnp.float32
    )
    grad_arrived_in = (
        jnp.einsum("erf,edf->erd", grad_gate_act, w_expert_gate, preferred_element_type=jnp.float32)
        + jnp.einsum("erf,edf->erd", grad_up_act, w_expert_up, preferred_element_type=jnp.float32)
    ).astype(jnp.bfloat16)
    sent_back = lax.all_to_all(
        grad_arrived_in.reshape(EXP_DEV, groups, capacity, D),
        "ctx",
        split_axis=1,
        concat_axis=1,
        tiled=True,
    ).reshape(spare_slot, D)
    sent_back = jnp.concatenate([sent_back, jnp.zeros((1, D), jnp.bfloat16)], axis=0)
    grad_moe = grad_moe + jnp.sum(sent_back[slot_index].astype(jnp.float32), axis=1)
    grad_chosen = jnp.where(kept_mask, grad_weight, 0.0)
    grad_probs = jnp.sum(onehot * grad_chosen[..., None], axis=1)
    grad_logits = gate_probs * (
        grad_probs - jnp.sum(gate_probs * grad_probs, axis=-1, keepdims=True)
    )
    grad_router = jnp.dot(moe_wide.T, grad_logits, precision=highest)
    grad_moe = grad_moe + jnp.dot(grad_logits, router_wide.T, precision=highest)
    grad_gain_two = jnp.sum(grad_moe * normed_two, axis=0)
    scaled_two = grad_moe * gain_two_wide
    grad_hidden = upstream + factor_two * (
        scaled_two - normed_two * jnp.mean(scaled_two * normed_two, axis=-1, keepdims=True)
    )
    grad_hidden_low = grad_hidden.astype(jnp.bfloat16)
    grad_output = jnp.dot(mixed_rows.T, grad_hidden_low, preferred_element_type=jnp.float32)
    grad_mixed = (
        jnp.dot(grad_hidden_low, w_output.T, preferred_element_type=jnp.float32)
        .astype(jnp.bfloat16)
        .reshape(length, HEADS, HEAD_DIM)
    )
    delta = jnp.einsum("qhd,hqd->hq", grad_mixed.astype(jnp.float32), attended)
    start_state = (
        jnp.zeros((length, HEADS, HEAD_DIM), jnp.float32),
        jnp.zeros((row_length, 2 * inner_width), jnp.float32),
    )
    back_key_all = lax.all_gather(key_rows, "ctx", axis=0, tiled=True)
    back_value_all = lax.all_gather(value_rows, "ctx", axis=0, tiled=True)
    back_docs_all = lax.all_gather(doc_wire, "ctx", axis=0, tiled=True)

    def visit(progress, within, rows_now):
        first_row = within

        def compute(progress):
            grad_query_acc, grad_kv_all = progress
            key_block = lax.dynamic_slice_in_dim(back_key_all, within, rows_now, 0)
            value_block = lax.dynamic_slice_in_dim(back_value_all, within, rows_now, 0)
            docs_block = lax.dynamic_slice_in_dim(back_docs_all, within, rows_now, 0).astype(
                jnp.float32
            )
            key_pos = first_row + jnp.arange(rows_now, dtype=jnp.int32)
            allowed = allowed_mask(positions, doc_here, key_pos, docs_block)[None]
            scores = jnp.einsum(
                "qhd,khd->hqk", queries, key_block, preferred_element_type=jnp.float32
            )
            scores = jnp.where(allowed, scores * score_scale, negative)
            shares = jnp.exp(scores - log_total[..., None]) * allowed
            grad_shares = jnp.einsum(
                "qhd,khd->hqk", grad_mixed, value_block, preferred_element_type=jnp.float32
            )
            grad_scores = (shares * (grad_shares - delta[..., None]) * score_scale).astype(
                jnp.bfloat16
            )
            grad_query_acc = grad_query_acc + jnp.einsum(
                "hqk,khd->qhd", grad_scores, key_block, preferred_element_type=jnp.float32
            )
            grad_key_rows = jnp.einsum(
                "hqk,qhd->khd", grad_scores, queries, preferred_element_type=jnp.float32
            ).reshape(rows_now, inner_width)
            grad_value_rows = jnp.einsum(
                "hqk,qhd->khd",
                shares.astype(jnp.bfloat16),
                grad_mixed,
                preferred_element_type=jnp.float32,
            ).reshape(rows_now, inner_width)
            current = lax.dynamic_slice_in_dim(grad_kv_all, first_row, rows_now, 0)
            grad_kv_all = lax.dynamic_update_slice_in_dim(
                grad_kv_all,
                current + jnp.concatenate([grad_key_rows, grad_value_rows], axis=1),
                first_row,
                0,
            )
            return (grad_query_acc, grad_kv_all)

        return lax.cond(first_row > last_here, unchanged, compute, progress)

    grad_query, grad_kv_all = blockwise(back_key_all.shape[0], visit, start_state)
    grad_kv = lax.psum_scatter(
        grad_kv_all.astype(jnp.bfloat16), "ctx", scatter_dimension=0, tiled=True
    ).astype(jnp.float32)
    grad_query_low = (
        unrotate(grad_query.astype(jnp.bfloat16).astype(jnp.float32), cosine, sine)
        .astype(jnp.bfloat16)
        .reshape(length, inner_width)
    )
    grad_key_turned = (
        grad_kv[:, :inner_width]
        .reshape(length, HEADS, HEAD_DIM)
        .astype(jnp.bfloat16)
        .astype(jnp.float32)
    )
    grad_key_low = (
        unrotate(grad_key_turned, cosine, sine).astype(jnp.bfloat16).reshape(length, inner_width)
    )
    grad_value_low = grad_kv[:, inner_width:].astype(jnp.bfloat16)
    grad_wquery = jnp.dot(attn_input.T, grad_query_low, preferred_element_type=jnp.float32)
    grad_wkey = jnp.dot(attn_input.T, grad_key_low, preferred_element_type=jnp.float32)
    grad_wvalue = jnp.dot(attn_input.T, grad_value_low, preferred_element_type=jnp.float32)
    grad_attn = (
        jnp.dot(grad_query_low, w_query.T, preferred_element_type=jnp.float32)
        + jnp.dot(grad_key_low, w_key.T, preferred_element_type=jnp.float32)
        + jnp.dot(grad_value_low, w_value.T, preferred_element_type=jnp.float32)
    )
    grad_gain_one = jnp.sum(grad_attn * normed_one, axis=0)
    scaled_one = grad_attn * gain_one_wide
    grad_inputs = grad_hidden + factor_one * (
        scaled_one - normed_one * jnp.mean(scaled_one * normed_one, axis=-1, keepdims=True)
    )
    owned = (
        lax.psum_scatter(
            grad_gain_one.astype(jnp.bfloat16), "fsdp", scatter_dimension=0, tiled=True
        ).astype(jnp.float32),
        lax.psum_scatter(
            grad_wquery.astype(jnp.bfloat16), "fsdp", scatter_dimension=0, tiled=True
        ).astype(jnp.float32),
        lax.psum_scatter(
            grad_wkey.astype(jnp.bfloat16), "fsdp", scatter_dimension=0, tiled=True
        ).astype(jnp.float32),
        lax.psum_scatter(
            grad_wvalue.astype(jnp.bfloat16), "fsdp", scatter_dimension=0, tiled=True
        ).astype(jnp.float32),
        lax.psum_scatter(
            grad_output.astype(jnp.bfloat16), "fsdp", scatter_dimension=0, tiled=True
        ).astype(jnp.float32),
        lax.psum_scatter(
            grad_gain_two.astype(jnp.bfloat16), "fsdp", scatter_dimension=0, tiled=True
        ).astype(jnp.float32),
        lax.psum_scatter(
            grad_router.astype(jnp.bfloat16), "fsdp", scatter_dimension=0, tiled=True
        ).astype(jnp.float32),
        lax.psum_scatter(
            grad_shared_gate.astype(jnp.bfloat16), "fsdp", scatter_dimension=0, tiled=True
        ).astype(jnp.float32),
        lax.psum_scatter(
            grad_shared_up.astype(jnp.bfloat16), "fsdp", scatter_dimension=0, tiled=True
        ).astype(jnp.float32),
        lax.psum_scatter(
            grad_shared_down.astype(jnp.bfloat16), "fsdp", scatter_dimension=0, tiled=True
        ).astype(jnp.float32),
        lax.psum_scatter(
            grad_expert_gate.astype(jnp.bfloat16), "fsdp", scatter_dimension=1, tiled=True
        ).astype(jnp.float32),
        lax.psum_scatter(
            grad_expert_up.astype(jnp.bfloat16), "fsdp", scatter_dimension=1, tiled=True
        ).astype(jnp.float32),
        lax.psum_scatter(
            grad_expert_down.astype(jnp.bfloat16), "fsdp", scatter_dimension=1, tiled=True
        ).astype(jnp.float32),
    )
    (
        own_gain_one,
        own_wquery,
        own_wkey,
        own_wvalue,
        own_output,
        own_gain_two,
        own_router,
        own_shared_gate,
        own_shared_up,
        own_shared_down,
        own_expert_gate,
        own_expert_up,
        own_expert_down,
    ) = owned
    dense = (
        lax.psum(own_gain_one.astype(jnp.bfloat16), "ctx").astype(jnp.float32),
        lax.psum(own_wquery.astype(jnp.bfloat16), "ctx").astype(jnp.float32),
        lax.psum(own_wkey.astype(jnp.bfloat16), "ctx").astype(jnp.float32),
        lax.psum(own_wvalue.astype(jnp.bfloat16), "ctx").astype(jnp.float32),
        lax.psum(own_output.astype(jnp.bfloat16), "ctx").astype(jnp.float32),
        lax.psum(own_gain_two.astype(jnp.bfloat16), "ctx").astype(jnp.float32),
        lax.psum(own_router.astype(jnp.bfloat16), "ctx").astype(jnp.float32),
        lax.psum(own_shared_gate.astype(jnp.bfloat16), "ctx").astype(jnp.float32),
        lax.psum(own_shared_up.astype(jnp.bfloat16), "ctx").astype(jnp.float32),
        lax.psum(own_shared_down.astype(jnp.bfloat16), "ctx").astype(jnp.float32),
    )
    return (
        output_rows[None],
        grad_inputs.astype(jnp.bfloat16)[None],
        dense[0],
        dense[1],
        dense[2],
        dense[3],
        dense[4],
        dense[5],
        dense[6],
        dense[7],
        dense[8],
        dense[9],
        own_expert_gate,
        own_expert_up,
        own_expert_down,
    )


def solution(mesh):
    return jax.shard_map(
        per_device,
        mesh=mesh,
        in_specs=(
            P("fsdp", "ctx", None),
            P("fsdp", "ctx"),
            P("fsdp", "ctx", None),
            P("fsdp", "ctx", None),
            P("fsdp"),
            P("fsdp", None),
            P("fsdp", None),
            P("fsdp", None),
            P("fsdp", None),
            P("fsdp"),
            P("fsdp", None),
            P("fsdp", None),
            P("fsdp", None),
            P("fsdp", None),
            P("ctx", "fsdp", None),
            P("ctx", "fsdp", None),
            P("ctx", "fsdp", None),
            P("fsdp", "ctx", None),
        ),
        out_specs=(
            P("fsdp", "ctx", None),
            P("fsdp", "ctx", None),
            P("fsdp"),
            P("fsdp", None),
            P("fsdp", None),
            P("fsdp", None),
            P("fsdp", None),
            P("fsdp"),
            P("fsdp", None),
            P("fsdp", None),
            P("fsdp", None),
            P("fsdp", None),
            P("ctx", "fsdp", None),
            P("ctx", "fsdp", None),
            P("ctx", "fsdp", None),
        ),
        check_vma=False,
    )
```

profile of v0, /device:TPU:21, one launch (start us, length us, event | category | flops | bytes accessed | tf_op | source)
XLA Modules:
  0.0 1761.3 jit_solution(1658939904572489490)
XLA Ops:
  20.8 54.2 %all-gather.19.cloned.1.call-done = bf16[1280,1280]{1,0:T(8,128)(2,1)} async-done(((bf16[320,1280]{1,0:T(8,128)(2,1)}), bf16[1280,1280]{1,0:T(8,128)(2,1)}) %all-gather.19.cloned.1.call-update) | async-done | bytes 3276816 | tf_op jit(solution)/shard_map/all_gather | solution.py:94
  80.6 60.3 %all-gather.15.cloned.1.call-done = bf16[1280,1280]{1,0:T(8,128)(2,1)} async-done(((bf16[320,1280]{1,0:T(8,128)(2,1)}), bf16[1280,1280]{1,0:T(8,128)(2,1)}) %all-gather.15.cloned.1.call-update) | async-done | bytes 3276816 | tf_op jit(solution)/shard_map/all_gather | solution.py:95
  151.8 55.0 %all-gather.21.cloned.1.call-done = bf16[1280,1280]{1,0:T(8,128)(2,1)} async-done(((bf16[320,1280]{1,0:T(8,128)(2,1)}), bf16[1280,1280]{1,0:T(8,128)(2,1)}) %all-gather.21.cloned.1.call-update) | async-done | bytes 3276816 | tf_op jit(solution)/shard_map/all_gather | solution.py:96
  244.1 28.4 %all-gather.23.cloned.1.call-done = bf16[1024,10,128]{0,2,1:T(8,128)(2,1)} async-done(((bf16[128,10,128]{0,2,1:T(8,128)(2,1)}), bf16[1024,10,128]{0,2,1:T(8,128)(2,1)}) %all-gather.23.cloned.1.call-update) | async-done | bytes 2621456 | tf_op jit(solution)/shard_map/all_gather | solution.py:162
  277.0 12.1 while.28
  289.5 48.7 %all-gather.25.cloned.1.call-done = bf16[1280,1280]{1,0:T(8,128)(2,1)} async-done(((bf16[320,1280]{1,0:T(8,128)(2,1)}), bf16[1280,1280]{1,0:T(8,128)(2,1)}) %all-gather.25.cloned.1.call-update) | async-done | bytes 3276816 | tf_op jit(solution)/shard_map/all_gather | solution.py:97
  382.6 11.5 scatter_custom_fusion.1
  409.9 15.6 all-gather.33.cloned.1.call-done
  433.3 79.5 %all-gather.35.cloned.1.call-done = bf16[2,1280,896]{2,1,0:T(8,128)(2,1)} async-done(((bf16[2,320,896]{2,1,0:T(8,128)(2,1)}), bf16[2,1280,896]{2,1,0:T(8,128)(2,1)}) %all-gather.35.cloned.1.call-update) | async-done | bytes 4587536 | tf_op jit(solution)/shard_map/all_gather | solution.py:104
  520.5 79.7 %all-gather.37.cloned.1.call-done = bf16[2,896,1280]{2,1,0:T(8,128)(2,1)} async-done(((bf16[2,224,1280]{2,1,0:T(8,128)(2,1)}), bf16[2,896,1280]{2,1,0:T(8,128)(2,1)}) %all-gather.37.cloned.1.call-update) | async-done | bytes 4587536 | tf_op jit(solution)/shard_map/all_gather | solution.py:105
  636.4 12.6 all-to-all-done.1
  660.5 39.2 %all-gather.29.cloned.1.call-done = bf16[1280,896]{1,0:T(8,128)(2,1)} async-done(((bf16[320,896]{1,0:T(8,128)(2,1)}), bf16[1280,896]{1,0:T(8,128)(2,1)}) %all-gather.29.cloned.1.call-update) | async-done | bytes 2293776 | tf_op jit(solution)/shard_map/all_gather | solution.py:101
  702.6 46.8 %all-gather.31.cloned.1.call-done = bf16[896,1280]{1,0:T(8,128)(2,1)} async-done(((bf16[224,1280]{1,0:T(8,128)(2,1)}), bf16[896,1280]{1,0:T(8,128)(2,1)}) %all-gather.31.cloned.1.call-update) | async-done | bytes 2293776 | tf_op jit(solution)/shard_map/all_gather | solution.py:102
  811.5 80.1 %while.29 = (s32[]{:T(128)}, f32[128,10,128]{0,2,1:T(8,128)S(1)}, f32[1024,2560]{0,1:T(8,128)}, s32[2]{0:T(128)S(1)}, s32[]{:T(128)}, /*index=5*/bf16[1024,10,12...) while((s32[]{:T(128)}, f32[128,10,128]{0,2,1:T(8,128)S(1)}, ...), condition=%wide.region_24.25_spmd.clone, body=%wide.region_21.24_spmd.clone.sunk | while | flops 850429056 | bytes 92767216 | solution.py:51
  813.0 39.1 %conditional.7 = ((f32[128,10,128]{0,2,1:T(8,128)S(1)}, f32[1024,2560]{0,1:T(8,128)})) conditional(s32[]{:T(128)} %convert_element_type.557, (s32[]{:T(128)}, bf16[1024,10,128]{2,0,1:T(8,128)(2,1)}, s32[]{:T(128)}, bf16[1024]{0:T(1024)(128)(2,1)S(1)}, f32[128]{0:T(128)S(1)}, /*index=5*/bf16[128,10,128]{0,2,1:T(8,128)(2,1)S(1)}, ...), branch_computations={%region_22.22_spmd, %region_23.23_spmd} | conditional | flops 850429056 | bytes 92766392 | solution.py:380
  826.7 25.4 %dynamic_update_slice.2 = f32[1024,2560]{0,1:T(8,128)} dynamic-update-slice(f32[1024,2560]{0,1:T(8,128)} %get-tuple-element.195, f32[512,2560]{0,1:T(8,128)} %maximum_add_fusion, s32[]{:T(128)S(6)} %select_n.114, s32[]{:T(128)} %constant.53.clone) | dynamic-update-slice | bytes 10485764 | tf_op jit(solution)/shard_map/while/body/eval_jaxpr/cond/branch_0_fun/dynamic_update_slice | solution.py:372
  853.4 38.2 %conditional.7 = ((f32[128,10,128]{0,2,1:T(8,128)S(1)}, f32[1024,2560]{0,1:T(8,128)})) conditional(s32[]{:T(128)} %convert_element_type.557, (s32[]{:T(128)}, bf16[1024,10,128]{2,0,1:T(8,128)(2,1)}, s32[]{:T(128)}, bf16[1024]{0:T(1024)(128)(2,1)S(1)}, f32[128]{0:T(128)S(1)}, /*index=5*/bf16[128,10,128]{0,2,1:T(8,128)(2,1)S(1)}, ...), branch_computations={%region_22.22_spmd, %region_23.23_spmd} | conditional | flops 850429056 | bytes 92766392 | solution.py:380
  867.1 24.5 %dynamic_update_slice.2 = f32[1024,2560]{0,1:T(8,128)} dynamic-update-slice(f32[1024,2560]{0,1:T(8,128)} %get-tuple-element.195, f32[512,2560]{0,1:T(8,128)} %maximum_add_fusion, s32[]{:T(128)S(6)} %select_n.114, s32[]{:T(128)} %constant.53.clone) | dynamic-update-slice | bytes 10485764 | tf_op jit(solution)/shard_map/while/body/eval_jaxpr/cond/branch_0_fun/dynamic_update_slice | solution.py:372
  916.6 46.8 %reduce-scatter.37.cloned.1.call-done = bf16[128,2560]{1,0:T(8,128)(2,1)} async-done(((bf16[1024,2560]{1,0:T(8,128)(2,1)}), bf16[128,2560]{1,0:T(8,128)(2,1)}) %reduce-scatter.37.cloned.1.call-update) | async-done | bytes 655376
  999.4 13.5 reduce-scatter.25.cloned.1.call-done
  1012.9 49.2 %reduce-scatter.27.cloned.1.call-done = bf16[320,896]{1,0:T(8,128)(2,1)} async-done(((bf16[1280,896]{1,0:T(8,128)(2,1)}), bf16[320,896]{1,0:T(8,128)(2,1)}) %reduce-scatter.27.cloned.1.call-update) | async-done | bytes 573456 | tf_op jit(solution)/shard_map/reduce_scatter | solution.py:439
  1062.1 49.4 %reduce-scatter.29.cloned.1.call-done = bf16[224,1280]{1,0:T(8,128)(2,1)} async-done(((bf16[896,1280]{1,0:T(8,128)(2,1)}), bf16[224,1280]{1,0:T(8,128)(2,1)}) %reduce-scatter.29.cloned.1.call-update) | async-done | bytes 573456 | tf_op jit(solution)/shard_map/reduce_scatter | solution.py:442
  1111.5 64.6 %reduce-scatter.23.cloned.1.call-done = bf16[320,1280]{1,0:T(8,128)(2,1)} async-done(((bf16[1280,1280]{1,0:T(8,128)(2,1)}), bf16[320,1280]{1,0:T(8,128)(2,1)}) %reduce-scatter.23.cloned.1.call-update) | async-done | bytes 819216 | tf_op jit(solution)/shard_map/reduce_scatter | solution.py:427
  1176.1 64.6 %reduce-scatter.17.cloned.1.call-done = bf16[320,1280]{1,0:T(8,128)(2,1)} async-done(((bf16[1280,1280]{1,0:T(8,128)(2,1)}), bf16[320,1280]{1,0:T(8,128)(2,1)}) %reduce-scatter.17.cloned.1.call-update) | async-done | bytes 819216 | tf_op jit(solution)/shard_map/reduce_scatter | solution.py:418
  1240.7 64.8 %reduce-scatter.19.cloned.1.call-done = bf16[320,1280]{1,0:T(8,128)(2,1)} async-done(((bf16[1280,1280]{1,0:T(8,128)(2,1)}), bf16[320,1280]{1,0:T(8,128)(2,1)}) %reduce-scatter.19.cloned.1.call-update) | async-done | bytes 819216 | tf_op jit(solution)/shard_map/reduce_scatter | solution.py:421
  1305.5 64.6 %reduce-scatter.21.cloned.1.call-done = bf16[320,1280]{1,0:T(8,128)(2,1)} async-done(((bf16[1280,1280]{1,0:T(8,128)(2,1)}), bf16[320,1280]{1,0:T(8,128)(2,1)}) %reduce-scatter.21.cloned.1.call-update) | async-done | bytes 819216 | tf_op jit(solution)/shard_map/reduce_scatter | solution.py:424
  1373.6 16.2 reduce-scatter.39.cloned.1.call-done
  1390.8 86.4 %reduce-scatter.31.cloned.1.call-done = bf16[2,320,896]{2,1,0:T(8,128)(2,1)} async-done(((bf16[2,1280,896]{2,1,0:T(8,128)(2,1)}), bf16[2,320,896]{2,1,0:T(8,128)(2,1)}) %reduce-scatter.31.cloned.1.call-update) | async-done | bytes 1146896 | tf_op jit(solution)/shard_map/reduce_scatter | solution.py:445
  1480.0 83.2 %reduce-scatter.33.cloned.1.call-done = bf16[2,320,896]{2,1,0:T(8,128)(2,1)} async-done(((bf16[2,1280,896]{2,1,0:T(8,128)(2,1)}), bf16[2,320,896]{2,1,0:T(8,128)(2,1)}) %reduce-scatter.33.cloned.1.call-update) | async-done | bytes 1146896 | tf_op jit(solution)/shard_map/reduce_scatter | solution.py:448
  1566.0 83.1 %reduce-scatter.35.cloned.1.call-done = bf16[2,224,1280]{2,1,0:T(8,128)(2,1)} async-done(((bf16[2,896,1280]{2,1,0:T(8,128)(2,1)}), bf16[2,224,1280]{2,1,0:T(8,128)(2,1)}) %reduce-scatter.35.cloned.1.call-update) | async-done | bytes 1146896 | tf_op jit(solution)/shard_map/reduce_scatter | solution.py:451
  1664.3 22.1 %all-reduce.6 = (bf16[320]{0:T(512)(128)(2,1)S(1)}, bf16[320]{0:T(512)(128)(2,1)S(1)}, bf16[320,16]{0,1:T(8,128)(2,1)S(1)}) all-reduce(bf16[320]{0:T(512)(128)(2,1)S(1)} %dynamic-slice.3, bf16[320]{0:T(512)(128)(2,1)S(1)} %dynamic-slice.5, bf16[320,16]{0,1:T(8,128)(2,1)S(1)} %copy.199), channel_id=1, replica_groups=mesh['ctx'=8,'fsdp'=4] {'ctx'}, use_global_device_ids=true, to_apply=%region_29.30 | all-reduce | flops 5760 | bytes 23040 | tf_op jit(solution)/shard_map/psum | solution.py:471
  1689.2 55.7 %all-reduce.12.cloned.1.call-done = (bf16[320,1280]{1,0:T(8,128)(2,1)}, bf16[320,1280]{1,0:T(8,128)(2,1)}, bf16[320,1280]{1,0:T(8,128)(2,1)}, bf16[320,1280]{1,0...) async-done(((bf16[320,1280]{1,0:T(8,128)(2,1)}, bf16[320,1280]{1,0:T(8,128)(2,1)}, bf16[320,1280]{1,0:T(8,128)(2,1)}, ...) | async-done | bytes 4997136 | tf_op jit(solution)/shard_map/psum | solution.py:472
  (438 shorter events, 405.1 us)
Async XLA Ops:
  7.2 67.8 %all-gather.19.cloned.1.call-start = ((), (), s32[]{:S(2)}) async-start(), calls=%async_computation.18 | async-start | bytes 4096000 | tf_op jit(solution)/shard_map/all_gather | solution.py:94
  7.9 133.0 %all-gather.15.cloned.1.call-start = ((), (), s32[]{:S(2)}) async-start(), calls=%async_computation.16 | async-start | bytes 4096000 | tf_op jit(solution)/shard_map/all_gather | solution.py:95
  8.7 198.1 %all-gather.21.cloned.1.call-start = ((), (), s32[]{:S(2)}) async-start(), calls=%async_computation.19 | async-start | bytes 4096000 | tf_op jit(solution)/shard_map/all_gather | solution.py:96
  9.4 230.2 %all-gather.17.cloned.1.call-start = ((), (), s32[]{:S(2)}) async-start(), calls=%async_computation.17 | async-start | bytes 2949120 | tf_op jit(solution)/shard_map/all_gather | solution.py:161
  151.8 120.7 %all-gather.23.cloned.1.call-start = ((), (), s32[]{:S(2)}) async-start(), calls=%async_computation.20 | async-start | bytes 2949120 | tf_op jit(solution)/shard_map/all_gather | solution.py:162
  210.3 127.9 %all-gather.25.cloned.1.call-start = ((), (), s32[]{:S(2)}) async-start(), calls=%async_computation.21 | async-start | bytes 4096000 | tf_op jit(solution)/shard_map/all_gather | solution.py:97
  210.9 214.6 %all-gather.33.cloned.1.call-start = ((), (), s32[]{:S(2)}) async-start(), calls=%async_computation.25 | async-start | bytes 5734400 | tf_op jit(solution)/shard_map/all_gather | solution.py:103
  211.6 301.2 %all-gather.35.cloned.1.call-start = ((), (), s32[]{:S(2)}) async-start(), calls=%async_computation.26 | async-start | bytes 5734400 | tf_op jit(solution)/shard_map/all_gather | solution.py:104
  212.4 387.8 %all-gather.37.cloned.1.call-start = ((), (), s32[]{:S(2)}) async-start(), calls=%async_computation.27 | async-start | bytes 5734400 | tf_op jit(solution)/shard_map/all_gather | solution.py:105
  213.1 444.3 %all-gather.27.cloned.1.call-start = ((), (), s32[]{:S(2)}) async-start(), calls=%async_computation.22 | async-start | bytes 2867200 | tf_op jit(solution)/shard_map/all_gather | solution.py:100
  368.2 36.8 %all-to-all-start = ((bf16[2,8,63,1280]{3,0,2,1:T(2,128)(2,1)}), bf16[2,8,63,1280]{3,0,2,1:T(2,128)(2,1)}, u32[]{:S(2)}, u32[]{:S(2)}) async-start(bf16[2,8,63,1280]{3,0,2,1:T(2,128)(2,1)} %copy.160), calls=%async_computation | async-start | bytes 5160960 | tf_op jit(solution)/shard_map/all_to_all | solution.py:224
  404.9 195.2 %all-to-all-start.2 = ((bf16[2,8,63,1280]{3,0,2,1:T(2,128)(2,1)}), bf16[2,8,63,1280]{3,0,2,1:T(2,128)(2,1)S(1)}, u32[]{:S(2)}, u32[]{:S(2)}) async-start(bf16[2,8,63,1280]{3,0,2,1:T(2,128)(2,1)} %copy.170), calls=%async_computation.2 | async-start | bytes 5160960 | tf_op jit(solution)/shard_map/all_to_all | solution.py:274
  409.2 290.5 %all-gather.29.cloned.1.call-start = ((), (), s32[]{:S(2)}) async-start(), calls=%async_computation.23 | async-start | bytes 2867200 | tf_op jit(solution)/shard_map/all_gather | solution.py:101
  616.4 32.6 %all-to-all-start.1 = ((bf16[2,8,63,1280]{3,0,2,1:T(2,128)(2,1)}), bf16[2,8,63,1280]{3,0,2,1:T(2,128)(2,1)S(1)}, u32[]{:S(2)}, u32[]{:S(2)}) async-start(bf16[2,8,63,1280]{3,0,2,1:T(2,128)(2,1)} %bitcast.213), calls=%async_computation.1 | async-start | bytes 5160960 | tf_op jit(solution)/shard_map/all_to_all | solution.py:240
  620.9 128.5 %all-gather.31.cloned.1.call-start = ((), (), s32[]{:S(2)}) async-start(), calls=%async_computation.24 | async-start | bytes 2867200 | tf_op jit(solution)/shard_map/all_gather | solution.py:102
  649.0 126.8 %all-to-all-start.3 = ((bf16[2,8,63,1280]{3,0,2,1:T(2,128)(2,1)}), bf16[2,8,63,1280]{3,0,2,1:T(2,128)(2,1)}, u32[]{:S(2)}, u32[]{:S(2)}) async-start(bf16[2,8,63,1280]{3,0,2,1:T(2,128)(2,1)} %bitcast.212), calls=%async_computation.3 | async-start | bytes 5160960 | tf_op jit(solution)/shard_map/all_to_all | solution.py:299
  657.0 306.3 %reduce-scatter.37.cloned.1.call-start = ((), (), s32[]{:S(2)}) async-start(), calls=%async_computation.38 | async-start | bytes 5898240
  906.7 106.2 %reduce-scatter.25.cloned.1.call-start = ((), (), s32[]{:S(2)}) async-start(), calls=%async_computation.32 | async-start | bytes 2867200 | tf_op jit(solution)/shard_map/reduce_scatter | solution.py:436
  909.0 153.1 %reduce-scatter.27.cloned.1.call-start = ((), (), s32[]{:S(2)}) async-start(), calls=%async_computation.33 | async-start | bytes 2867200 | tf_op jit(solution)/shard_map/reduce_scatter | solution.py:439
  911.3 200.2 %reduce-scatter.29.cloned.1.call-start = ((), (), s32[]{:S(2)}) async-start(), calls=%async_computation.34 | async-start | bytes 2867200 | tf_op jit(solution)/shard_map/reduce_scatter | solution.py:442
  913.6 262.5 %reduce-scatter.23.cloned.1.call-start = ((), (), s32[]{:S(2)}) async-start(), calls=%async_computation.31 | async-start | bytes 4096000 | tf_op jit(solution)/shard_map/reduce_scatter | solution.py:427
  916.5 324.2 %reduce-scatter.17.cloned.1.call-start = ((), (), s32[]{:S(2)}) async-start(), calls=%async_computation.28 | async-start | bytes 4096000 | tf_op jit(solution)/shard_map/reduce_scatter | solution.py:418
  968.2 337.3 %reduce-scatter.19.cloned.1.call-start = ((), (), s32[]{:S(2)}) async-start(), calls=%async_computation.29 | async-start | bytes 4096000 | tf_op jit(solution)/shard_map/reduce_scatter | solution.py:421
  971.4 398.6 %reduce-scatter.21.cloned.1.call-start = ((), (), s32[]{:S(2)}) async-start(), calls=%async_computation.30 | async-start | bytes 4096000 | tf_op jit(solution)/shard_map/reduce_scatter | solution.py:424
  975.4 414.5 %reduce-scatter.39.cloned.1.call-start = ((), (), s32[]{:S(2)}) async-start(), calls=%async_computation.39 | async-start | bytes 409600
  977.2 500.0 %reduce-scatter.31.cloned.1.call-start = ((), (), s32[]{:S(2)}) async-start(), calls=%async_computation.35 | async-start | bytes 5734400 | tf_op jit(solution)/shard_map/reduce_scatter | solution.py:445
  984.6 578.6 %reduce-scatter.33.cloned.1.call-start = ((), (), s32[]{:S(2)}) async-start(), calls=%async_computation.36 | async-start | bytes 5734400 | tf_op jit(solution)/shard_map/reduce_scatter | solution.py:448
  992.0 657.0 %reduce-scatter.35.cloned.1.call-start = ((), (), s32[]{:S(2)}) async-start(), calls=%async_computation.37 | async-start | bytes 5734400 | tf_op jit(solution)/shard_map/reduce_scatter | solution.py:451
  999.2 371.5 %copy-start.4 = (f32[128,1280]{1,0:T(8,128)S(1)}, f32[128,1280]{1,0:T(8,128)}, u32[]{:S(2)}) copy-start(f32[128,1280]{1,0:T(8,128)} %copy-done.2) | copy-start | bytes 1966084
  999.2 371.5 %copy-start.22 = (f32[128,1280]{1,0:T(8,128)S(1)}, f32[128,1280]{1,0:T(8,128)}, u32[]{:S(2)}) copy-start(f32[128,1280]{1,0:T(8,128)} %get-tuple-element.438) | copy-start | bytes 1966084
  999.2 371.5 %copy-start.29 = (bf16[128,896]{1,0:T(8,128)(2,1)S(1)}, bf16[128,896]{1,0:T(8,128)(2,1)}, u32[]{:S(2)}) copy-start(bf16[128,896]{1,0:T(8,128)(2,1)} %get-tuple-element.526) | copy-start | bytes 688132
  999.2 745.7 %all-reduce.12.cloned.1.call-start = ((), (), s32[]{:S(2)}) async-start(), calls=%async_computation.40 | async-start | bytes 9994240 | tf_op jit(solution)/shard_map/psum | solution.py:472
  (84 other events, 1365.1 us)
Sparse Core Ops, SparseCore 0:
  9.6 65.3 all-gather.18
  76.6 64.2 all-gather.14
  142.5 64.2 all-gather.20
  209.1 30.4 all-gather.16
  241.9 30.4 all-gather.22
  273.9 64.2 all-gather.24
  339.8 85.6 all-gather.32
  427.1 85.7 all-gather.34
  514.4 85.7 all-gather.36
  601.6 48.2 all-gather.26
  651.5 48.2 all-gather.28
  701.1 48.2 all-gather.30
  906.9 56.4 reduce-scatter.36
  966.2 46.6 reduce-scatter.24
  1015.6 46.4 reduce-scatter.26
  1065.0 46.4 reduce-scatter.28
  1113.7 62.4 reduce-scatter.22
  1178.3 62.3 reduce-scatter.16
  1243.0 62.3 reduce-scatter.18
  1307.6 62.3 reduce-scatter.20
  1372.9 16.8 reduce-scatter.38
  1392.2 84.9 reduce-scatter.30
  1479.5 83.6 reduce-scatter.32
  1565.4 83.6 reduce-scatter.34
  1653.3 91.5 all-reduce.11
where the time goes:
time: 1770 us; the launch traced here: 1760 us
  waiting for transfers between devices  1270 us (72%)
  local copies, waits for them, and re-layouts  186 us (11%)
  matrix products  139 us (8%)
  other arithmetic  62.8 us (4%)
  blocking collectives  55.8 us (3%)
  starting transfers between devices  24 us (1%)
    reduce_scatter x1, waiting for transfers between devices, per_device(): lax.psum_scatter(grad_expert_gate.astype(jnp.bfloat16), 'fsdp', scatter_d...  86.4 us
    reduce_scatter x1, waiting for transfers between devices, per_device(): lax.psum_scatter(grad_expert_up.astype(jnp.bfloat16), 'fsdp', scatter_dim...  83.2 us
    reduce_scatter x1, waiting for transfers between devices, per_device(): lax.psum_scatter(grad_expert_down.astype(jnp.bfloat16), 'fsdp', scatter_d...  83.1 us
    all_gather x1, waiting for transfers between devices, per_device(): lax.all_gather(expert_down, 'fsdp', axis=1, tiled=True)  79.7 us
    all_gather x1, waiting for transfers between devices, per_device(): lax.all_gather(expert_up, 'fsdp', axis=1, tiled=True)  79.5 us
    unnamed x27, waiting for transfers between devices  69.3 us
    reduce_scatter x1, waiting for transfers between devices, per_device(): lax.psum_scatter(grad_wkey.astype(jnp.bfloat16), 'fsdp', scatter_dimensio...  64.8 us
    reduce_scatter x1, waiting for transfers between devices, per_device(): lax.psum_scatter(grad_output.astype(jnp.bfloat16), 'fsdp', scatter_dimens...  64.6 us
  transfers between devices with their start and end apart: 29, of which 25 were waited for; matrix products, arithmetic and copies ran while one was open for 14% of the time, Pallas kernels for 0%

commit v1 on v0

--- a/solution.py
+++ b/solution.py
@@ -3,6 +3,8 @@
 import jax
 import jax.numpy as jnp
 from jax import lax
+from jax.experimental import pallas as pl
+from jax.experimental.pallas import tpu as pltpu
 from jax.sharding import PartitionSpec as P
 
 D = 1280
@@ -67,6 +69,449 @@
 
 def unchanged(progress):
     return progress
+
+
+NZ = 4
+SLOTS = 64
+WIDE = 256
+MESH = pl.DeviceIdType.MESH
+PEERS = ((0, 1), (1, 0), (1, 1))
+NN = (((1,), (0,)), ((), ()))
+NT = (((1,), (1,)), ((), ()))
+TN = (((0,), (0,)), ((), ()))
+
+
+def dot(left, right, dims=NN):
+    return lax.dot_general(left, right, dims, preferred_element_type=jnp.float32)
+
+
+def flip(c, fy, fx, fk):
+    return 4 * ((c // 4 + fy) % 2) + 2 * (((c // 2) % 2 + fx) % 2) + (c % 2 + fk) % 2
+
+
+def remote(src, dst, send, recv, c, z):
+    return pltpu.make_async_remote_copy(
+        src_ref=src, dst_ref=dst, send_sem=send, recv_sem=recv, device_id=(c, z), device_id_type=MESH
+    )
+
+
+def greet(c, z):
+    barrier = pltpu.get_barrier_semaphore()
+    peers = [(c, (z + d) % NZ) for d in range(1, NZ)]
+    peers += [(flip(c, fy, fx, 0), z) for fy, fx in PEERS] + [(flip(c, 0, 0, 1), z)]
+    for peer in peers:
+        pl.semaphore_signal(barrier, inc=1, device_id=peer, device_id_type=MESH)
+    pl.semaphore_wait(barrier, len(peers))
+
+
+class Spread:
+    def __init__(self, src, dst, sems, c, z):
+        self.src, self.dst, self.c, self.z = src, dst, c, z
+        self.local, self.zs, self.zr, self.xs, self.xr, self.ms, self.mr = sems
+
+    def block(self, c, d):
+        return self.dst.at[c, (self.z + NZ - d) % NZ]
+
+    def zcopy(self, d):
+        return remote(
+            self.src, self.dst.at[self.c, self.z], self.zs.at[d - 1], self.zr.at[d - 1], self.c, (self.z + d) % NZ
+        )
+
+    def zwait(self, d):
+        block = self.block(self.c, d)
+        remote(block, block, self.zs.at[d - 1], self.zr.at[d - 1], self.c, self.z).wait_recv()
+
+    def xcopy(self, i, d):
+        src = self.src if d == 0 else self.block(self.c, d)
+        fy, fx = PEERS[i]
+        return remote(
+            src, self.block(self.c, d), self.xs.at[i, d], self.xr.at[i, d], flip(self.c, fy, fx, 0), self.z
+        )
+
+    def xwait(self, i, d):
+        fy, fx = PEERS[i]
+        block = self.block(flip(self.c, fy, fx, 0), d)
+        remote(block, block, self.xs.at[i, d], self.xr.at[i, d], self.c, self.z).wait_recv()
+
+    def mcopy(self, i, d):
+        fy, fx = (((0, 0),) + PEERS)[i]
+        block = self.block(flip(self.c, fy, fx, 0), d)
+        src = self.src if (i == 0 and d == 0) else block
+        return remote(src, block, self.ms.at[i, d], self.mr.at[i, d], flip(self.c, 0, 0, 1), self.z)
+
+    def mwait(self, i, d):
+        fy, fx = (((0, 0),) + PEERS)[i]
+        block = self.block(flip(self.c, fy, fx, 1), d)
+        remote(block, block, self.ms.at[i, d], self.mr.at[i, d], self.c, self.z).wait_recv()
+
+    def start(self):
+        self.own = pltpu.make_async_copy(self.src, self.dst.at[self.c, self.z], self.local)
+        self.own.start()
+        for d in range(1, NZ):
+            self.zcopy(d).start()
+        for i in range(3):
+            self.xcopy(i, 0).start()
+        self.mcopy(0, 0).start()
+
+    def relay_z(self):
+        for d in range(1, NZ):
+            self.zwait(d)
+            for i in range(3):
+                self.xcopy(i, d).start()
+            self.mcopy(0, d).start()
+
+    def relay_x(self):
+        for d in range(NZ):
+            for i in range(3):
+                self.xwait(i, d)
+                self.mcopy(i + 1, d).start()
+
+    def finish(self):
+        self.own.wait()
+        for d in range(NZ):
+            for i in range(4):
+                self.mwait(i, d)
+        for d in range(1, NZ):
+            self.zcopy(d).wait_send()
+        for d in range(NZ):
+            for i in range(3):
+                self.xcopy(i, d).wait_send()
+            for i in range(4):
+                self.mcopy(i, d).wait_send()
+
+
+def spread_sems():
+    dma = pltpu.SemaphoreType.DMA
+    return [dma, dma((3,)), dma((3,)), dma((3, NZ)), dma((3, NZ)), dma((4, NZ)), dma((4, NZ))]
+
+
+def swish(values):
+    sigma = 1.0 / (1.0 + jnp.exp(-values))
+    return values * sigma, sigma * (1.0 + values * (1.0 - sigma))
+
+
+def expert_kernel(
+    b_ref, t_ref, g_ref, wsend_ref, wdn_ref,
+    y_ref, db_ref, dg_ref, dgu_ref, ddn_ref, dsgu_ref, dsdn_ref, ball, tall, gall, mrecv, xrecv,
+    wgu, acc, bg, gg, tg, oh, xs, gs, ys, ds, st, ld, zbuf, zrecv, gst,
+    sb0, sb1, sb2, sb3, sb4, sb5, sb6, sg0, sg1, sg2, sg3, sg4, sg5, sg6, st0, st1, st2, st3, st4, st5, st6,
+    wl, wss, wrs, lsem, ms, mr, xs_s, xs_r, ldsem, zs, zr, gl, gss, grs,
+):
+    c = lax.axis_index("ctx")
+    z = lax.axis_index("fsdp")
+    f32, bf16 = jnp.float32, jnp.bfloat16
+    mate = flip(c, 0, 0, 1)
+    length = b_ref.shape[0]
+    group = NZ * length
+    rows = wgu.shape[1] // NZ
+    greet(c, z)
+    spread_b = Spread(b_ref, ball, (sb0, sb1, sb2, sb3, sb4, sb5, sb6), c, z)
+    spread_t = Spread(t_ref, tall, (st0, st1, st2, st3, st4, st5, st6), c, z)
+    spread_g = Spread(g_ref, gall, (sg0, sg1, sg2, sg3, sg4, sg5, sg6), c, z)
+
+    def wcopy(d):
+        there = (z + d) % NZ
+        return remote(
+            wsend_ref.at[there], wgu.at[:, pl.ds(pl.multiple_of(z * rows, rows), rows), :],
+            wss.at[d - 1], wrs.at[d - 1], c, there,
+        )
+
+    def wwait(d):
+        here = wgu.at[:, pl.ds(pl.multiple_of((z + NZ - d) % NZ * rows, rows), rows), :]
+        remote(wsend_ref.at[0], here, wss.at[d - 1], wrs.at[d - 1], c, z).wait_recv()
+
+    wown = pltpu.make_async_copy(wsend_ref.at[z], wgu.at[:, pl.ds(pl.multiple_of(z * rows, rows), rows), :], wl)
+    spread_t.start()
+    spread_b.start()
+    spread_g.start()
+    wown.start()
+    for d in range(1, NZ):
+        wcopy(d).start()
+    acc[...] = jnp.zeros_like(acc)
+    ddn_ref[...] = jnp.zeros_like(ddn_ref)
+    st[...] = jnp.zeros_like(st)
+    zbuf[...] = jnp.zeros_like(zbuf)
+    spread_t.relay_z()
+    spread_b.relay_z()
+    spread_t.relay_x()
+    spread_b.relay_x()
+    spread_g.relay_z()
+    spread_g.relay_x()
+    spread_t.finish()
+    spread_b.finish()
+    spread_g.finish()
+    wown.wait()
+    for d in range(1, NZ):
+        wwait(d)
+
+    def target(g):
+        left = 3 - g // 2
+        return flip(c, left % 2, left // 2, 1 - g % 2)
+
+    def loads(g):
+        slot = g % 2
+        there = target(g)
+        return (
+            pltpu.make_async_copy(ball.at[there], bg.at[slot], lsem.at[slot, 0]),
+            pltpu.make_async_copy(gall.at[there], gg.at[slot], lsem.at[slot, 1]),
+            pltpu.make_async_copy(tall.at[there], tg.at[slot], lsem.at[slot, 2]),
+        )
+
+    def to_mate(s):
+        return remote(st.at[0], mrecv.at[s], ms.at[s], mr.at[s], mate, z)
+
+    def to_chip(s):
+        left = 3 - s
+        return remote(st.at[1], xrecv.at[s], xs_s.at[s], xs_r.at[s], flip(c, left % 2, left // 2, 0), z)
+
+    for copy in loads(0):
+        copy.start()
+    slot_ids = lax.broadcasted_iota(jnp.int32, (SLOTS, length), 0).astype(f32)
+    row_ids = lax.broadcasted_iota(jnp.int32, (16, length), 0)
+    table_rows = lax.broadcasted_iota(jnp.int32, (16, 2 * length), 0)
+
+    def step(g, carry):
+        slot = g % 2
+        s = g // 2
+        par = g % 2
+        for copy in loads(g):
+            copy.wait()
+
+        @pl.when(g < 7)
+        def _():
+            for copy in loads(g + 1):
+                copy.start()
+
+        @pl.when((s > 0) & (par == 0))
+        def _():
+            to_mate(s - 1).wait_send()
+
+        @pl.when((s > 0) & (par == 1))
+        def _():
+            to_chip(s - 1).wait_send()
+
+        scales = [[], []]
+        for q in range(NZ):
+            hits = []
+            for e in range(2):
+                mine = jnp.sum(jnp.where(table_rows == 2 * c + e, tg[slot, q], 0.0), axis=0, keepdims=True)
+                rank = mine[:, :length]
+                share = mine[:, length:]
+                hit = slot_ids == rank
+                scales[e].append(jnp.sum(jnp.where(hit, share, 0.0), axis=1, keepdims=True))
+                hits.append(jnp.where(hit, 1.0, 0.0))
+            hot = jnp.concatenate(hits, axis=0).astype(bf16)
+            oh[q] = hot
+            part = dot(hot, bg[slot, q]).astype(bf16)
+            xs[0, q * SLOTS : (q + 1) * SLOTS] = part[:SLOTS]
+            xs[1, q * SLOTS : (q + 1) * SLOTS] = part[SLOTS:]
+            part = dot(hot, gg[slot, q]).astype(bf16)
+            gs[0, q * SLOTS : (q + 1) * SLOTS] = part[:SLOTS]
+            gs[1, q * SLOTS : (q + 1) * SLOTS] = part[SLOTS:]
+        back = [0.0] * NZ
+        for e in range(2):
+            scale = jnp.concatenate(scales[e], axis=0)
+            both = dot(xs[e], wgu[e])
+            up = both[:, WIDE:]
+            silu, slope = swish(both[:, :WIDE])
+            inner = (silu * up).astype(bf16)
+            scaled = (inner.astype(f32) * scale).astype(bf16)
+            out = dot(scaled, wdn_ref[e]).astype(bf16)
+            pull = dot(gs[e], wdn_ref[e], NT)
+            gain = jnp.sum(inner.astype(f32) * pull, axis=1, keepdims=True)
+            pull = pull * scale
+            turn = jnp.concatenate([(pull * up * slope).astype(bf16), (pull * silu).astype(bf16)], axis=1)
+            ddn_ref[e] += dot(scaled, gs[e], TN)
+            acc[e] += dot(xs[e], turn, TN)
+            into = dot(turn, wgu[e], NT).astype(bf16)
+            for q in range(NZ):
+                part = slice(q * SLOTS, (q + 1) * SLOTS)
+                ys[q, e * SLOTS : (e + 1) * SLOTS] = out[part]
+                ds[q, e * SLOTS : (e + 1) * SLOTS] = into[part]
+                hit = oh[q, e * SLOTS : (e + 1) * SLOTS].astype(f32)
+                line = jnp.sum(hit * gain[part], axis=0, keepdims=True)
+                back[q] = back[q] + jnp.where(row_ids == 2 * c + e, line, 0.0)
+        for q in range(NZ):
+            st[par, q * length : (q + 1) * length] = dot(oh[q], ds[q], TN).astype(bf16)
+            st[par, group + q * length : group + (q + 1) * length] = dot(oh[q], ys[q], TN).astype(bf16)
+            st[par, 2 * group :, q * length : (q + 1) * length] = back[q].astype(bf16)
+
+        @pl.when(g == 7)
+        def _():
+            for h in range(2):
+                tokens = bg[slot, 2 * h : 2 * h + 2].reshape(2 * length, bg.shape[3])
+                upper = gg[slot, 2 * h : 2 * h + 2].reshape(2 * length, bg.shape[3])
+                both = dot(tokens, wgu[2])
+                up = both[:, WIDE:]
+                silu, slope = swish(both[:, :WIDE])
+                inner = (silu * up).astype(bf16)
+                part = slice(2 * h * length, 2 * (h + 1) * length)
+                more = slice(group + 2 * h * length, group + 2 * (h + 1) * length)
+                st[1, more] = (st[1, more].astype(f32) + dot(inner, wdn_ref[2])).astype(bf16)
+                pull = dot(upper, wdn_ref[2], NT)
+                turn = jnp.concatenate([(pull * up * slope).astype(bf16), (pull * silu).astype(bf16)], axis=1)
+                st[1, part] = (st[1, part].astype(f32) + dot(turn, wgu[2], NT)).astype(bf16)
+                if h == 0:
+                    dsdn_ref[...] = dot(inner, upper, TN)
+                    dsgu_ref[...] = dot(tokens, turn, TN)
+                else:
+                    dsdn_ref[...] += dot(inner, upper, TN)
+                    dsgu_ref[...] += dot(tokens, turn, TN)
+
+        @pl.when(par == 0)
+        def _():
+            to_mate(s).start()
+
+        @pl.when(par == 1)
+        def _():
+            to_mate(s).wait_recv()
+            copy = pltpu.make_async_copy(mrecv.at[s], ld.at[0], ldsem.at[0])
+            copy.start()
+            copy.wait()
+
+            def add(i, carry):
+                part = pl.ds(pl.multiple_of(i * 16, 16), 16)
+                st[1, part] = (st[1, part].astype(f32) + ld[0, part].astype(f32)).astype(bf16)
+                return carry
+
+            lax.fori_loop(0, st.shape[1] // 16, add, 0)
+
+            @pl.when(s < 3)
+            def _():
+                to_chip(s).start()
+
+        return carry
+
+    lax.fori_loop(0, 8, step, 0)
+    to_mate(3).wait_send()
+    for e in range(2):
+        gst[e] = acc[e].astype(bf16)
+
+    def gcopy(d):
+        there = (z + d) % NZ
+        return remote(
+            gst.at[:, pl.ds(pl.multiple_of(there * rows, rows), rows), :], dgu_ref.at[z],
+            gss.at[d - 1], grs.at[d - 1], c, there,
+        )
+
+    gown = pltpu.make_async_copy(gst.at[:, pl.ds(pl.multiple_of(z * rows, rows), rows), :], dgu_ref.at[z], gl)
+    gown.start()
+    for i in range(3):
+        to_chip(i).wait_recv()
+        pltpu.make_async_copy(xrecv.at[i], ld.at[i], ldsem.at[i]).start()
+    for i in range(3):
+        pltpu.make_async_copy(xrecv.at[i], ld.at[i], ldsem.at[i]).wait()
+
+    def total(part, lanes=slice(None)):
+        value = st[1, part, lanes].astype(f32)
+        for i in range(3):
+            value = value + ld[i, part, lanes].astype(f32)
+        return value.astype(bf16)
+
+    for q in range(NZ):
+
+        def add(i, carry):
+            base = pl.multiple_of(i * 16, 16)
+            zbuf[q, pl.ds(base, 16)] = total(pl.ds(pl.multiple_of(base + q * length, 16), 16))
+            zbuf[q, pl.ds(pl.multiple_of(base + length, 16), 16)] = total(
+                pl.ds(pl.multiple_of(base + group + q * length, 16), 16)
+            )
+            return carry
+
+        lax.fori_loop(0, length // 16, add, 0)
+        zbuf[q, 2 * length : 2 * length + 16, 0:length] = total(
+            slice(2 * group, 2 * group + 16), slice(q * length, (q + 1) * length)
+        )
+
+    def zcopy(d):
+        there = (z + d) % NZ
+        return remote(zbuf.at[there], zrecv.at[d - 1], zs.at[d - 1], zr.at[d - 1], c, there)
+
+    for d in range(1, NZ):
+        zcopy(d).start()
+    for d in range(1, NZ):
+        gcopy(d).start()
+    for d in range(1, NZ):
+        zcopy(d).wait_recv()
+
+    def settle(i, carry):
+        base = pl.multiple_of(i * 16, 16)
+        for ref, start in ((db_ref, 0), (y_ref, length)):
+            part = pl.ds(pl.multiple_of(base + start, 16), 16)
+            value = zbuf[z, part].astype(f32)
+            for d in range(3):
+                value = value + zrecv[d, part].astype(f32)
+            ref[pl.ds(base, 16)] = value
+        return carry
+
+    lax.fori_loop(0, length // 16, settle, 0)
+    last = slice(2 * length, 2 * length + 16)
+    value = zbuf[z, last, 0:length].astype(f32)
+    for d in range(3):
+        value = value + zrecv[d, last, 0:length].astype(f32)
+    dg_ref[...] = value
+    for d in range(1, NZ):
+        zcopy(d).wait_send()
+        wcopy(d).wait_send()
+        gcopy(d).wait()
+    gown.wait()
+
+
+def expert_stage(moe_input, table, upstream_low, wsend, wdn):
+    length, width = moe_input.shape
+    dma = pltpu.SemaphoreType.DMA
+    hbm = pl.BlockSpec(memory_space=pl.ANY)
+    vmem = pl.BlockSpec(memory_space=pltpu.VMEM)
+    f32, bf16 = jnp.float32, jnp.bfloat16
+    shape = jax.ShapeDtypeStruct
+    inner = 2 * WIDE
+    group = NZ * length
+    rows = width // NZ
+    return pl.pallas_call(
+        expert_kernel,
+        name="experts",
+        out_shape=[
+            shape((length, width), f32),
+            shape((length, width), f32),
+            shape((16, length), f32),
+            shape((NZ, 2, rows, inner), bf16),
+            shape((2, WIDE, width), f32),
+            shape((width, inner), f32),
+            shape((WIDE, width), f32),
+            shape((8, NZ, length, width), bf16),
+            shape((8, NZ, 16, 2 * length), f32),
+            shape((8, NZ, length, width), bf16),
+            shape((4, 2 * group + 16, width), bf16),
+            shape((3, 2 * group + 16, width), bf16),
+        ],
+        in_specs=[hbm, hbm, hbm, hbm, vmem],
+        out_specs=[vmem, vmem, vmem, hbm, vmem, vmem, vmem, hbm, hbm, hbm, hbm, hbm],
+        scratch_shapes=[
+            pltpu.VMEM((3, width, inner), bf16),
+            pltpu.VMEM((2, width, inner), f32),
+            pltpu.VMEM((2, NZ, length, width), bf16),
+            pltpu.VMEM((2, NZ, length, width), bf16),
+            pltpu.VMEM((2, NZ, 16, 2 * length), f32),
+            pltpu.VMEM((NZ, 2 * SLOTS, length), bf16),
+            pltpu.VMEM((2, NZ * SLOTS, width), bf16),
+            pltpu.VMEM((2, NZ * SLOTS, width), bf16),
+            pltpu.VMEM((NZ, 2 * SLOTS, width), bf16),
+            pltpu.VMEM((NZ, 2 * SLOTS, width), bf16),
+            pltpu.VMEM((2, 2 * group + 16, width), bf16),
+            pltpu.VMEM((3, 2 * group + 16, width), bf16),
+            pltpu.VMEM((NZ, 2 * length + 16, width), bf16),
+            pltpu.VMEM((3, 2 * length + 16, width), bf16),
+            pltpu.VMEM((2, width, inner), bf16),
+        ]
+        + spread_sems() + spread_sems() + spread_sems()
+        + [
+            dma, dma((3,)), dma((3,)), dma((2, 3)), dma((4,)), dma((4,)), dma((3,)), dma((3,)), dma((3,)),
+            dma((3,)), dma((3,)), dma, dma((3,)), dma((3,)),
+        ],
+        compiler_params=pltpu.CompilerParams(
+            collective_id=1, has_side_effects=True, vmem_limit_bytes=62 * 1024 * 1024
+        ),
+    )(moe_input, table, upstream_low, wsend, wdn)
 
 
 def per_device(
@@ -498,9 +943,343 @@
     )
 
 
+def per_device_fast(
+    tokens,
+    documents,
+    routes,
+    priority,
+    attention_gain,
+    query_weight,
+    key_weight,
+    value_weight,
+    output_weight,
+    feedforward_gain,
+    router_weight,
+    shared_gate,
+    shared_up,
+    shared_down,
+    expert_gate,
+    expert_up,
+    expert_down,
+    cotangent,
+):
+    gathered = (
+        lax.all_gather(attention_gain, "fsdp", axis=0, tiled=True),
+        lax.all_gather(query_weight, "fsdp", axis=0, tiled=True),
+        lax.all_gather(key_weight, "fsdp", axis=0, tiled=True),
+        lax.all_gather(value_weight, "fsdp", axis=0, tiled=True),
+        lax.all_gather(output_weight, "fsdp", axis=0, tiled=True),
+        lax.all_gather(feedforward_gain, "fsdp", axis=0, tiled=True),
+        lax.all_gather(router_weight, "fsdp", axis=0, tiled=True),
+    )
+    (
+        gain_one,
+        w_query,
+        w_key,
+        w_value,
+        w_output,
+        gain_two,
+        w_router,
+    ) = gathered
+    groups = lax.axis_size("ctx")
+    length = tokens.shape[1]
+    row_length = length * groups
+    experts = EXP_DEV * groups
+    capacity = 9 * length * TOPK // (8 * experts)
+    inner_width = HEADS * HEAD_DIM
+    score_scale = HEAD_DIM ** (-0.5)
+    spare_slot = experts * capacity
+    first_here = lax.axis_index("ctx") * length
+    positions = first_here + jnp.arange(length, dtype=jnp.int32)
+    last_here = first_here + length - 1
+    doc_here = documents[0].astype(jnp.float32)
+    doc_wire = documents[0].astype(jnp.bfloat16)
+    inputs = tokens[0].astype(jnp.float32)
+    upstream_low = cotangent[0]
+    upstream = upstream_low.astype(jnp.float32)
+    factor_one = rms_factor(inputs)
+    normed_one = inputs * factor_one
+    gain_one_wide = gain_one.astype(jnp.float32)
+    attn_input = (normed_one * gain_one_wide).astype(jnp.bfloat16)
+    query_pre = jnp.dot(attn_input, w_query, preferred_element_type=jnp.float32).reshape(
+        length, HEADS, HEAD_DIM
+    )
+    key_pre = jnp.dot(attn_input, w_key, preferred_element_type=jnp.float32).reshape(
+        length, HEADS, HEAD_DIM
+    )
+    cosine, sine = rotary_tables(positions, HEAD_DIM // 2)
+    queries = rotate(query_pre, cosine, sine).astype(jnp.bfloat16)
+    key_rows = rotate(key_pre, cosine, sine).astype(jnp.bfloat16)
+    value_rows = (
+        jnp.dot(attn_input, w_value, preferred_element_type=jnp.float32)
+        .astype(jnp.bfloat16)
+        .reshape(length, HEADS, HEAD_DIM)
+    )
+    initial = (
+        jnp.zeros((HEADS, length, HEAD_DIM), jnp.float32),
+        jnp.full((HEADS, length), negative, jnp.float32),
+        jnp.zeros((HEADS, length), jnp.float32),
+    )
+    key_all = lax.all_gather(key_rows, "ctx", axis=0, tiled=True)
+    value_all = lax.all_gather(value_rows, "ctx", axis=0, tiled=True)
+    docs_all = lax.all_gather(doc_wire, "ctx", axis=0, tiled=True)
+
+    def visit(progress, within, rows_now):
+
+        def compute(progress):
+            accum, highest_seen, totals = progress
+            key_block = lax.dynamic_slice_in_dim(key_all, within, rows_now, 0)
+            value_block = lax.dynamic_slice_in_dim(value_all, within, rows_now, 0)
+            docs_block = lax.dynamic_slice_in_dim(docs_all, within, rows_now, 0).astype(jnp.float32)
+            key_pos = within + jnp.arange(rows_now, dtype=jnp.int32)
+            allowed = allowed_mask(positions, doc_here, key_pos, docs_block)[None]
+            scores = jnp.einsum(
+                "qhd,khd->hqk", queries, key_block, preferred_element_type=jnp.float32
+            )
+            scores = jnp.where(allowed, scores * score_scale, negative)
+            newest = jnp.maximum(highest_seen, jnp.max(scores, axis=-1))
+            shrink = jnp.exp(highest_seen - newest)
+            shares = jnp.exp(scores - newest[..., None]) * allowed
+            totals = totals * shrink + jnp.sum(shares, axis=-1)
+            accum = accum * shrink[..., None] + jnp.einsum(
+                "hqk,khd->hqd",
+                shares.astype(jnp.bfloat16),
+                value_block,
+                preferred_element_type=jnp.float32,
+            )
+            return (accum, newest, totals)
+
+        return lax.cond(within > last_here, unchanged, compute, progress)
+
+    accum, highest_seen, totals = blockwise(key_all.shape[0], visit, initial)
+    attended = accum / totals[..., None]
+    log_total = highest_seen + jnp.log(totals)
+    mixed_rows = (
+        jnp.transpose(attended, (1, 0, 2)).reshape(length, inner_width).astype(jnp.bfloat16)
+    )
+    hidden = inputs + jnp.dot(mixed_rows, w_output, preferred_element_type=jnp.float32)
+    factor_two = rms_factor(hidden)
+    normed_two = hidden * factor_two
+    gain_two_wide = gain_two.astype(jnp.float32)
+    moe_input = (normed_two * gain_two_wide).astype(jnp.bfloat16)
+    moe_wide = moe_input.astype(jnp.float32)
+    router_wide = w_router.astype(jnp.float32)
+    gate_probs = jax.nn.softmax(jnp.dot(moe_wide, router_wide, precision=highest), axis=-1)
+    route_now = routes[0]
+    order_now = priority[0, 0]
+    onehot = (route_now[:, :, None] == jnp.arange(experts, dtype=jnp.int32)).astype(jnp.float32)
+    counts = jnp.sum(onehot, axis=1)
+    earlier = (order_now[None, :] < order_now[:, None]).astype(jnp.bfloat16)
+    before = jnp.dot(earlier, counts.astype(jnp.bfloat16), preferred_element_type=jnp.float32)
+    kept = (counts > 0) & (before < capacity)
+    table = jnp.concatenate(
+        [jnp.where(kept, before, -1.0).T, jnp.where(kept, gate_probs, 0.0).T], axis=1
+    )
+    hidden_dev = expert_gate.shape[2] // NZ
+
+    def slices(weights):
+        parts = weights.reshape(weights.shape[0], weights.shape[1], NZ, hidden_dev)
+        parts = jnp.pad(parts, ((0, 0), (0, 0), (0, 0), (0, WIDE - hidden_dev)))
+        return jnp.transpose(parts, (2, 0, 1, 3))
+
+    wsend = jnp.concatenate(
+        [
+            jnp.concatenate([slices(expert_gate), slices(shared_gate[None])], axis=1),
+            jnp.concatenate([slices(expert_up), slices(shared_up[None])], axis=1),
+        ],
+        axis=3,
+    )
+    wdn = jnp.pad(
+        jnp.concatenate([expert_down, shared_down[None]], axis=0), ((0, 0), (0, WIDE - hidden_dev), (0, 0))
+    )
+    (routed, grad_moe, grad_table, gu_back, grad_down, shared_gu, shared_dn) = expert_stage(
+        moe_input, table, upstream_low, wsend, wdn
+    )[:7]
+    output_rows = (hidden + routed).astype(jnp.bfloat16)
+    grad_probs = grad_table.T
+
+    def joined(parts, at):
+        return jnp.concatenate([parts[i][..., at : at + hidden_dev] for i in range(NZ)], axis=-1).astype(jnp.float32)
+
+    own_expert_gate = joined(gu_back, 0)
+    own_expert_up = joined(gu_back, WIDE)
+    own_expert_down = grad_down[:, :hidden_dev]
+    shared_sum = lax.psum(shared_gu.astype(jnp.bfloat16), "ctx")
+    shared_back = lax.all_to_all(
+        shared_sum.reshape(NZ, shared_sum.shape[0] // NZ, 2 * WIDE), "fsdp", split_axis=0, concat_axis=0, tiled=True
+    )
+    own_shared_gate = joined(shared_back, 0)
+    own_shared_up = joined(shared_back, WIDE)
+    own_shared_down = lax.psum(shared_dn[:hidden_dev].astype(jnp.bfloat16), "ctx").astype(jnp.float32)
+    grad_logits = gate_probs * (
+        grad_probs - jnp.sum(gate_probs * grad_probs, axis=-1, keepdims=True)
+    )
+    grad_router = jnp.dot(moe_wide.T, grad_logits, precision=highest)
+    grad_moe = grad_moe + jnp.dot(grad_logits, router_wide.T, precision=highest)
+    grad_gain_two = jnp.sum(grad_moe * normed_two, axis=0)
+    scaled_two = grad_moe * gain_two_wide
+    grad_hidden = upstream + factor_two * (
+        scaled_two - normed_two * jnp.mean(scaled_two * normed_two, axis=-1, keepdims=True)
+    )
+    grad_hidden_low = grad_hidden.astype(jnp.bfloat16)
+    grad_output = jnp.dot(mixed_rows.T, grad_hidden_low, preferred_element_type=jnp.float32)
+    grad_mixed = (
+        jnp.dot(grad_hidden_low, w_output.T, preferred_element_type=jnp.float32)
+        .astype(jnp.bfloat16)
+        .reshape(length, HEADS, HEAD_DIM)
+    )
+    delta = jnp.einsum("qhd,hqd->hq", grad_mixed.astype(jnp.float32), attended)
+    start_state = (
+        jnp.zeros((length, HEADS, HEAD_DIM), jnp.float32),
+        jnp.zeros((row_length, 2 * inner_width), jnp.float32),
+    )
+    back_key_all = lax.all_gather(key_rows, "ctx", axis=0, tiled=True)
+    back_value_all = lax.all_gather(value_rows, "ctx", axis=0, tiled=True)
+    back_docs_all = lax.all_gather(doc_wire, "ctx", axis=0, tiled=True)
+
+    def visit(progress, within, rows_now):
+        first_row = within
+
+        def compute(progress):
+            grad_query_acc, grad_kv_all = progress
+            key_block = lax.dynamic_slice_in_dim(back_key_all, within, rows_now, 0)
+            value_block = lax.dynamic_slice_in_dim(back_value_all, within, rows_now, 0)
+            docs_block = lax.dynamic_slice_in_dim(back_docs_all, within, rows_now, 0).astype(
+                jnp.float32
+            )
+            key_pos = first_row + jnp.arange(rows_now, dtype=jnp.int32)
+            allowed = allowed_mask(positions, doc_here, key_pos, docs_block)[None]
+            scores = jnp.einsum(
+                "qhd,khd->hqk", queries, key_block, preferred_element_type=jnp.float32
+            )
+            scores = jnp.where(allowed, scores * score_scale, negative)
+            shares = jnp.exp(scores - log_total[..., None]) * allowed
+            grad_shares = jnp.einsum(
+                "qhd,khd->hqk", grad_mixed, value_block, preferred_element_type=jnp.float32
+            )
+            grad_scores = (shares * (grad_shares - delta[..., None]) * score_scale).astype(
+                jnp.bfloat16
+            )
+            grad_query_acc = grad_query_acc + jnp.einsum(
+                "hqk,khd->qhd", grad_scores, key_block, preferred_element_type=jnp.float32
+            )
+            grad_key_rows = jnp.einsum(
+                "hqk,qhd->khd", grad_scores, queries, preferred_element_type=jnp.float32
+            ).reshape(rows_now, inner_width)
+            grad_value_rows = jnp.einsum(
+                "hqk,qhd->khd",
+                shares.astype(jnp.bfloat16),
+                grad_mixed,
+                preferred_element_type=jnp.float32,
+            ).reshape(rows_now, inner_width)
+            current = lax.dynamic_slice_in_dim(grad_kv_all, first_row, rows_now, 0)
+            grad_kv_all = lax.dynamic_update_slice_in_dim(
+                grad_kv_all,
+                current + jnp.concatenate([grad_key_rows, grad_value_rows], axis=1),
+                first_row,
+                0,
+            )
+            return (grad_query_acc, grad_kv_all)
+
+        return lax.cond(first_row > last_here, unchanged, compute, progress)
+
+    grad_query, grad_kv_all = blockwise(back_key_all.shape[0], visit, start_state)
+    grad_kv = lax.psum_scatter(
+        grad_kv_all.astype(jnp.bfloat16), "ctx", scatter_dimension=0, tiled=True
+    ).astype(jnp.float32)
+    grad_query_low = (
+        unrotate(grad_query.astype(jnp.bfloat16).astype(jnp.float32), cosine, sine)
+        .astype(jnp.bfloat16)
+        .reshape(length, inner_width)
+    )
+    grad_key_turned = (
+        grad_kv[:, :inner_width]
+        .reshape(length, HEADS, HEAD_DIM)
+        .astype(jnp.bfloat16)
+        .astype(jnp.float32)
+    )
+    grad_key_low = (
+        unrotate(grad_key_turned, cosine, sine).astype(jnp.bfloat16).reshape(length, inner_width)
+    )
+    grad_value_low = grad_kv[:, inner_width:].astype(jnp.bfloat16)
+    grad_wquery = jnp.dot(attn_input.T, grad_query_low, preferred_element_type=jnp.float32)
+    grad_wkey = jnp.dot(attn_input.T, grad_key_low, preferred_element_type=jnp.float32)
+    grad_wvalue = jnp.dot(attn_input.T, grad_value_low, preferred_element_type=jnp.float32)
+    grad_attn = (
+        jnp.dot(grad_query_low, w_query.T, preferred_element_type=jnp.float32)
+        + jnp.dot(grad_key_low, w_key.T, preferred_element_type=jnp.float32)
+        + jnp.dot(grad_value_low, w_value.T, preferred_element_type=jnp.float32)
+    )
+    grad_gain_one = jnp.sum(grad_attn * normed_one, axis=0)
+    scaled_one = grad_attn * gain_one_wide
+    grad_inputs = grad_hidden + factor_one * (
+        scaled_one - normed_one * jnp.mean(scaled_one * normed_one, axis=-1, keepdims=True)
+    )
+    owned = (
+        lax.psum_scatter(
+            grad_gain_one.astype(jnp.bfloat16), "fsdp", scatter_dimension=0, tiled=True
+        ).astype(jnp.float32),
+        lax.psum_scatter(
+            grad_wquery.astype(jnp.bfloat16), "fsdp", scatter_dimension=0, tiled=True
+        ).astype(jnp.float32),
+        lax.psum_scatter(
+            grad_wkey.astype(jnp.bfloat16), "fsdp", scatter_dimension=0, tiled=True
+        ).astype(jnp.float32),
+        lax.psum_scatter(
+            grad_wvalue.astype(jnp.bfloat16), "fsdp", scatter_dimension=0, tiled=True
+        ).astype(jnp.float32),
+        lax.psum_scatter(
+            grad_output.astype(jnp.bfloat16), "fsdp", scatter_dimension=0, tiled=True
+        ).astype(jnp.float32),
+        lax.psum_scatter(
+            grad_gain_two.astype(jnp.bfloat16), "fsdp", scatter_dimension=0, tiled=True
+        ).astype(jnp.float32),
+        lax.psum_scatter(
+            grad_router.astype(jnp.bfloat16), "fsdp", scatter_dimension=0, tiled=True
+        ).astype(jnp.float32),
+    )
+    (
+        own_gain_one,
+        own_wquery,
+        own_wkey,
+        own_wvalue,
+        own_output,
+        own_gain_two,
+        own_router,
+    ) = owned
+    dense = (
+        lax.psum(own_gain_one.astype(jnp.bfloat16), "ctx").astype(jnp.float32),
+        lax.psum(own_wquery.astype(jnp.bfloat16), "ctx").astype(jnp.float32),
+        lax.psum(own_wkey.astype(jnp.bfloat16), "ctx").astype(jnp.float32),
+        lax.psum(own_wvalue.astype(jnp.bfloat16), "ctx").astype(jnp.float32),
+        lax.psum(own_output.astype(jnp.bfloat16), "ctx").astype(jnp.float32),
+        lax.psum(own_gain_two.astype(jnp.bfloat16), "ctx").astype(jnp.float32),
+        lax.psum(own_router.astype(jnp.bfloat16), "ctx").astype(jnp.float32),
+    )
+    return (
+        output_rows[None],
+        grad_inputs.astype(jnp.bfloat16)[None],
+        dense[0],
+        dense[1],
+        dense[2],
+        dense[3],
+        dense[4],
+        dense[5],
+        dense[6],
+        own_shared_gate,
+        own_shared_up,
+        own_shared_down,
+        own_expert_gate,
+        own_expert_up,
+        own_expert_down,
+    )
+
+
 def solution(mesh):
+    fast = mesh.shape['ctx'] == 8 and mesh.shape['fsdp'] == NZ
+    body = per_device_fast if fast else per_device
     return jax.shard_map(
-        per_device,
+        body,
         mesh=mesh,
         in_specs=(
             P("fsdp", "ctx", None),

time: 1770 us -> 1470 us (0.83)
  waiting for transfers between devices: 1270 us -> 654 us
  Pallas kernels: 0 us -> 471 us
  matrix products: 139 us -> 57.8 us
  local copies, waits for them, and re-layouts: 186 us -> 131 us
  starting transfers between devices: 24 us -> 5.33 us
    pallas_call x0 -> x1, Pallas kernels: none -> 471 us  [expert_stage(): pl.pallas_call(expert_kernel, name='experts', out_shape=[shape((length, w...]
    reduce_scatter x10 -> x4, waiting for transfers between devices: 623 us -> 243 us  [the longest x1 64.9 us: per_device_fast(): lax.psum_scatter(grad_wvalue.astype(jnp.bfloat16), 'fsdp', scatter_dimens...]
    all_gather x12 -> x6, waiting for transfers between devices: 512 us -> 226 us  [the longest x1 60.3 us: per_device_fast(): lax.all_gather(key_weight, 'fsdp', axis=0, tiled=True)]
    dot_general x34 -> x16, matrix products: 113 us -> 30.2 us  [the longest x1 3.28 us: per_device_fast(): jnp.dot(grad_query_low, w_query.T, preferred_element_type=jnp.float32)]
    psum x1, waiting for transfers between devices: 55.7 us -> 90.9 us  [per_device_fast(): lax.psum(own_wquery.astype(jnp.bfloat16), 'ctx').astype(jnp.float32)]
    reshape x9 -> x4, local copies, waits for them, and re-layouts: 35.9 us -> 9.51 us  [slices(): parts = weights.reshape(weights.shape[0], weights.shape[1], NZ, hidden_dev)]
    unnamed x27 -> x15, waiting for transfers between devices: 69.3 us -> 93.5 us
  transfers between devices with their start and end apart: 29 -> 14, of which waited for: 25 -> 12; matrix products, arithmetic and copies ran while one was open for 14% -> 8% of each run, Pallas kernels for 0% -> 0%
where the time goes in v1:
time: 1470 us; the launch traced here: 1450 us
  waiting for transfers between devices  654 us (44%)
  Pallas kernels  471 us (32%)
  local copies, waits for them, and re-layouts  131 us (9%)
  blocking collectives  63.4 us (4%)
  matrix products  57.8 us (4%)
  other arithmetic  49.5 us (3%)
  between operations  16.3 us (1%)
    pallas_call x1, Pallas kernels, expert_stage(): pl.pallas_call(expert_kernel, name='experts', out_shape=[shape((length, w...  471 us
    unnamed x15, waiting for transfers between devices  93.5 us
    psum x1, waiting for transfers between devices, per_device_fast(): lax.psum(own_wquery.astype(jnp.bfloat16), 'ctx').astype(jnp.float32)  90.9 us
    reduce_scatter x1, waiting for transfers between devices, per_device_fast(): lax.psum_scatter(grad_wvalue.astype(jnp.bfloat16), 'fsdp', scatter_dimens...  64.9 us
    reduce_scatter x1, waiting for transfers between devices, per_device_fast(): lax.psum_scatter(grad_wkey.astype(jnp.bfloat16), 'fsdp', scatter_dimensio...  64.8 us
    reduce_scatter x1, waiting for transfers between devices, per_device_fast(): lax.psum_scatter(grad_wquery.astype(jnp.bfloat16), 'fsdp', scatter_dimens...  64.7 us
    all_gather x1, waiting for transfers between devices, per_device_fast(): lax.all_gather(key_weight, 'fsdp', axis=0, tiled=True)  60.3 us
    all_gather x1, waiting for transfers between devices, per_device_fast(): lax.all_gather(query_weight, 'fsdp', axis=0, tiled=True)  54.3 us
  transfers between devices with their start and end apart: 14, of which 12 were waited for; matrix products, arithmetic and copies ran while one was open for 8% of the time, Pallas kernels for 0%

profile of v1, /device:TPU:21, one launch (start us, length us, event | category | flops | bytes accessed | tf_op | source)
XLA Modules:
  0.0 1451.3 jit_solution(462873050266341426)
XLA Ops:
  13.2 7.1 all-reduce.12
  20.7 54.3 %all-gather.13.cloned.1.call-done = bf16[1280,1280]{1,0:T(8,128)(2,1)} async-done(((bf16[320,1280]{1,0:T(8,128)(2,1)}), bf16[1280,1280]{1,0:T(8,128)(2,1)}) %all-gather.13.cloned.1.call-update) | async-done | bytes 3276816 | tf_op jit(solution)/shard_map/all_gather | solution.py:968
  75.0 5.6 copy.102
  80.6 60.3 %all-gather.9.cloned.1.call-done = bf16[1280,1280]{1,0:T(8,128)(2,1)} async-done(((bf16[320,1280]{1,0:T(8,128)(2,1)}), bf16[1280,1280]{1,0:T(8,128)(2,1)}) %all-gather.9.cloned.1.call-update) | async-done | bytes 3276816 | tf_op jit(solution)/shard_map/all_gather | solution.py:969
  140.9 5.7 copy.101
  152.6 54.2 %all-gather.15.cloned.1.call-done = bf16[1280,1280]{1,0:T(8,128)(2,1)} async-done(((bf16[320,1280]{1,0:T(8,128)(2,1)}), bf16[1280,1280]{1,0:T(8,128)(2,1)}) %all-gather.15.cloned.1.call-update) | async-done | bytes 3276816 | tf_op jit(solution)/shard_map/all_gather | solution.py:970
  210.9 10.1 all-gather.1
  240.7 12.1 all-gather
  264.0 8.6 all-gather.17.cloned.1.call-done
  277.1 12.1 while.28
  278.3 4.7 conditional.6
  284.4 4.7 conditional.6
  289.5 48.8 %all-gather.19.cloned.1.call-done = bf16[1280,1280]{1,0:T(8,128)(2,1)} async-done(((bf16[320,1280]{1,0:T(8,128)(2,1)}), bf16[1280,1280]{1,0:T(8,128)(2,1)}) %all-gather.19.cloned.1.call-update) | async-done | bytes 3276816 | tf_op jit(solution)/shard_map/all_gather | solution.py:971
  342.0 471.0 %experts.1 = (f32[128,1280]{1,0:T(8,128)}, f32[128,1280]{1,0:T(8,128)}, f32[16,128]{1,0:T(8,128)}, bf16[4,2,320,512]{3,2,1,0:T(8,128)(2,1)}, f32[2,256,1280]{2,1...) custom-call(bf16[128,1280]{1,0:T(8,128)(2,1)} %copy-done.9, ...), custom_call_target="tpu_custom_call" | custom-call | tf_op jit(solution)/shard_map/experts/pallas_call | solution.py:470
  821.9 5.4 broadcast_in_dim.62
  828.2 80.9 %while.29 = (s32[]{:T(128)}, f32[128,10,128]{0,2,1:T(8,128)}, f32[1024,2560]{0,1:T(8,128)}, s32[2]{0:T(128)S(1)}, s32[]{:T(128)}, /*index=5*/bf16[1024,10,128]{2...) while((s32[]{:T(128)}, f32[128,10,128]{0,2,1:T(8,128)}, ...), condition=%wide.region_16.17_spmd.clone, body=%wide.region_13.16_spmd.clone.sunk | while | flops 850429056 | bytes 92767208 | solution.py:53
  829.5 39.6 %conditional.7 = ((f32[128,10,128]{0,2,1:T(8,128)}, f32[1024,2560]{0,1:T(8,128)})) conditional(s32[]{:T(128)} %convert_element_type.433, (s32[]{:T(128)}, bf16[1024,10,128]{2,0,1:T(8,128)(2,1)}, s32[]{:T(128)}, bf16[1024]{0:T(1024)(128)(2,1)S(1)}, f32[128]{0:T(128)S(1)}, /*index=5*/bf16[128,10,128]{0,2,1:T(8,128)(2,1)S(1)}, ...), branch_computations={%region_14.14_spmd, %region_15.15_spmd} | conditional | flops 850429056 | bytes 92766392 | solution.py:1184
  840.6 25.4 %dynamic_update_slice.2 = f32[1024,2560]{0,1:T(8,128)} dynamic-update-slice(f32[1024,2560]{0,1:T(8,128)} %get-tuple-element.195, f32[512,2560]{0,1:T(8,128)} %maximum_add_fusion, s32[]{:T(128)S(6)} %select_n.24, s32[]{:T(128)} %constant.39.clone) | dynamic-update-slice | bytes 10485764 | tf_op jit(solution)/shard_map/while/body/eval_jaxpr/cond/branch_0_fun/dynamic_update_slice | solution.py:1176
  870.3 38.7 %conditional.7 = ((f32[128,10,128]{0,2,1:T(8,128)}, f32[1024,2560]{0,1:T(8,128)})) conditional(s32[]{:T(128)} %convert_element_type.433, (s32[]{:T(128)}, bf16[1024,10,128]{2,0,1:T(8,128)(2,1)}, s32[]{:T(128)}, bf16[1024]{0:T(1024)(128)(2,1)S(1)}, f32[128]{0:T(128)S(1)}, /*index=5*/bf16[128,10,128]{0,2,1:T(8,128)(2,1)S(1)}, ...), branch_computations={%region_14.14_spmd, %region_15.15_spmd} | conditional | flops 850429056 | bytes 92766392 | solution.py:1184
  881.5 24.5 %dynamic_update_slice.2 = f32[1024,2560]{0,1:T(8,128)} dynamic-update-slice(f32[1024,2560]{0,1:T(8,128)} %get-tuple-element.195, f32[512,2560]{0,1:T(8,128)} %maximum_add_fusion, s32[]{:T(128)S(6)} %select_n.24, s32[]{:T(128)} %constant.39.clone) | dynamic-update-slice | bytes 10485764 | tf_op jit(solution)/shard_map/while/body/eval_jaxpr/cond/branch_0_fun/dynamic_update_slice | solution.py:1176
  909.1 7.1 convert_element_type.285
  916.1 7.8 copy.130
  929.3 67.4 %reduce-scatter.19.cloned.1.call-done = bf16[128,2560]{1,0:T(8,128)(2,1)} async-done(((bf16[1024,2560]{1,0:T(8,128)(2,1)}), bf16[128,2560]{1,0:T(8,128)(2,1)}) %reduce-scatter.19.cloned.1.call-update) | async-done | bytes 655376
  1013.1 48.8 %reduce-scatter.17.cloned.1.call-done = bf16[320,1280]{1,0:T(8,128)(2,1)} async-done(((bf16[1280,1280]{1,0:T(8,128)(2,1)}), bf16[320,1280]{1,0:T(8,128)(2,1)}) %reduce-scatter.17.cloned.1.call-update) | async-done | bytes 819216 | tf_op jit(solution)/shard_map/reduce_scatter | solution.py:1231
  1061.8 64.8 %reduce-scatter.13.cloned.1.call-done = bf16[320,1280]{1,0:T(8,128)(2,1)} async-done(((bf16[1280,1280]{1,0:T(8,128)(2,1)}), bf16[320,1280]{1,0:T(8,128)(2,1)}) %reduce-scatter.13.cloned.1.call-update) | async-done | bytes 819216 | tf_op jit(solution)/shard_map/reduce_scatter | solution.py:1225
  1126.6 64.7 %reduce-scatter.11.cloned.1.call-done = bf16[320,1280]{1,0:T(8,128)(2,1)} async-done(((bf16[1280,1280]{1,0:T(8,128)(2,1)}), bf16[320,1280]{1,0:T(8,128)(2,1)}) %reduce-scatter.11.cloned.1.call-update) | async-done | bytes 819216 | tf_op jit(solution)/shard_map/reduce_scatter | solution.py:1222
  1191.3 64.9 %reduce-scatter.15.cloned.1.call-done = bf16[320,1280]{1,0:T(8,128)(2,1)} async-done(((bf16[1280,1280]{1,0:T(8,128)(2,1)}), bf16[320,1280]{1,0:T(8,128)(2,1)}) %reduce-scatter.15.cloned.1.call-update) | async-done | bytes 819216 | tf_op jit(solution)/shard_map/reduce_scatter | solution.py:1228
  1263.5 90.9 %all-reduce.15.cloned.1.call-done = (bf16[320,1280]{1,0:T(8,128)(2,1)}, bf16[320,1280]{1,0:T(8,128)(2,1)}, bf16[320,1280]{1,0:T(8,128)(2,1)}, bf16[320,1280]{1,0...) async-done(((bf16[320,1280]{1,0:T(8,128)(2,1)}, bf16[320,1280]{1,0:T(8,128)(2,1)}, bf16[320,1280]{1,0:T(8,128)(2,1)}, bf16[320,1280]{1,0:T(8,128)(2,1)}, ...) | async-done | bytes 5160976 | tf_op jit(solution)/shard_map/psum | solution.py:1252
  1354.4 4.6 all-to-all-start
  1366.2 23.3 %reduce-scatter.21.cloned.1.call-done = bf16[320,16]{1,0:T(8,128)(2,1)} async-done(((bf16[1280,16]{1,0:T(8,128)(2,1)}), bf16[320,16]{1,0:T(8,128)(2,1)}) %reduce-scatter.21.cloned.1.call-update) | async-done | bytes 10256
  1397.2 6.7 all-reduce.11
  1404.0 27.4 %all-reduce.9 = (bf16[320]{0:T(512)(128)(2,1)S(1)}, bf16[320]{0:T(512)(128)(2,1)S(1)}, bf16[320,16]{0,1:T(8,128)(2,1)S(1)}) all-reduce(bf16[320]{0:T(512)(128)(2,1)S(1)} %dynamic-slice.3, bf16[320]{0:T(512)(128)(2,1)S(1)} %dynamic-slice.5, bf16[320,16]{0,1:T(8,128)(2,1)S(1)} %copy.133), channel_id=1, replica_groups=mesh['ctx'=8,'fsdp'=4] {'ctx'}, use_global_device_ids=true, to_apply=%region_21.22 | all-reduce | flops 5760 | bytes 23040 | tf_op jit(solution)/shard_map/psum | solution.py:1251
  (272 shorter events, 160.5 us)
Async XLA Ops:
  7.2 13.2 copy-start
  7.2 67.8 %all-gather.13.cloned.1.call-start = ((), (), s32[]{:S(2)}) async-start(), calls=%async_computation.9 | async-start | bytes 4096000 | tf_op jit(solution)/shard_map/all_gather | solution.py:968
  7.9 133.0 %all-gather.9.cloned.1.call-start = ((), (), s32[]{:S(2)}) async-start(), calls=%async_computation.7 | async-start | bytes 4096000 | tf_op jit(solution)/shard_map/all_gather | solution.py:969
  8.7 198.1 %all-gather.15.cloned.1.call-start = ((), (), s32[]{:S(2)}) async-start(), calls=%async_computation.10 | async-start | bytes 4096000 | tf_op jit(solution)/shard_map/all_gather | solution.py:970
  9.4 250.1 %all-gather.11.cloned.1.call-start = ((), (), s32[]{:S(2)}) async-start(), calls=%async_computation.8 | async-start | bytes 2949120 | tf_op jit(solution)/shard_map/all_gather | solution.py:1023
  152.5 58.4 %copy-start.30 = (bf16[320,16]{0,1:T(8,128)(2,1)S(1)}, bf16[320,16]{0,1:T(8,128)(2,1)}, u32[]{:S(2)}) copy-start(bf16[320,16]{0,1:T(8,128)(2,1)} %param.36) | copy-start | bytes 30724
  152.5 68.6 %copy-start.31 = (s32[1,128,7]{1,0,2:T(1,128)S(1)}, s32[1,128,7]{1,0,2:T(1,128)}, u32[]{:S(2)}) copy-start(s32[1,128,7]{1,0,2:T(1,128)} %param.28) | copy-start | bytes 10756
  152.5 120.0 %all-gather.17.cloned.1.call-start = ((), (), s32[]{:S(2)}) async-start(), calls=%async_computation.11 | async-start | bytes 2949120 | tf_op jit(solution)/shard_map/all_gather | solution.py:1024
  210.3 128.0 %all-gather.19.cloned.1.call-start = ((), (), s32[]{:S(2)}) async-start(), calls=%async_computation.12 | async-start | bytes 4096000 | tf_op jit(solution)/shard_map/all_gather | solution.py:971
  210.9 785.9 %reduce-scatter.19.cloned.1.call-start = ((), (), s32[]{:S(2)}) async-start(), calls=%async_computation.17 | async-start | bytes 5898240
  230.7 10.0 copy-start.32
  289.4 51.5 %copy-start.7 = (f32[10,128,128]{1,2,0:T(8,128)}, f32[10,128,128]{1,2,0:T(8,128)S(1)}, u32[]{:S(2)}) copy-start(f32[10,128,128]{1,2,0:T(8,128)S(1)} %copy.107) | copy-start | bytes 1966084
  289.5 51.5 %copy-start.11 = (bf16[10,128,128]{1,2,0:T(8,128)(2,1)}, bf16[10,128,128]{1,2,0:T(8,128)(2,1)S(1)}, u32[]{:S(2)}) copy-start(bf16[10,128,128]{1,2,0:T(8,128)(2,1)S(1)} %fusion.81) | copy-start | bytes 983044
  813.7 5.0 copy-start.3
  829.8 7.1 slice-start
  831.8 5.1 slice-start.1
  870.7 7.1 slice-start
  872.7 5.1 slice-start.1
  924.0 137.8 %reduce-scatter.17.cloned.1.call-start = ((), (), s32[]{:S(2)}) async-start(), calls=%async_computation.16 | async-start | bytes 4096000 | tf_op jit(solution)/shard_map/reduce_scatter | solution.py:1231
  927.9 198.7 %reduce-scatter.13.cloned.1.call-start = ((), (), s32[]{:S(2)}) async-start(), calls=%async_computation.14 | async-start | bytes 4096000 | tf_op jit(solution)/shard_map/reduce_scatter | solution.py:1225
  1001.1 190.2 %reduce-scatter.11.cloned.1.call-start = ((), (), s32[]{:S(2)}) async-start(), calls=%async_computation.13 | async-start | bytes 4096000 | tf_op jit(solution)/shard_map/reduce_scatter | solution.py:1222
  1004.0 252.2 %reduce-scatter.15.cloned.1.call-start = ((), (), s32[]{:S(2)}) async-start(), calls=%async_computation.15 | async-start | bytes 4096000 | tf_op jit(solution)/shard_map/reduce_scatter | solution.py:1228
  1007.9 346.5 %all-reduce.15.cloned.1.call-start = ((), (), s32[]{:S(2)}) async-start(), calls=%async_computation.19 | async-start | bytes 10321920 | tf_op jit(solution)/shard_map/psum | solution.py:1252
  1013.0 243.9 %copy-start.10 = (bf16[128,1280]{1,0:T(8,128)(2,1)S(1)}, bf16[128,1280]{1,0:T(8,128)(2,1)}, u32[]{:S(2)}) copy-start(bf16[128,1280]{1,0:T(8,128)(2,1)} %copy-done.9) | copy-start | bytes 983044
  1013.0 243.9 %copy-start.29 = (f32[16,128]{1,0:T(8,128)S(1)}, f32[16,128]{1,0:T(8,128)}, u32[]{:S(2)}) copy-start(f32[16,128]{1,0:T(8,128)} %get-tuple-element.244) | copy-start | bytes 24580
  1256.2 133.3 %reduce-scatter.21.cloned.1.call-start = ((), (), s32[]{:S(2)}) async-start(), calls=%async_computation.18 | async-start | bytes 409600
  1354.4 87.2 %all-to-all-start = ((bf16[4,320,512]{2,1,0:T(8,128)(2,1)}), bf16[4,320,512]{2,1,0:T(8,128)(2,1)S(1)}, u32[]{:S(2)}, u32[]{:S(2)}) async-start(bf16[4,320,512]{2,1,0:T(8,128)(2,1)} %get-tuple-element.488), calls=%async_computation.4 | async-start | bytes 2621440 | tf_op jit(solution)/shard_map/all_to_all | solution.py:1108
  1359.0 3.2 copy-start.19
  1359.0 3.2 copy-start.20
  1390.5 3.3 copy-start.1
  1431.4 5.3 copy-start.24
  1434.2 3.8 copy-start.23
  (24 other events, 49.2 us)
Sparse Core Ops, SparseCore 0:
  9.6 65.3 all-gather.12
  76.6 64.2 all-gather.8
  142.5 64.2 all-gather.14
  209.1 30.5 all-gather.10
  242.0 30.4 all-gather.16
  273.9 64.2 all-gather.18
  924.1 72.6 reduce-scatter.18
  999.2 62.5 reduce-scatter.16
  1064.2 62.3 reduce-scatter.12
  1128.9 62.3 reduce-scatter.10
  1193.8 62.3 reduce-scatter.14
  1261.9 92.5 all-reduce.14
  1357.4 32.0 reduce-scatter.20

commit v2 on v0

--- a/solution.py
+++ b/solution.py
@@ -1,8 +1,11 @@
+import functools
 import math
 
 import jax
 import jax.numpy as jnp
 from jax import lax
+from jax.experimental import pallas as pl
+from jax.experimental.pallas import tpu as pltpu
 from jax.sharding import PartitionSpec as P
 
 D = 1280
@@ -67,6 +70,1151 @@
 
 def unchanged(progress):
     return progress
+
+
+NZ = 4
+SLOTS = 64
+WIDE = 256
+MESH = pl.DeviceIdType.MESH
+PEERS = ((0, 1), (1, 0), (1, 1))
+NN = (((1,), (0,)), ((), ()))
+NT = (((1,), (1,)), ((), ()))
+TN = (((0,), (0,)), ((), ()))
+MIB = 1024 * 1024
+
+
+def dot(left, right, dims=NN):
+    return lax.dot_general(left, right, dims, preferred_element_type=jnp.float32)
+
+
+def split_dot(left, right, dims=NN):
+    high = left.astype(jnp.bfloat16)
+    low = (left - high.astype(jnp.float32)).astype(jnp.bfloat16)
+    return dot(high, right, dims) + dot(low, right, dims)
+
+
+def flip(c, fy, fx, fk):
+    return 4 * ((c // 4 + fy) % 2) + 2 * (((c // 2) % 2 + fx) % 2) + (c % 2 + fk) % 2
+
+
+def rows_at(start, count):
+    return pl.ds(pl.multiple_of(start, 16), count)
+
+
+def lanes_at(start, count):
+    return pl.ds(pl.multiple_of(start, 128), count)
+
+
+def remote(src, dst, send, recv, c, z):
+    return pltpu.make_async_remote_copy(
+        src_ref=src, dst_ref=dst, send_sem=send, recv_sem=recv, device_id=(c, z), device_id_type=MESH
+    )
+
+
+def greet(c, z):
+    barrier = pltpu.get_barrier_semaphore()
+    peers = [(c, (z + d) % NZ) for d in range(1, NZ)]
+    peers += [(flip(c, fy, fx, 0), z) for fy, fx in PEERS] + [(flip(c, 0, 0, 1), z)]
+    for peer in peers:
+        pl.semaphore_signal(barrier, inc=1, device_id=peer, device_id_type=MESH)
+    pl.semaphore_wait(barrier, len(peers))
+
+
+class Spread:
+    def __init__(self, src, block, sems, c, z, hops=NZ, peers=PEERS, copy_own=True):
+        self.src, self.block, self.c, self.z = src, block, c, z
+        self.hops, self.peers, self.all = hops, peers, ((0, 0),) + peers
+        self.local, self.zs, self.zr, self.xs, self.xr, self.ms, self.mr = sems
+        self.own = pltpu.make_async_copy(src(z), block(c, z), self.local) if copy_own else None
+
+    def at(self, c, d):
+        return self.block(c, (self.z + NZ - d) % NZ)
+
+    def mine(self, c, d):
+        return self.src(self.z) if d == 0 else self.at(c, d)
+
+    def zcopy(self, d):
+        there = (self.z + d) % NZ
+        return remote(
+            self.src(there), self.block(self.c, self.z), self.zs.at[d - 1], self.zr.at[d - 1], self.c, there
+        )
+
+    def zwait(self, d):
+        block = self.at(self.c, d)
+        remote(block, block, self.zs.at[d - 1], self.zr.at[d - 1], self.c, self.z).wait_recv()
+
+    def xcopy(self, i, d):
+        there = flip(self.c, self.peers[i][0], self.peers[i][1], 0)
+        return remote(self.mine(self.c, d), self.at(self.c, d), self.xs.at[i, d], self.xr.at[i, d], there, self.z)
+
+    def xwait(self, i, d):
+        block = self.at(flip(self.c, self.peers[i][0], self.peers[i][1], 0), d)
+        remote(block, block, self.xs.at[i, d], self.xr.at[i, d], self.c, self.z).wait_recv()
+
+    def mcopy(self, i, d):
+        origin = flip(self.c, self.all[i][0], self.all[i][1], 0)
+        src = self.mine(origin, d) if i == 0 else self.at(origin, d)
+        return remote(src, self.at(origin, d), self.ms.at[i, d], self.mr.at[i, d], flip(self.c, 0, 0, 1), self.z)
+
+    def mwait(self, i, d):
+        block = self.at(flip(self.c, self.all[i][0], self.all[i][1], 1), d)
+        remote(block, block, self.ms.at[i, d], self.mr.at[i, d], self.c, self.z).wait_recv()
+
+    def start_z(self):
+        if self.own is not None:
+            self.own.start()
+        for d in range(1, self.hops):
+            self.zcopy(d).start()
+
+    def start_x(self):
+        for i in range(len(self.peers)):
+            self.xcopy(i, 0).start()
+        self.mcopy(0, 0).start()
+
+    def relay_z(self):
+        for d in range(1, self.hops):
+            self.zwait(d)
+            for i in range(len(self.peers)):
+                self.xcopy(i, d).start()
+            self.mcopy(0, d).start()
+
+    def relay_x(self):
+        for d in range(self.hops):
+            for i in range(len(self.peers)):
+                self.xwait(i, d)
+                self.mcopy(i + 1, d).start()
+
+    def arrive(self):
+        if self.own is not None:
+            self.own.wait()
+        for d in range(self.hops):
+            for i in range(len(self.all)):
+                self.mwait(i, d)
+
+    def drain(self):
+        for d in range(1, self.hops):
+            self.zcopy(d).wait_send()
+        for d in range(self.hops):
+            for i in range(len(self.peers)):
+                self.xcopy(i, d).wait_send()
+            for i in range(len(self.all)):
+                self.mcopy(i, d).wait_send()
+
+
+def spread_sems(hops=NZ, peers=3):
+    dma = pltpu.SemaphoreType.DMA
+    return [
+        dma, dma((3,)), dma((3,)), dma((peers, hops)), dma((peers, hops)), dma((peers + 1, hops)), dma((peers + 1, hops)),
+    ]
+
+
+def plane_reduce(part, c, z, refs):
+    out4, in4, out3, in3, ms, mr, xs, xr = refs
+    mate = flip(c, 0, 0, 1)
+    order = PEERS + ((0, 0),)
+
+    def to_mate(i):
+        return remote(out4.at[i], in4.at[i], ms.at[i], mr.at[i], mate, z)
+
+    def to_chip(i):
+        return remote(out3.at[i], in3.at[i], xs.at[i], xr.at[i], flip(c, PEERS[i][0], PEERS[i][1], 0), z)
+
+    for i, (fy, fx) in enumerate(order):
+        out4[i] = part(flip(c, fy, fx, 1)).astype(jnp.bfloat16)
+        to_mate(i).start()
+    for i, (fy, fx) in enumerate(order):
+        value = part(flip(c, fy, fx, 0))
+        to_mate(i).wait_recv()
+        value = value + in4[i].astype(jnp.float32)
+        if i < 3:
+            out3[i] = value.astype(jnp.bfloat16)
+            to_chip(i).start()
+    for i in range(3):
+        to_chip(i).wait_recv()
+        value = value + in3[i].astype(jnp.float32)
+    for i in range(4):
+        to_mate(i).wait_send()
+    for i in range(3):
+        to_chip(i).wait_send()
+    return value
+
+
+def plane_scratch(length, width):
+    dma = pltpu.SemaphoreType.DMA
+    block = lambda n: pltpu.VMEM((n, length, width), jnp.bfloat16)
+    return [block(4), block(4), block(3), block(3), dma((4,)), dma((4,)), dma((3,)), dma((3,))]
+
+
+def swish(values):
+    sigma = 1.0 / (1.0 + jnp.exp(-values))
+    return values * sigma, sigma * (1.0 + values * (1.0 - sigma))
+
+
+def norm_factor(values):
+    return lax.rsqrt(jnp.mean(values * values, axis=1, keepdims=True) + epsilon)
+
+
+def turned(values, cosine, sine):
+    return values * cosine + pltpu.roll(values, 64, 1) * sine
+
+
+def head_rows(c):
+    blocks = [2 * c, 2 * c + 1, 16 + 2 * (c // 4), 17 + 2 * (c // 4)]
+    return [(b, b // 5) for b in blocks]
+
+
+def visible(first, count, keys, boundary):
+    query = (lax.broadcasted_iota(jnp.int32, (count, 1), 0) + first).astype(jnp.float32)
+    key = lax.broadcasted_iota(jnp.int32, (1, keys), 1).astype(jnp.float32)
+    query_doc = jnp.where(query >= boundary, 1.0, 0.0)
+    key_doc = jnp.where(key >= boundary, 1.0, 0.0)
+    return (key <= query) & (key_doc == query_doc)
+
+
+def attention_kernel(
+    capacity,
+    x_ref, p_ref, docs_ref, routes_ref, prio_ref, cos_ref, sin_ref, g_ref, wq_ref, wk_ref, wv_ref, wo_ref, wsend_ref,
+    hidden_ref, b_ref, table_ref, gates_ref, psum_ref, bound_ref, aall, wall, woall, q1, k1, v1, q2, k2, v2,
+    att1, lse1, att2, lse2, mixed, gall, wgu,
+    xall, docs, pall, *sems,
+):
+    f32, bf16 = jnp.float32, jnp.bfloat16
+    c = lax.axis_index("ctx")
+    z = lax.axis_index("fsdp")
+    length, width = x_ref.shape
+    count = aall.shape[0]
+    shard = width // NZ
+    sub = shard // 4
+    quarter = c % 4
+    sems = list(sems)
+
+    def take(n):
+        taken = sems[:n]
+        del sems[:n]
+        return taken
+
+    spread_x = Spread(lambda _: x_ref, lambda o, _: xall.at[o], take(7), c, z, 1)
+    spread_docs = Spread(lambda _: docs_ref, lambda o, _: docs.at[o], take(7), c, z, 1)
+    second = lambda o, s: wall.at[rows_at(s * shard + (o % 4) * sub, sub), 384:768]
+    spread_h2 = Spread(lambda _: second(c, z), second, take(7), c, z, NZ, ((0, 1),), False)
+    spread_g = Spread(lambda _: g_ref, lambda o, s: gall.at[o, s], take(7), c, z)
+    shared_in = lambda s: wsend_ref.at[s, 2, rows_at((c // 2) * sub, sub), lanes_at(c % 2 * WIDE, WIDE)]
+    shared_to = lambda o, s: wgu.at[2, rows_at(s * shard + (o // 2) * sub, sub), lanes_at(o % 2 * WIDE, WIDE)]
+    spread_s = Spread(shared_in, shared_to, take(7), c, z)
+    ps, pr, wl, w1s, w1r, wol, wos, wor, wgl, wgs, wgr = take(11)
+    reduce_refs = take(8)
+    greet(c, z)
+    spread_x.start_z()
+    spread_x.start_x()
+    spread_docs.start_z()
+    spread_docs.start_x()
+
+    def pcopy(d):
+        return remote(p_ref, pall.at[d - 1], ps.at[d - 1], pr.at[d - 1], c, (z + d) % NZ)
+
+    for d in range(1, NZ):
+        pcopy(d).start()
+    own_rows = rows_at(z * shard, shard)
+    sub_rows = rows_at(z * shard + quarter * sub, sub)
+    copies = []
+    for i, ref in enumerate((wq_ref, wk_ref, wv_ref)):
+        copies.append(
+            pltpu.make_async_copy(
+                ref.at[:, lanes_at(c * 128, 128)], wall.at[own_rows, i * 128 : (i + 1) * 128], wl.at[i]
+            )
+        )
+        copies.append(
+            pltpu.make_async_copy(
+                ref.at[rows_at(quarter * sub, sub), lanes_at((8 + c // 4) * 128, 128)],
+                wall.at[sub_rows, 384 + i * 128 : 512 + i * 128],
+                wl.at[3 + i],
+            )
+        )
+    for copy in copies:
+        copy.start()
+    for copy in copies:
+        copy.wait()
+
+    def h1copy(d):
+        return remote(
+            wall.at[own_rows, 0:384], wall.at[own_rows, 0:384], w1s.at[d - 1], w1r.at[d - 1], c, (z + d) % NZ
+        )
+
+    def h1wait(d):
+        here = wall.at[rows_at((z + NZ - d) % NZ * shard, shard), 0:384]
+        remote(here, here, w1s.at[d - 1], w1r.at[d - 1], c, z).wait_recv()
+
+    spread_h2.start_z()
+    for d in range(1, NZ):
+        h1copy(d).start()
+    spread_h2.start_x()
+
+    def wo_local(j):
+        b, _ = head_rows(c)[j]
+        return pltpu.make_async_copy(wo_ref.at[rows_at(b % 5 * 64, 64)], woall.at[64 * j : 64 * j + 64], wol.at[j])
+
+    def wo_remote(j, d):
+        b, _ = head_rows(c)[j]
+        return remote(
+            wo_ref.at[rows_at(b % 5 * 64, 64)], woall.at[64 * j : 64 * j + 64],
+            wos.at[j, d - 1], wor.at[j], c, (z + d) % NZ,
+        )
+
+    for j, (_, owner) in enumerate(head_rows(c)):
+
+        @pl.when(owner == z)
+        def _(j=j):
+            wo_local(j).start()
+            for d in range(1, NZ):
+                wo_remote(j, d).start()
+
+    spread_x.relay_x()
+    spread_docs.relay_x()
+    packed = p_ref[...].astype(f32)
+    for d in range(1, NZ):
+        pcopy(d).wait_recv()
+        packed = packed + pall[d - 1].astype(f32)
+    psum_ref[...] = packed
+    gain_one = packed[17:18]
+    gain_two = packed[16:17]
+    spread_x.arrive()
+
+    def make_a(i, carry):
+        values = xall[i].astype(f32)
+        aall[rows_at(i * length, length)] = (values * norm_factor(values) * gain_one).astype(bf16)
+        return carry
+
+    lax.fori_loop(0, 8, make_a, 0)
+    spread_h2.relay_z()
+    spread_h2.relay_x()
+    spread_h2.arrive()
+    for d in range(1, NZ):
+        h1wait(d)
+
+    def wgcopy(d):
+        there = (z + d) % NZ
+        return remote(
+            wsend_ref.at[there, 0:2], wgu.at[0:2, own_rows, :], wgs.at[d - 1], wgr.at[d - 1], c, there
+        )
+
+    def wgwait(d):
+        here = wgu.at[0:2, rows_at((z + NZ - d) % NZ * shard, shard), :]
+        remote(here, here, wgs.at[d - 1], wgr.at[d - 1], c, z).wait_recv()
+
+    wgown = pltpu.make_async_copy(wsend_ref.at[z, 0:2], wgu.at[0:2, own_rows, :], wgl)
+    spread_g.start_z()
+    spread_g.start_x()
+    spread_s.start_z()
+    spread_s.start_x()
+    wgown.start()
+    for d in range(1, NZ):
+        wgcopy(d).start()
+    step = 2 * length
+    for i in range(count // step):
+        part = slice(i * step, (i + 1) * step)
+        values = dot(aall[part], wall[...])
+        cosine, sine = cos_ref[part], sin_ref[part]
+        q1[part] = turned(values[:, 0:128], cosine, sine).astype(bf16)
+        k1[part] = turned(values[:, 128:256], cosine, sine).astype(bf16)
+        v1[part] = values[:, 256:384].astype(bf16)
+        q2[part] = turned(values[:, 384:512], cosine, sine).astype(bf16)
+        k2[part] = turned(values[:, 512:640], cosine, sine).astype(bf16)
+        v2[part] = values[:, 640:768].astype(bf16)
+    spread_docs.arrive()
+    flags = jnp.where(docs[...] == 0.0, 1.0, 0.0)
+    boundary = jnp.sum(jnp.sum(flags, axis=0), axis=(0, 1), keepdims=True)
+    bound_ref[...] = jnp.broadcast_to(boundary, bound_ref.shape)
+    spread_g.relay_z()
+    spread_s.relay_z()
+
+    def attend(queries, first, keys, values, n):
+        scores = dot(queries, keys[0:n], NT) * (HEAD_DIM**-0.5)
+        scores = jnp.where(visible(first, step, n, boundary), scores, negative)
+        top = jnp.max(scores, axis=1, keepdims=True)
+        shares = jnp.exp(scores - top)
+        total = jnp.sum(shares, axis=1, keepdims=True)
+        probs = (shares * (1.0 / total)).astype(bf16)
+        return dot(probs, values[0:n]), jnp.broadcast_to(top + jnp.log(total), (step, 128))
+
+    mixed[...] = jnp.zeros_like(mixed)
+    for i in range(count // step):
+        part = slice(i * step, (i + 1) * step)
+        out, lse = attend(q1[part], i * step, k1, v1, (i + 1) * step)
+        att1[part] = out
+        lse1[part] = lse
+        mixed[part, 0:128] = out.astype(bf16)
+    mine = rows_at(quarter * step, step)
+    out, lse = attend(q2[mine], quarter * step, k2, v2, count)
+    att2[...] = out
+    lse2[...] = lse
+    mixed[mine, 128:256] = out.astype(bf16)
+    spread_s.relay_x()
+    for j, (_, owner) in enumerate(head_rows(c)):
+
+        @pl.when(owner == z)
+        def _(j=j):
+            wo_local(j).wait()
+            for d in range(1, NZ):
+                wo_remote(j, d).wait_send()
+
+        @pl.when(owner != z)
+        def _(j=j):
+            wo_remote(j, 1).wait_recv()
+
+    value = plane_reduce(lambda o: dot(mixed[rows_at(o * length, length)], woall[...]), c, z, reduce_refs)
+    hidden = x_ref[...].astype(f32) + value
+    hidden_ref[...] = hidden
+    tokens = (hidden * norm_factor(hidden) * gain_two).astype(bf16)
+    b_ref[...] = tokens
+    logits = dot(packed[0:16].astype(bf16), tokens, NT)
+    shifted = jnp.exp(logits - jnp.max(logits, axis=0, keepdims=True))
+    gates = shifted / jnp.sum(shifted, axis=0, keepdims=True)
+    gates_ref[...] = gates
+    lane = lax.broadcasted_iota(jnp.int32, (length, 128), 1)
+    named = jnp.zeros((length, 128), f32)
+    for k in range(routes_ref.shape[1]):
+        named = named + jnp.where(lane == routes_ref[:, k : k + 1], 1.0, 0.0)
+    named = named.T[0:16]
+    order = jnp.broadcast_to(prio_ref[...].astype(f32), (length, length))
+    earlier = jnp.where(order.T < order, 1.0, 0.0).astype(bf16)
+    rank = dot(named.astype(bf16), earlier)
+    kept = (named > 0.0) & (rank < float(capacity))
+    table_ref[:, 0:length] = jnp.where(kept, rank, -1.0)
+    table_ref[:, length : 2 * length] = jnp.where(kept, gates, 0.0)
+    spread_g.relay_x()
+    spread_g.arrive()
+    spread_s.arrive()
+    wgown.wait()
+    for d in range(1, NZ):
+        wgwait(d)
+        wgcopy(d).wait_send()
+        h1copy(d).wait_send()
+        pcopy(d).wait_send()
+    for spread in (spread_x, spread_docs, spread_h2, spread_g, spread_s):
+        spread.drain()
+
+
+def attention_stage(capacity, x, packed, docs, routes, prio, cosine, sine, upstream, wq, wk, wv, wo, wsend):
+    length, width = x.shape
+    count = cosine.shape[0]
+    dma = pltpu.SemaphoreType.DMA
+    hbm = pl.BlockSpec(memory_space=pl.ANY)
+    vmem = pl.BlockSpec(memory_space=pltpu.VMEM)
+    f32, bf16 = jnp.float32, jnp.bfloat16
+    shape = jax.ShapeDtypeStruct
+    head = lambda rows, kind: shape((rows, HEAD_DIM), kind)
+    return pl.pallas_call(
+        functools.partial(attention_kernel, capacity),
+        name="attention",
+        out_shape=[
+            shape((length, width), f32), shape((length, width), bf16), shape((16, 2 * length), f32),
+            shape((16, length), f32), shape((32, width), f32), shape((8, 128), f32),
+            shape((count, width), bf16), shape((width, 768), bf16), shape((256, width), bf16),
+            head(count, bf16), head(count, bf16), head(count, bf16), head(count, bf16), head(count, bf16),
+            head(count, bf16), head(count, f32), head(count, f32), head(2 * length, f32), head(2 * length, f32),
+            shape((count, 256), bf16), shape((8, NZ, length, width), bf16), shape((3, width, 2 * WIDE), bf16),
+        ],
+        in_specs=[vmem] * 7 + [hbm] * 6,
+        out_specs=[vmem] * 20 + [hbm] * 2,
+        scratch_shapes=[
+            pltpu.VMEM((8, length, width), bf16), pltpu.VMEM((8, 8, 128), f32), pltpu.VMEM((3, 32, width), bf16),
+        ]
+        + spread_sems(1) + spread_sems(1) + spread_sems(NZ, 1) + spread_sems() + spread_sems()
+        + [
+            dma((3,)), dma((3,)), dma((6,)), dma((3,)), dma((3,)), dma((4,)), dma((4, 3)), dma((4,)),
+            dma, dma((3,)), dma((3,)),
+        ]
+        + plane_scratch(length, width),
+        compiler_params=pltpu.CompilerParams(
+            collective_id=2, has_side_effects=True, vmem_limit_bytes=60 * MIB
+        ),
+    )(x, packed, docs, routes, prio, cosine, sine, upstream, wq, wk, wv, wo, wsend)
+
+
+def expert_kernel(
+    b_ref, t_ref, gall, wgu, wdn_ref,
+    y_ref, db_ref, dg_ref, dgu_ref, ddn_ref, dsgu_ref, dsdn_ref, ball, tall, mrecv, xrecv,
+    acc, bg, gg, tg, oh, xs, gs, ys, ds, st, ld, zbuf, zrecv, gst,
+    sb0, sb1, sb2, sb3, sb4, sb5, sb6, st0, st1, st2, st3, st4, st5, st6,
+    lsem, ms, mr, xs_s, xs_r, ldsem, zs, zr, gl, gss, grs,
+):
+    c = lax.axis_index("ctx")
+    z = lax.axis_index("fsdp")
+    f32, bf16 = jnp.float32, jnp.bfloat16
+    mate = flip(c, 0, 0, 1)
+    length = b_ref.shape[0]
+    group = NZ * length
+    rows = wgu.shape[1] // NZ
+    greet(c, z)
+    spread_b = Spread(lambda _: b_ref, lambda o, q: ball.at[o, q], (sb0, sb1, sb2, sb3, sb4, sb5, sb6), c, z)
+    spread_t = Spread(lambda _: t_ref, lambda o, q: tall.at[o, q], (st0, st1, st2, st3, st4, st5, st6), c, z)
+    for spread in (spread_t, spread_b):
+        spread.start_z()
+        spread.start_x()
+    acc[...] = jnp.zeros_like(acc)
+    ddn_ref[...] = jnp.zeros_like(ddn_ref)
+    st[...] = jnp.zeros_like(st)
+    zbuf[...] = jnp.zeros_like(zbuf)
+    spread_t.relay_z()
+    spread_b.relay_z()
+    spread_t.relay_x()
+    spread_b.relay_x()
+    spread_t.arrive()
+    spread_b.arrive()
+
+    def target(g):
+        left = 3 - g // 2
+        return flip(c, left % 2, left // 2, 1 - g % 2)
+
+    def loads(g):
+        slot = g % 2
+        there = target(g)
+        return (
+            pltpu.make_async_copy(ball.at[there], bg.at[slot], lsem.at[slot, 0]),
+            pltpu.make_async_copy(gall.at[there], gg.at[slot], lsem.at[slot, 1]),
+            pltpu.make_async_copy(tall.at[there], tg.at[slot], lsem.at[slot, 2]),
+        )
+
+    def to_mate(s):
+        return remote(st.at[0], mrecv.at[s], ms.at[s], mr.at[s], mate, z)
+
+    def to_chip(s):
+        left = 3 - s
+        return remote(st.at[1], xrecv.at[s], xs_s.at[s], xs_r.at[s], flip(c, left % 2, left // 2, 0), z)
+
+    for copy in loads(0):
+        copy.start()
+    slot_ids = lax.broadcasted_iota(jnp.int32, (SLOTS, length), 0).astype(f32)
+    row_ids = lax.broadcasted_iota(jnp.int32, (16, length), 0)
+    table_rows = lax.broadcasted_iota(jnp.int32, (16, 2 * length), 0)
+
+    def step(g, carry):
+        slot = g % 2
+        s = g // 2
+        par = g % 2
+        for copy in loads(g):
+            copy.wait()
+
+        @pl.when(g < 7)
+        def _():
+            for copy in loads(g + 1):
+                copy.start()
+
+        @pl.when((s > 0) & (par == 0))
+        def _():
+            to_mate(s - 1).wait_send()
+
+        @pl.when((s > 0) & (par == 1))
+        def _():
+            to_chip(s - 1).wait_send()
+
+        scales = [[], []]
+        for q in range(NZ):
+            hits = []
+            for e in range(2):
+                mine = jnp.sum(jnp.where(table_rows == 2 * c + e, tg[slot, q], 0.0), axis=0, keepdims=True)
+                rank = mine[:, :length]
+                share = mine[:, length:]
+                hit = slot_ids == rank
+                scales[e].append(jnp.sum(jnp.where(hit, share, 0.0), axis=1, keepdims=True))
+                hits.append(jnp.where(hit, 1.0, 0.0))
+            hot = jnp.concatenate(hits, axis=0).astype(bf16)
+            oh[q] = hot
+            part = dot(hot, bg[slot, q]).astype(bf16)
+            xs[0, q * SLOTS : (q + 1) * SLOTS] = part[:SLOTS]
+            xs[1, q * SLOTS : (q + 1) * SLOTS] = part[SLOTS:]
+            part = dot(hot, gg[slot, q]).astype(bf16)
+            gs[0, q * SLOTS : (q + 1) * SLOTS] = part[:SLOTS]
+            gs[1, q * SLOTS : (q + 1) * SLOTS] = part[SLOTS:]
+        back = [0.0] * NZ
+        for e in range(2):
+            scale = jnp.concatenate(scales[e], axis=0)
+            both = dot(xs[e], wgu[e])
+            up = both[:, WIDE:]
+            silu, slope = swish(both[:, :WIDE])
+            inner = (silu * up).astype(bf16)
+            scaled = (inner.astype(f32) * scale).astype(bf16)
+            out = dot(scaled, wdn_ref[e]).astype(bf16)
+            pull = dot(gs[e], wdn_ref[e], NT)
+            gain = jnp.sum(inner.astype(f32) * pull, axis=1, keepdims=True)
+            pull = pull * scale
+            turn = jnp.concatenate([(pull * up * slope).astype(bf16), (pull * silu).astype(bf16)], axis=1)
+            ddn_ref[e] += dot(scaled, gs[e], TN)
+            acc[e] += dot(xs[e], turn, TN)
+            into = dot(turn, wgu[e], NT).astype(bf16)
+            for q in range(NZ):
+                part = slice(q * SLOTS, (q + 1) * SLOTS)
+                ys[q, e * SLOTS : (e + 1) * SLOTS] = out[part]
+                ds[q, e * SLOTS : (e + 1) * SLOTS] = into[part]
+                hit = oh[q, e * SLOTS : (e + 1) * SLOTS].astype(f32)
+                line = jnp.sum(hit * gain[part], axis=0, keepdims=True)
+                back[q] = back[q] + jnp.where(row_ids == 2 * c + e, line, 0.0)
+        for q in range(NZ):
+            st[par, q * length : (q + 1) * length] = dot(oh[q], ds[q], TN).astype(bf16)
+            st[par, group + q * length : group + (q + 1) * length] = dot(oh[q], ys[q], TN).astype(bf16)
+            st[par, 2 * group :, q * length : (q + 1) * length] = back[q].astype(bf16)
+
+        @pl.when(g == 7)
+        def _():
+            for h in range(2):
+                tokens = bg[slot, 2 * h : 2 * h + 2].reshape(2 * length, bg.shape[3])
+                upper = gg[slot, 2 * h : 2 * h + 2].reshape(2 * length, bg.shape[3])
+                both = dot(tokens, wgu[2])
+                up = both[:, WIDE:]
+                silu, slope = swish(both[:, :WIDE])
+                inner = (silu * up).astype(bf16)
+                part = slice(2 * h * length, 2 * (h + 1) * length)
+                more = slice(group + 2 * h * length, group + 2 * (h + 1) * length)
+                st[1, more] = (st[1, more].astype(f32) + dot(inner, wdn_ref[2])).astype(bf16)
+                pull = dot(upper, wdn_ref[2], NT)
+                turn = jnp.concatenate([(pull * up * slope).astype(bf16), (pull * silu).astype(bf16)], axis=1)
+                st[1, part] = (st[1, part].astype(f32) + dot(turn, wgu[2], NT)).astype(bf16)
+                if h == 0:
+                    dsdn_ref[...] = dot(inner, upper, TN)
+                    dsgu_ref[...] = dot(tokens, turn, TN)
+                else:
+                    dsdn_ref[...] += dot(inner, upper, TN)
+                    dsgu_ref[...] += dot(tokens, turn, TN)
+
+        @pl.when(par == 0)
+        def _():
+            to_mate(s).start()
+
+        @pl.when(par == 1)
+        def _():
+            to_mate(s).wait_recv()
+            copy = pltpu.make_async_copy(mrecv.at[s], ld.at[0], ldsem.at[0])
+            copy.start()
+            copy.wait()
+
+            def add(i, carry):
+                part = pl.ds(pl.multiple_of(i * 16, 16), 16)
+                st[1, part] = (st[1, part].astype(f32) + ld[0, part].astype(f32)).astype(bf16)
+                return carry
+
+            lax.fori_loop(0, st.shape[1] // 16, add, 0)
+
+            @pl.when(s < 3)
+            def _():
+                to_chip(s).start()
+
+        return carry
+
+    lax.fori_loop(0, 8, step, 0)
+    to_mate(3).wait_send()
+    for e in range(2):
+        gst[e] = acc[e].astype(bf16)
+
+    def gcopy(d):
+        there = (z + d) % NZ
+        return remote(
+            gst.at[:, pl.ds(pl.multiple_of(there * rows, rows), rows), :], dgu_ref.at[z],
+            gss.at[d - 1], grs.at[d - 1], c, there,
+        )
+
+    gown = pltpu.make_async_copy(gst.at[:, pl.ds(pl.multiple_of(z * rows, rows), rows), :], dgu_ref.at[z], gl)
+    gown.start()
+    for i in range(3):
+        to_chip(i).wait_recv()
+        pltpu.make_async_copy(xrecv.at[i], ld.at[i], ldsem.at[i]).start()
+    for i in range(3):
+        pltpu.make_async_copy(xrecv.at[i], ld.at[i], ldsem.at[i]).wait()
+
+    def total(part, lanes=slice(None)):
+        value = st[1, part, lanes].astype(f32)
+        for i in range(3):
+            value = value + ld[i, part, lanes].astype(f32)
+        return value.astype(bf16)
+
+    for q in range(NZ):
+
+        def add(i, carry):
+            base = pl.multiple_of(i * 16, 16)
+            zbuf[q, pl.ds(base, 16)] = total(pl.ds(pl.multiple_of(base + q * length, 16), 16))
+            zbuf[q, pl.ds(pl.multiple_of(base + length, 16), 16)] = total(
+                pl.ds(pl.multiple_of(base + group + q * length, 16), 16)
+            )
+            return carry
+
+        lax.fori_loop(0, length // 16, add, 0)
+        zbuf[q, 2 * length : 2 * length + 16, 0:length] = total(
+            slice(2 * group, 2 * group + 16), slice(q * length, (q + 1) * length)
+        )
+
+    def zcopy(d):
+        there = (z + d) % NZ
+        return remote(zbuf.at[there], zrecv.at[d - 1], zs.at[d - 1], zr.at[d - 1], c, there)
+
+    for d in range(1, NZ):
+        zcopy(d).start()
+    for d in range(1, NZ):
+        gcopy(d).start()
+    for d in range(1, NZ):
+        zcopy(d).wait_recv()
+
+    def settle(i, carry):
+        base = pl.multiple_of(i * 16, 16)
+        for ref, start in ((db_ref, 0), (y_ref, length)):
+            part = pl.ds(pl.multiple_of(base + start, 16), 16)
+            value = zbuf[z, part].astype(f32)
+            for d in range(3):
+                value = value + zrecv[d, part].astype(f32)
+            ref[pl.ds(base, 16)] = value
+        return carry
+
+    lax.fori_loop(0, length // 16, settle, 0)
+    last = slice(2 * length, 2 * length + 16)
+    value = zbuf[z, last, 0:length].astype(f32)
+    for d in range(3):
+        value = value + zrecv[d, last, 0:length].astype(f32)
+    dg_ref[...] = value
+    for d in range(1, NZ):
+        zcopy(d).wait_send()
+        gcopy(d).wait()
+    gown.wait()
+    spread_t.drain()
+    spread_b.drain()
+
+
+def expert_stage(moe_input, table, gall, wgu, wdn):
+    length, width = moe_input.shape
+    dma = pltpu.SemaphoreType.DMA
+    hbm = pl.BlockSpec(memory_space=pl.ANY)
+    vmem = pl.BlockSpec(memory_space=pltpu.VMEM)
+    f32, bf16 = jnp.float32, jnp.bfloat16
+    shape = jax.ShapeDtypeStruct
+    inner = 2 * WIDE
+    group = NZ * length
+    rows = width // NZ
+    return pl.pallas_call(
+        expert_kernel,
+        name="experts",
+        out_shape=[
+            shape((length, width), f32),
+            shape((length, width), f32),
+            shape((16, length), f32),
+            shape((NZ, 2, rows, inner), bf16),
+            shape((2, WIDE, width), f32),
+            shape((width, inner), f32),
+            shape((WIDE, width), f32),
+            shape((8, NZ, length, width), bf16),
+            shape((8, NZ, 16, 2 * length), f32),
+            shape((4, 2 * group + 16, width), bf16),
+            shape((3, 2 * group + 16, width), bf16),
+        ],
+        in_specs=[hbm, hbm, hbm, vmem, vmem],
+        out_specs=[vmem, vmem, vmem, hbm, vmem, vmem, vmem, hbm, hbm, hbm, hbm],
+        scratch_shapes=[
+            pltpu.VMEM((2, width, inner), f32),
+            pltpu.VMEM((2, NZ, length, width), bf16),
+            pltpu.VMEM((2, NZ, length, width), bf16),
+            pltpu.VMEM((2, NZ, 16, 2 * length), f32),
+            pltpu.VMEM((NZ, 2 * SLOTS, length), bf16),
+            pltpu.VMEM((2, NZ * SLOTS, width), bf16),
+            pltpu.VMEM((2, NZ * SLOTS, width), bf16),
+            pltpu.VMEM((NZ, 2 * SLOTS, width), bf16),
+            pltpu.VMEM((NZ, 2 * SLOTS, width), bf16),
+            pltpu.VMEM((2, 2 * group + 16, width), bf16),
+            pltpu.VMEM((3, 2 * group + 16, width), bf16),
+            pltpu.VMEM((NZ, 2 * length + 16, width), bf16),
+            pltpu.VMEM((3, 2 * length + 16, width), bf16),
+            pltpu.VMEM((2, width, inner), bf16),
+        ]
+        + spread_sems() + spread_sems()
+        + [
+            dma((2, 3)), dma((4,)), dma((4,)), dma((3,)), dma((3,)), dma((3,)),
+            dma((3,)), dma((3,)), dma, dma((3,)), dma((3,)),
+        ],
+        compiler_params=pltpu.CompilerParams(
+            collective_id=1, has_side_effects=True, vmem_limit_bytes=60 * MIB
+        ),
+    )(moe_input, table, gall, wgu, wdn)
+
+
+def backward_kernel(
+    db_ref, dg_ref, g_ref, x_ref, hidden_ref, b_ref, gates_ref, psum_ref, bound_ref, cos_ref, sin_ref,
+    aall, wall, woall, q1, k1, v1, q2, k2, v2, att1, lse1, att2, lse2, mixed,
+    gtok_ref, small_ref, gwq_ref, gwk_ref, gwv_ref, gwo_ref,
+    dhb, dhall, dm, dk, dv, cat, wst, wrecv, wsum, wfinal, dwo, worecv, wosum, wofinal, small4, *sems,
+):
+    f32, bf16 = jnp.float32, jnp.bfloat16
+    c = lax.axis_index("ctx")
+    z = lax.axis_index("fsdp")
+    length, width = x_ref.shape
+    count = aall.shape[0]
+    shard = width // NZ
+    quarter = c % 4
+    mate = flip(c, 0, 0, 1)
+    scale = HEAD_DIM**-0.5
+    sems = list(sems)
+
+    def take(n):
+        taken = sems[:n]
+        del sems[:n]
+        return taken
+
+    spread_h = Spread(lambda _: dhb, lambda o, _: dhall.at[o], take(7), c, z, 1)
+    spread_w = Spread(lambda _: wsum, lambda o, _: wfinal.at[o], take(7), c, z, 1)
+    wzs, wzr, ozs, ozr, oxs, oxr, oms, omr, ss, sr = take(10)
+    reduce_refs = take(8)
+    greet(c, z)
+    packed = psum_ref[...]
+    gain_one = packed[17:18]
+    gain_two = packed[16:17]
+    router = packed[0:16].astype(bf16)
+    hidden = hidden_ref[...]
+    factor_two = norm_factor(hidden)
+    normed_two = hidden * factor_two
+    gates = gates_ref[...]
+    d_gates = dg_ref[...]
+    d_logits = gates * (d_gates - jnp.sum(gates * d_gates, axis=0, keepdims=True))
+    d_b = db_ref[...] + split_dot(d_logits, router, TN)
+    small_ref[...] = jnp.zeros_like(small_ref)
+    small_ref[0:16] = split_dot(d_logits, b_ref[...])
+    small_ref[16:17] = jnp.sum(d_b * normed_two, axis=0, keepdims=True)
+    pulled = d_b * gain_two
+    d_hidden = g_ref[...].astype(f32) + factor_two * (
+        pulled - normed_two * jnp.mean(pulled * normed_two, axis=1, keepdims=True)
+    )
+    dhb[...] = d_hidden.astype(bf16)
+    spread_h.start_z()
+    spread_h.start_x()
+    dk[...] = jnp.zeros_like(dk)
+    dv[...] = jnp.zeros_like(dv)
+    cat[:, 384:512] = jnp.zeros((count, 128), bf16)
+    spread_h.relay_x()
+    spread_h.arrive()
+    step = 2 * length
+    for i in range(count // step):
+        block = dhall[2 * i : 2 * i + 2].reshape(step, width)
+        dm[i * step : (i + 1) * step] = dot(block, woall[...], NT).astype(bf16)
+        part = dot(mixed[i * step : (i + 1) * step], block, TN)
+        if i == 0:
+            dwo[...] = part
+        else:
+            dwo[...] += part
+    wosum[...] = dwo[...].astype(bf16).reshape(wosum.shape)
+
+    def oz(j, owner):
+        d = (owner + NZ - z) % NZ
+        return remote(wosum.at[j], worecv.at[j, d - 1], ozs.at[j], ozr.at[j, d - 1], c, owner)
+
+    def oz_wait(j, d):
+        return remote(wosum.at[j], worecv.at[j, d], ozs.at[j], ozr.at[j, d], c, z)
+
+    for j, (_, owner) in enumerate(head_rows(c)):
+
+        @pl.when(owner != z)
+        def _(j=j, owner=owner):
+            oz(j, owner).start()
+
+    boundary = bound_ref[0:1, 0:1]
+
+    def pull_back(queries, first, keys, values, n, upper, out, lse, which):
+        scores = dot(queries, keys[0:n], NT) * scale
+        scores = jnp.where(visible(first, step, n, boundary), scores, negative)
+        shares = jnp.exp(scores - lse[:, 0:1])
+        delta = jnp.sum(upper.astype(f32) * out, axis=1, keepdims=True)
+        pulled = (scale * (shares * (dot(upper, values[0:n], NT) - delta))).astype(bf16)
+        dk[which, 0:n] += dot(pulled, queries, TN)
+        dv[which, 0:n] += dot(shares.astype(bf16), upper, TN)
+        return dot(pulled, keys[0:n]).astype(bf16).astype(f32)
+
+    for i in range(count // step):
+        part = slice(i * step, (i + 1) * step)
+        got = pull_back(q1[part], i * step, k1, v1, (i + 1) * step, dm[part, 0:128], att1[part], lse1[part], 0)
+        cat[part, 0:128] = turned(got, cos_ref[part], -sin_ref[part]).astype(bf16)
+    mine = rows_at(quarter * step, step)
+    got = pull_back(q2[mine], quarter * step, k2, v2, count, dm[mine, 128:256], att2[...], lse2[...], 1)
+    cat[mine, 384:512] = turned(got, cos_ref[mine], -sin_ref[mine]).astype(bf16)
+    for which in range(2):
+        at = 384 * which
+        keys = dk[which].astype(bf16).astype(f32)
+        cat[:, at + 128 : at + 256] = turned(keys, cos_ref[...], -sin_ref[...]).astype(bf16)
+        cat[:, at + 256 : at + 384] = dv[which].astype(bf16)
+    for i in range(width // 256):
+        wst[256 * i : 256 * i + 256] = dot(aall[:, 256 * i : 256 * i + 256], cat[...], TN).astype(bf16)
+
+    def wz(d):
+        there = (z + d) % NZ
+        return remote(
+            wst.at[rows_at(there * shard, shard)], wrecv.at[d - 1], wzs.at[d - 1], wzr.at[d - 1], c, there
+        )
+
+    for d in range(1, NZ):
+        wz(d).start()
+
+    def ox(j, i):
+        there = flip(c, PEERS[i][0], PEERS[i][1], 0)
+        return remote(wosum.at[j], wofinal.at[c, j], oxs.at[j, i], oxr.at[j, i], there, z)
+
+    def om(j, i):
+        fy, fx = (((0, 0),) + PEERS)[i]
+        origin = flip(c, fy, fx, 0)
+        src = wosum.at[j] if i == 0 else wofinal.at[origin, j]
+        return remote(src, wofinal.at[origin, j], oms.at[j, i], omr.at[j, i], mate, z)
+
+    for j, (_, owner) in enumerate(head_rows(c)):
+
+        @pl.when(owner == z)
+        def _(j=j):
+            for d in range(3):
+                oz_wait(j, d).wait_recv()
+            total = wosum[j].astype(f32)
+            for d in range(3):
+                total = total + worecv[j, d].astype(f32)
+            wosum[j] = total.astype(bf16)
+            wofinal[c, j] = total.astype(bf16)
+            for i in range(3):
+                ox(j, i).start()
+            om(j, 0).start()
+
+    value = plane_reduce(
+        lambda o: dot(cat[rows_at(o * length, length)], wall[...], NT), c, z, reduce_refs
+    )
+    x = x_ref[...].astype(f32)
+    factor_one = norm_factor(x)
+    normed_one = x * factor_one
+    small_ref[17:18] = jnp.sum(value * normed_one, axis=0, keepdims=True)
+    pulled = value * gain_one
+    gtok_ref[...] = (
+        d_hidden
+        + factor_one * (pulled - normed_one * jnp.mean(pulled * normed_one, axis=1, keepdims=True))
+    ).astype(bf16)
+
+    total = wst[rows_at(z * shard, shard)].astype(f32)
+    for d in range(1, NZ):
+        wz(d).wait_recv()
+        total = total + wrecv[d - 1].astype(f32)
+    wsum[...] = total.astype(bf16)
+    spread_w.start_z()
+    spread_w.start_x()
+
+    def exchange(stage, slots, targets):
+        copies = [
+            remote(small4.at[stage], small4.at[slot], ss.at[slot], sr.at[slot], tc, tz)
+            for slot, (tc, tz) in zip(slots, targets)
+        ]
+        for copy in copies:
+            copy.start()
+        for copy in copies:
+            copy.wait_recv()
+        value = small4[stage]
+        for slot in slots:
+            value = value + small4[slot]
+        return value, copies
+
+    small4[0] = small_ref[...]
+    value, sent = exchange(0, (1,), ((mate, z),))
+    small4[2] = value
+    value, more = exchange(2, (3, 4, 5), [(flip(c, fy, fx, 0), z) for fy, fx in PEERS])
+    sent += more
+    small4[6] = value
+    value, more = exchange(6, (7, 8, 9), [(c, (z + d) % NZ) for d in range(1, NZ)])
+    sent += more
+    small_ref[...] = value
+    for i in range(3):
+        for j, (_, owner) in enumerate(head_rows(flip(c, PEERS[i][0], PEERS[i][1], 0))):
+
+            @pl.when(owner == z)
+            def _(j=j, i=i):
+                origin = flip(c, PEERS[i][0], PEERS[i][1], 0)
+                block = wofinal.at[origin, j]
+                remote(block, block, oxs.at[j, i], oxr.at[j, i], c, z).wait_recv()
+                om(j, i + 1).start()
+
+    spread_w.relay_x()
+    for i in range(4):
+        fy, fx = (((0, 0),) + PEERS)[i]
+        for j, (_, owner) in enumerate(head_rows(flip(c, fy, fx, 1))):
+
+            @pl.when(owner == z)
+            def _(j=j, i=i, fy=fy, fx=fx):
+                block = wofinal.at[flip(c, fy, fx, 1), j]
+                remote(block, block, oms.at[j, i], omr.at[j, i], c, z).wait_recv()
+
+    for i in range(5):
+        b = 5 * z + i
+
+        @pl.when(b < 16)
+        def _(b=b, i=i):
+            low = jnp.minimum(b, 15)
+            gwo_ref[64 * i : 64 * i + 64] = wofinal[low // 2, low % 2].astype(f32)
+
+        @pl.when(b >= 16)
+        def _(b=b, i=i):
+            high = jnp.maximum(b, 16) - 16
+            gwo_ref[64 * i : 64 * i + 64] = sum(
+                wofinal[4 * (high // 2) + k, 2 + high % 2].astype(f32) for k in range(4)
+            )
+
+    spread_w.arrive()
+    for n, ref in enumerate((gwq_ref, gwk_ref, gwv_ref)):
+        for o in range(8):
+            ref[:, 128 * o : 128 * o + 128] = wfinal[o, :, 128 * n : 128 * n + 128].astype(f32)
+        for y in range(2):
+            lanes = slice(384 + 128 * n, 512 + 128 * n)
+            ref[:, 1024 + 128 * y : 1152 + 128 * y] = sum(
+                wfinal[4 * y + k, :, lanes].astype(f32) for k in range(4)
+            )
+    for copy in sent:
+        copy.wait_send()
+    for j, (_, owner) in enumerate(head_rows(c)):
+
+        @pl.when(owner != z)
+        def _(j=j, owner=owner):
+            oz(j, owner).wait_send()
+
+        @pl.when(owner == z)
+        def _(j=j):
+            for i in range(3):
+                ox(j, i).wait_send()
+            om(j, 0).wait_send()
+
+    for i in range(3):
+        for j, (_, owner) in enumerate(head_rows(flip(c, PEERS[i][0], PEERS[i][1], 0))):
+
+            @pl.when(owner == z)
+            def _(j=j, i=i):
+                om(j, i + 1).wait_send()
+
+    for d in range(1, NZ):
+        wz(d).wait_send()
+    spread_h.drain()
+    spread_w.drain()
+
+
+def backward_stage(*operands):
+    x, aall = operands[3], operands[11]
+    length, width = x.shape
+    count = aall.shape[0]
+    shard = width // NZ
+    dma = pltpu.SemaphoreType.DMA
+    vmem = pl.BlockSpec(memory_space=pltpu.VMEM)
+    f32, bf16 = jnp.float32, jnp.bfloat16
+    shape = jax.ShapeDtypeStruct
+    return pl.pallas_call(
+        backward_kernel,
+        name="backward",
+        out_shape=[
+            shape((length, width), bf16), shape((32, width), f32), shape((shard, width), f32),
+            shape((shard, width), f32), shape((shard, width), f32), shape((shard, width), f32),
+        ],
+        in_specs=[vmem] * len(operands),
+        out_specs=[vmem] * 6,
+        scratch_shapes=[
+            pltpu.VMEM((length, width), bf16), pltpu.VMEM((8, length, width), bf16), pltpu.VMEM((count, 256), bf16),
+            pltpu.VMEM((2, count, 128), f32), pltpu.VMEM((2, count, 128), f32), pltpu.VMEM((count, 768), bf16),
+            pltpu.VMEM((width, 768), bf16), pltpu.VMEM((3, shard, 768), bf16), pltpu.VMEM((shard, 768), bf16),
+            pltpu.VMEM((8, shard, 768), bf16), pltpu.VMEM((256, width), f32), pltpu.VMEM((4, 3, 64, width), bf16),
+            pltpu.VMEM((4, 64, width), bf16), pltpu.VMEM((8, 4, 64, width), bf16), pltpu.VMEM((10, 32, width), f32),
+        ]
+        + spread_sems(1) + spread_sems(1)
+        + [
+            dma((3,)), dma((3,)), dma((4,)), dma((4, 3)), dma((4, 3)), dma((4, 3)), dma((4, 4)), dma((4, 4)),
+            dma((10,)), dma((10,)),
+        ]
+        + plane_scratch(length, width),
+        compiler_params=pltpu.CompilerParams(
+            collective_id=3, has_side_effects=True, vmem_limit_bytes=60 * MIB
+        ),
+    )(*operands)
+
+
+def per_device_fast(
+    tokens,
+    documents,
+    routes,
+    priority,
+    attention_gain,
+    query_weight,
+    key_weight,
+    value_weight,
+    output_weight,
+    feedforward_gain,
+    router_weight,
+    shared_gate,
+    shared_up,
+    shared_down,
+    expert_gate,
+    expert_up,
+    expert_down,
+    cotangent,
+):
+    f32, bf16 = jnp.float32, jnp.bfloat16
+    z = lax.axis_index("fsdp")
+    length = tokens.shape[1]
+    row_length = length * 8
+    experts = EXP_DEV * 8
+    capacity = 9 * length * TOPK // (8 * experts)
+    shard = query_weight.shape[0]
+    hidden_dev = expert_gate.shape[2] // NZ
+    cosine, sine = rotary_tables(jnp.arange(row_length, dtype=jnp.int32), HEAD_DIM // 2)
+    cosine, sine = cosine[:, 0], sine[:, 0]
+    cosine_wide = jnp.concatenate([cosine, cosine], axis=1)
+    sine_wide = jnp.concatenate([-sine, sine], axis=1)
+    small = jnp.concatenate(
+        [router_weight.T, feedforward_gain[None], attention_gain[None], jnp.zeros((14, shard), bf16)], axis=0
+    )
+    packed = lax.dynamic_update_slice(jnp.zeros((32, NZ * shard), bf16), small, (0, z * shard))
+    docs = jnp.concatenate([documents.astype(f32), jnp.ones((7, length), f32)], axis=0)
+
+    def slices(weights):
+        parts = weights.reshape(weights.shape[0], weights.shape[1], NZ, hidden_dev)
+        parts = jnp.pad(parts, ((0, 0), (0, 0), (0, 0), (0, WIDE - hidden_dev)))
+        return jnp.transpose(parts, (2, 0, 1, 3))
+
+    wsend = jnp.concatenate(
+        [
+            jnp.concatenate([slices(expert_gate), slices(shared_gate[None])], axis=1),
+            jnp.concatenate([slices(expert_up), slices(shared_up[None])], axis=1),
+        ],
+        axis=3,
+    )
+    wdn = jnp.pad(
+        jnp.concatenate([expert_down, shared_down[None]], axis=0), ((0, 0), (0, WIDE - hidden_dev), (0, 0))
+    )
+    front = attention_stage(
+        capacity, tokens[0], packed, docs, routes[0], priority[0], cosine_wide, sine_wide, cotangent[0],
+        query_weight, key_weight, value_weight, output_weight, wsend,
+    )
+    hidden, moe_input, table, gates, packed_sum, bound = front[:6]
+    kept = front[6:20]
+    (routed, grad_moe, grad_table, gu_back, grad_down, shared_gu, shared_dn) = expert_stage(
+        moe_input, table, front[20], front[21], wdn
+    )[:7]
+    output_rows = (hidden + routed).astype(bf16)
+
+    def joined(parts, at):
+        return jnp.concatenate([parts[i][..., at : at + hidden_dev] for i in range(NZ)], axis=-1).astype(f32)
+
+    shared_sum = lax.psum(shared_gu.astype(bf16), "ctx")
+    shared_down_sum = lax.psum(shared_dn[:hidden_dev].astype(bf16), "ctx")
+    grad_tokens, small, grad_wq, grad_wk, grad_wv, grad_wo = backward_stage(
+        grad_moe, grad_table, cotangent[0], tokens[0], hidden, moe_input, gates, packed_sum, bound, cosine_wide,
+        sine_wide, *kept
+    )
+    shared_back = lax.all_to_all(
+        shared_sum.reshape(NZ, shard, 2 * WIDE), "fsdp", split_axis=0, concat_axis=0, tiled=True
+    )
+    mine = lax.dynamic_slice_in_dim(small, z * shard, shard, 1)
+    return (
+        output_rows[None],
+        grad_tokens[None],
+        mine[17],
+        grad_wq,
+        grad_wk,
+        grad_wv,
+        grad_wo,
+        mine[16],
+        mine[:16].T,
+        joined(shared_back, 0),
+        joined(shared_back, WIDE),
+        shared_down_sum.astype(f32),
+        joined(gu_back, 0),
+        joined(gu_back, WIDE),
+        grad_down[:, :hidden_dev],
+    )
 
 
 def per_device(
@@ -499,8 +1647,10 @@
 
 
 def solution(mesh):
+    fast = mesh.shape['ctx'] == 8 and mesh.shape['fsdp'] == NZ
+    body = per_device_fast if fast else per_device
     return jax.shard_map(
-        per_device,
+        body,
         mesh=mesh,
         in_specs=(
             P("fsdp", "ctx", None),

time: 1770 us -> 901 us (0.51)
  waiting for transfers between devices: 1270 us -> 60.4 us
  Pallas kernels: 0 us -> 751 us
  local copies, waits for them, and re-layouts: 186 us -> 43.9 us
  matrix products: 139 us -> 0 us
  blocking collectives: 55.8 us -> 0 us
  other arithmetic: 62.8 us -> 20 us
  starting transfers between devices: 24 us -> 4.8 us
    pallas_call x0 -> x3, Pallas kernels: none -> 751 us  [the longest x1 442 us: expert_stage(): pl.pallas_call(expert_kernel, name='experts', out_shape=[shape((length, w...]
    reduce_scatter x10 -> x0, waiting for transfers between devices: 623 us -> none  [the longest x1 86.4 us: per_device(): lax.psum_scatter(grad_expert_gate.astype(jnp.bfloat16), 'fsdp', scatter_d...]
    all_gather x12 -> x0, waiting for transfers between devices: 512 us -> none  [the longest x1 79.7 us: per_device(): lax.all_gather(expert_down, 'fsdp', axis=1, tiled=True)]
    dot_general x48 -> x0, matrix products: 139 us -> none  [the longest x1 9.59 us: per_device(): jnp.einsum('erd,efd->erf', grad_arrived, w_expert_down, preferred_element...]
    unnamed x27 -> x1, waiting for transfers between devices: 69.3 us -> 0.02 us
    dynamic_update_slice x2 -> x1, local copies, waits for them, and re-layouts: 49.9 us -> 0.37 us  [per_device_fast(): lax.dynamic_update_slice(jnp.zeros((32, NZ * shard), bf16), small, (0, z...]
    reshape x9 -> x4, local copies, waits for them, and re-layouts: 35.9 us -> 9.51 us  [slices(): parts = weights.reshape(weights.shape[0], weights.shape[1], NZ, hidden_dev)]
    psum x1 -> x0, blocking collectives: 22.1 us -> none  [per_device(): lax.psum(own_gain_one.astype(jnp.bfloat16), 'ctx').astype(jnp.float32)]
  transfers between devices with their start and end apart: 29 -> 2, of which waited for: 25 -> 1; matrix products, arithmetic and copies ran while one was open for 14% -> 2% of each run, Pallas kernels for 0% -> 17%
where the time goes in v2:
time: 901 us; the launch traced here: 895 us
  Pallas kernels  751 us (83%)
  waiting for transfers between devices  60.4 us (7%)
  local copies, waits for them, and re-layouts  43.9 us (5%)
  other arithmetic  20 us (2%)
  between operations  14.6 us (2%)
    pallas_call x1, Pallas kernels, expert_stage(): pl.pallas_call(expert_kernel, name='experts', out_shape=[shape((length, w...  442 us
    pallas_call x1, Pallas kernels, attention_stage(): pl.pallas_call(functools.partial(attention_kernel, capacity), name='atten...  156 us
    pallas_call x1, Pallas kernels, backward_stage(): pl.pallas_call(backward_kernel, name='backward', out_shape=[shape((length...  153 us
    psum x1, waiting for transfers between devices, per_device_fast(): shared_sum = lax.psum(shared_gu.astype(bf16), 'ctx')  60.4 us
  transfers between devices with their start and end apart: 2, of which 1 were waited for; matrix products, arithmetic and copies ran while one was open for 2% of the time, Pallas kernels for 17%

profile of v2, /device:TPU:21, one launch (start us, length us, event | category | flops | bytes accessed | tf_op | source)
XLA Modules:
  0.0 894.6 jit_solution(7279388438857341680)
XLA Ops:
  8.6 3.6 reshape.49
  12.4 4.2 reshape.50
  16.6 1.5 copy.37
  18.2 1.4 reshape_broadcast_in_dim.6
  19.6 1.2 copy.36
  20.8 3.0 reshape_broadcast_in_dim.7
  23.7 2.0 copy.38
  26.5 3.1 fusion.4
  29.7 2.0 pad_bitcast_fusion
  31.7 1.3 pad_bitcast_fusion.2
  33.6 1.4 fusion.2.wdn_ref
  35.6 1.3 pad_maximum_fusion
  37.4 3.0 maximum_maximum_fusion.wsend_ref
  40.5 155.6 %attention.1 = (f32[128,1280]{1,0:T(8,128)}, bf16[128,1280]{1,0:T(8,128)(2,1)}, f32[16,256]{1,0:T(8,128)}, f32[16,128]{1,0:T(8,128)}, f32[32,1280]{1,0:T(8,128)}...) custom-call(bf16[128,1280]{1,0:T(8,128)(2,1)} %bitcast.37, ...), custom_call_target="tpu_custom_call" | custom-call | tf_op jit(solution)/shard_map/attention/pallas_call | solution.py:506
  196.0 442.1 %experts.1 = (f32[128,1280]{1,0:T(8,128)}, f32[128,1280]{1,0:T(8,128)}, f32[16,128]{1,0:T(8,128)}, bf16[4,2,320,512]{3,2,1,0:T(8,128)(2,1)}, f32[2,256,1280]{2,1...) custom-call(bf16[128,1280]{1,0:T(8,128)(2,1)} %get-tuple-element.51., ...), custom_call_target="tpu_custom_call" | custom-call | tf_op jit(solution)/shard_map/experts/pallas_call | solution.py:789
  638.2 3.0 convert_element_type.49
  641.2 2.1 slice.155
  643.3 60.4 %all-reduce.9.cloned.1.call-done = (bf16[4,320,512]{2,1,0:T(8,128)(2,1)}, bf16[224,1280]{1,0:T(8,128)(2,1)}) async-done(((bf16[4,320,512]{2,1,0:T(8,128)(2,1)}, bf16[224,1280]{1,0:T(8,128)(2,1)}), (bf16[4,320,512]{2,1,0:T(8,128)(2,1)}, bf16[224,1280]{1,0:T(8,128)(2,1)})) %all-reduce.9.cloned.1.call-update) | async-done | bytes 1884176 | tf_op jit(solution)/shard_map/psum | solution.py:1191
  703.7 4.8 all-to-all-start
  708.4 2.8 slice_bitcast_fusion.3
  711.2 153.2 %backward.1 = (bf16[128,1280]{1,0:T(8,128)(2,1)}, f32[32,1280]{1,0:T(8,128)}, f32[320,1280]{1,0:T(8,128)}, f32[320,1280]{1,0:T(8,128)}, f32[320,1280]{1,0:T(8,128)}, /*index=5*/f32[320,1280]{1,0:T(8,128)}) custom-call(f32[128,1280]{1,0:T(8,128)} %get-tuple-element.56.db_ref, f32[16,128]{1,0:T(8,128)} %get-tuple-element.57.dg_ref, ...), custom_call_target="tpu_custom_call" | custom-call | tf_op jit(solution)/shard_map/backward/pallas_call | solution.py:1096
  864.5 3.2 slice.124
  867.7 1.5 dynamic-slice_reduce_fusion
  869.2 1.4 dynamic-slice_bitcast_fusion
  870.8 1.8 maximum_convert_fusion.1
  872.7 1.8 maximum_convert_fusion
  877.0 1.3 maximum_convert_fusion.3
  878.2 1.3 maximum_convert_fusion.2
  880.2 1.2 copy.48
  882.3 1.2 copy.49
  884.3 1.2 copy.50
  886.3 1.2 copy.51
  (74 shorter events, 10.1 us)
Async XLA Ops:
  7.2 696.5 %all-reduce.9.cloned.1.call-start = ((), (), s32[]{:S(2)}) async-start(), calls=%async_computation.1 | async-start | bytes 3768320 | tf_op jit(solution)/shard_map/psum | solution.py:1191
  16.6 1.6 copy-start.16
  19.6 6.2 copy-start.21
  19.6 6.9 copy-start.22
  29.7 2.0 copy-start.4
  31.7 1.9 copy-start.13
  31.7 1.9 copy-start.15
  33.6 1.5 copy-start.6
  33.6 1.5 copy-start.7
  33.6 2.1 copy-start.8
  33.6 3.4 copy-start.20
  33.6 3.8 copy-start.5
  35.0 2.4 copy-start
  35.0 2.4 copy-start.1
  37.4 3.1 copy-start.18
  703.7 173.1 %all-to-all-start = ((bf16[4,320,512]{2,1,0:T(8,128)(2,1)}), bf16[4,320,512]{2,1,0:T(8,128)(2,1)S(1)}, u32[]{:S(2)}, u32[]{:S(2)}) async-start(bf16[4,320,512]{2,1,0:T(8,128)(2,1)} %get-tuple-element.87), calls=%async_computation | async-start | bytes 2621440 | tf_op jit(solution)/shard_map/all_to_all | solution.py:1197
  864.4 6.2 copy-start.3
  872.7 1.9 copy-start.2
  872.7 1.9 copy-start.14
  874.5 1.2 copy-start.17
  877.0 2.5 copy-start.19
  878.2 2.0 copy-start.12
  880.2 2.0 copy-start.11
  882.3 2.0 copy-start.10
  884.3 2.0 copy-start.9
Sparse Core Ops, SparseCore 0:
  643.4 60.2 all-reduce.8

commit v3 on v2

--- a/solution.py
+++ b/solution.py
@@ -1,8 +1,10 @@
 import functools
 import math
+import types
 
 import jax
 import jax.numpy as jnp
+import numpy as np
 from jax import lax
 from jax.experimental import pallas as pl
 from jax.experimental.pallas import tpu as pltpu
@@ -125,6 +127,8 @@
         self.src, self.block, self.c, self.z = src, block, c, z
         self.hops, self.peers, self.all = hops, peers, ((0, 0),) + peers
         self.local, self.zs, self.zr, self.xs, self.xr, self.ms, self.mr = sems
+        self.forwards = hops == NZ and len(peers) == 3
+        self.direct = 2 if self.forwards else len(peers)
         self.own = pltpu.make_async_copy(src(z), block(c, z), self.local) if copy_own else None
 
     def at(self, c, d):
@@ -147,6 +151,12 @@
         there = flip(self.c, self.peers[i][0], self.peers[i][1], 0)
         return remote(self.mine(self.c, d), self.at(self.c, d), self.xs.at[i, d], self.xr.at[i, d], there, self.z)
 
+    def fcopy(self, i, d):
+        origin = flip(self.c, self.peers[i][0], self.peers[i][1], 0)
+        there = flip(self.c, self.peers[1 - i][0], self.peers[1 - i][1], 0)
+        block = self.at(origin, d)
+        return remote(block, block, self.xs.at[2, d], self.xr.at[2, d], there, self.z)
+
     def xwait(self, i, d):
         block = self.at(flip(self.c, self.peers[i][0], self.peers[i][1], 0), d)
         remote(block, block, self.xs.at[i, d], self.xr.at[i, d], self.c, self.z).wait_recv()
@@ -167,22 +177,37 @@
             self.zcopy(d).start()
 
     def start_x(self):
-        for i in range(len(self.peers)):
+        for i in range(self.direct):
             self.xcopy(i, 0).start()
         self.mcopy(0, 0).start()
 
     def relay_z(self):
         for d in range(1, self.hops):
             self.zwait(d)
-            for i in range(len(self.peers)):
+            for i in range(self.direct):
                 self.xcopy(i, d).start()
             self.mcopy(0, d).start()
 
     def relay_x(self):
         for d in range(self.hops):
-            for i in range(len(self.peers)):
-                self.xwait(i, d)
-                self.mcopy(i + 1, d).start()
+            self.relay_near(d)
+        self.relay_far()
+
+    def relay_near(self, d):
+        for i in range(min(2, len(self.peers))):
+            self.xwait(i, d)
+            self.mcopy(i + 1, d).start()
+            if self.forwards and i == (d >= 2):
+                self.fcopy(i, d).start()
+
+    def relay_far(self):
+        for d in range(self.hops if len(self.peers) > 2 else 0):
+            self.xwait(2, d)
+            self.mcopy(3, d).start()
+
+    def arrive_from(self, i):
+        for d in range(self.hops):
+            self.mwait(i, d)
 
     def arrive(self):
         if self.own is not None:
@@ -195,8 +220,10 @@
         for d in range(1, self.hops):
             self.zcopy(d).wait_send()
         for d in range(self.hops):
-            for i in range(len(self.peers)):
+            for i in range(self.direct):
                 self.xcopy(i, d).wait_send()
+            if self.forwards:
+                self.fcopy(int(d >= 2), d).wait_send()
             for i in range(len(self.all)):
                 self.mcopy(i, d).wait_send()
 
@@ -258,6 +285,12 @@
     return values * cosine + pltpu.roll(values, 64, 1) * sine
 
 
+def take(refs, count):
+    taken = refs[:count]
+    del refs[:count]
+    return taken
+
+
 def head_rows(c):
     blocks = [2 * c, 2 * c + 1, 16 + 2 * (c // 4), 17 + 2 * (c // 4)]
     return [(b, b // 5) for b in blocks]
@@ -271,161 +304,257 @@
     return (key <= query) & (key_doc == query_doc)
 
 
-def attention_kernel(
-    capacity,
-    x_ref, p_ref, docs_ref, routes_ref, prio_ref, cos_ref, sin_ref, g_ref, wq_ref, wk_ref, wv_ref, wo_ref, wsend_ref,
-    hidden_ref, b_ref, table_ref, gates_ref, psum_ref, bound_ref, aall, wall, woall, q1, k1, v1, q2, k2, v2,
-    att1, lse1, att2, lse2, mixed, gall, wgu,
-    xall, docs, pall, *sems,
-):
+FRONT_IN = (
+    "x", "router", "gains", "doc", "routes", "prio", "cos", "sin", "g", "wq", "wk", "wv", "wo", "eg", "eu", "sg", "su",
+    "ed", "sd",
+)
+FRONT_OUT = (
+    "hidden", "tokens", "gates", "psum", "bound", "aall", "wall", "woall", "q1", "k1", "v1", "q2", "k2", "v2",
+    "att1", "lse1", "att2", "lse2", "mixed", "db", "dg", "ddn", "dsgu", "dsdn",
+    "gall", "wsend", "ball", "tall", "ypart", "accout",
+)
+FRONT_TMP = (
+    "pool", "docs", "pown", "pall", "cut", "wgu", "wdn", "table", "acc", "bg", "gg", "tg", "oh", "ys", "ds",
+    "st", "stc", "sty", "ld", "xrecv", "zbuf", "zrecv",
+)
+
+
+def front_kernel(capacity, *refs):
     f32, bf16 = jnp.float32, jnp.bfloat16
+    names = FRONT_IN + FRONT_OUT + FRONT_TMP
+    r = types.SimpleNamespace(**dict(zip(names, refs)))
+    sems = list(refs[len(names) :])
     c = lax.axis_index("ctx")
     z = lax.axis_index("fsdp")
-    length, width = x_ref.shape
-    count = aall.shape[0]
+    length, width = r.x.shape
+    count = r.cos.shape[0]
     shard = width // NZ
     sub = shard // 4
     quarter = c % 4
-    sems = list(sems)
-
-    def take(n):
-        taken = sems[:n]
-        del sems[:n]
-        return taken
-
-    spread_x = Spread(lambda _: x_ref, lambda o, _: xall.at[o], take(7), c, z, 1)
-    spread_docs = Spread(lambda _: docs_ref, lambda o, _: docs.at[o], take(7), c, z, 1)
-    second = lambda o, s: wall.at[rows_at(s * shard + (o % 4) * sub, sub), 384:768]
-    spread_h2 = Spread(lambda _: second(c, z), second, take(7), c, z, NZ, ((0, 1),), False)
-    spread_g = Spread(lambda _: g_ref, lambda o, s: gall.at[o, s], take(7), c, z)
-    shared_in = lambda s: wsend_ref.at[s, 2, rows_at((c // 2) * sub, sub), lanes_at(c % 2 * WIDE, WIDE)]
-    shared_to = lambda o, s: wgu.at[2, rows_at(s * shard + (o // 2) * sub, sub), lanes_at(o % 2 * WIDE, WIDE)]
-    spread_s = Spread(shared_in, shared_to, take(7), c, z)
-    ps, pr, wl, w1s, w1r, wol, wos, wor, wgl, wgs, wgr = take(11)
-    reduce_refs = take(8)
+    mate = flip(c, 0, 0, 1)
+    step = 2 * length
+    group = NZ * length
+    final = group + 16
+    hidden_dev = r.ed.shape[1]
+
+    spread_x = Spread(
+        lambda _: r.x, lambda o, _: r.pool.at[rows_at(o * length, length)], take(sems, 7), c, z, 1
+    )
+    spread_docs = Spread(lambda _: r.docs.at[8], lambda o, _: r.docs.at[o], take(sems, 7), c, z, 1)
+    second = lambda o, s: r.wall.at[rows_at(s * shard + (o % 4) * sub, sub), 384:768]
+    spread_h2 = Spread(lambda _: second(c, z), second, take(sems, 7), c, z, NZ, ((0, 1),), False)
+    spread_g = Spread(lambda _: r.g, lambda o, s: r.gall.at[o, rows_at(s * length, length)], take(sems, 7), c, z)
+    shared_in = lambda s: r.wsend.at[s, 2, rows_at((c // 2) * sub, sub), lanes_at(c % 2 * WIDE, WIDE)]
+    shared_to = lambda o, s: r.wgu.at[2, rows_at(s * shard + (o // 2) * sub, sub), lanes_at(o % 2 * WIDE, WIDE)]
+    spread_s = Spread(shared_in, shared_to, take(sems, 7), c, z)
+    spread_b = Spread(lambda _: r.tokens, lambda o, s: r.ball.at[o, rows_at(s * length, length)], take(sems, 7), c, z)
+    spread_t = Spread(lambda _: r.table, lambda o, s: r.tall.at[o, s], take(sems, 7), c, z)
+    ps, pr, wl, w1s, w1r, wol, wos, wor, wgl, wgs, wgr, rawsem, cutsem, dnsem, acsem = take(sems, 15)
+    lsem, ms, mr, xs_s, xs_r, zs, zr, ysem, accsem = take(sems, 9)
+    reduce_refs = [r.ys, r.ds, r.zbuf.at[0:3, 0:length]] + take(sems, 5)
+
     greet(c, z)
-    spread_x.start_z()
-    spread_x.start_x()
-    spread_docs.start_z()
-    spread_docs.start_x()
-
-    def pcopy(d):
-        return remote(p_ref, pall.at[d - 1], ps.at[d - 1], pr.at[d - 1], c, (z + d) % NZ)
-
-    for d in range(1, NZ):
-        pcopy(d).start()
     own_rows = rows_at(z * shard, shard)
     sub_rows = rows_at(z * shard + quarter * sub, sub)
     copies = []
-    for i, ref in enumerate((wq_ref, wk_ref, wv_ref)):
+    for i, ref in enumerate((r.wq, r.wk, r.wv)):
         copies.append(
             pltpu.make_async_copy(
-                ref.at[:, lanes_at(c * 128, 128)], wall.at[own_rows, i * 128 : (i + 1) * 128], wl.at[i]
+                ref.at[:, lanes_at(c * 128, 128)], r.wall.at[own_rows, i * 128 : (i + 1) * 128], wl.at[i]
             )
         )
         copies.append(
             pltpu.make_async_copy(
                 ref.at[rows_at(quarter * sub, sub), lanes_at((8 + c // 4) * 128, 128)],
-                wall.at[sub_rows, 384 + i * 128 : 512 + i * 128],
+                r.wall.at[sub_rows, 384 + i * 128 : 512 + i * 128],
                 wl.at[3 + i],
             )
         )
     for copy in copies:
         copy.start()
+    spread_x.start_z()
+    spread_x.start_x()
+    down = [pltpu.make_async_copy(r.ed.at[e], r.wdn.at[e, 0:hidden_dev], dnsem.at[e]) for e in range(2)]
+    down.append(pltpu.make_async_copy(r.sd, r.wdn.at[2, 0:hidden_dev], dnsem.at[2]))
+    for copy in down:
+        copy.start()
+    raws = ((r.eg.at[0], r.eu.at[0]), (r.eg.at[1], r.eu.at[1]), (r.sg, r.su))
+
+    units = r.eg.shape[2]
+    raw = lambda h: r.gg.at[h * shard : (h + 1) * shard, 0:units]
+
+    def load_raw(e):
+        return [pltpu.make_async_copy(raws[e][h], raw(h), rawsem.at[h]) for h in range(2)]
+
+    def store_cut(e):
+        return pltpu.make_async_copy(r.cut, r.wsend.at[:, e], cutsem)
+
+    for copy in load_raw(0):
+        copy.start()
+    row = lax.broadcasted_iota(jnp.int32, (shard, width), 0)
+    lane = lax.broadcasted_iota(jnp.int32, (shard, width), 1)
+    place = jnp.where(lane == row + z * shard, 1.0, 0.0).astype(bf16)
+    r.pown[0:16] = dot(r.router[...], place, TN).astype(bf16)
+    r.pown[16:32] = dot(r.gains[...], place).astype(bf16)
+
+    def pcopy(d):
+        return remote(r.pown, r.pall.at[d - 1], ps.at[d - 1], pr.at[d - 1], c, (z + d) % NZ)
+
+    for d in range(1, NZ):
+        pcopy(d).start()
+    spread_g.start_z()
     for copy in copies:
         copy.wait()
 
     def h1copy(d):
         return remote(
-            wall.at[own_rows, 0:384], wall.at[own_rows, 0:384], w1s.at[d - 1], w1r.at[d - 1], c, (z + d) % NZ
+            r.wall.at[own_rows, 0:384], r.wall.at[own_rows, 0:384], w1s.at[d - 1], w1r.at[d - 1], c, (z + d) % NZ
         )
 
     def h1wait(d):
-        here = wall.at[rows_at((z + NZ - d) % NZ * shard, shard), 0:384]
+        here = r.wall.at[rows_at((z + NZ - d) % NZ * shard, shard), 0:384]
         remote(here, here, w1s.at[d - 1], w1r.at[d - 1], c, z).wait_recv()
 
     spread_h2.start_z()
     for d in range(1, NZ):
         h1copy(d).start()
     spread_h2.start_x()
-
-    def wo_local(j):
-        b, _ = head_rows(c)[j]
-        return pltpu.make_async_copy(wo_ref.at[rows_at(b % 5 * 64, 64)], woall.at[64 * j : 64 * j + 64], wol.at[j])
-
-    def wo_remote(j, d):
-        b, _ = head_rows(c)[j]
-        return remote(
-            wo_ref.at[rows_at(b % 5 * 64, 64)], woall.at[64 * j : 64 * j + 64],
-            wos.at[j, d - 1], wor.at[j], c, (z + d) % NZ,
+    def wo_local(j, b):
+        return pltpu.make_async_copy(
+            r.wo.at[rows_at(b % 5 * 64, 64)], r.woall.at[64 * j : 64 * j + 64], wol.at[j]
         )
 
-    for j, (_, owner) in enumerate(head_rows(c)):
-
+    def wo_hop(j, up, b, owner):
+        src = r.wo.at[rows_at(b % 5 * 64, 64)] if owner else r.woall.at[64 * j : 64 * j + 64]
+        there = z + 1 if up else z - 1
+        return remote(src, r.woall.at[64 * j : 64 * j + 64], wos.at[j, int(up)], wor.at[j], c, there)
+
+    def wo_each(visit):
+        for j, (b, owner) in enumerate(head_rows(c)):
+            visit(j, b, owner)
+
+    def wo_start(j, b, owner):
         @pl.when(owner == z)
-        def _(j=j):
-            wo_local(j).start()
-            for d in range(1, NZ):
-                wo_remote(j, d).start()
-
+        def _():
+            wo_local(j, b).start()
+
+        @pl.when((owner == z) & (z < NZ - 1))
+        def _():
+            wo_hop(j, True, b, True).start()
+
+        @pl.when((owner == z) & (z > 0))
+        def _():
+            wo_hop(j, False, b, True).start()
+
+    def wo_relay(j, b, owner):
+        @pl.when(owner != z)
+        def _():
+            wo_hop(j, True, b, False).wait_recv()
+
+        @pl.when((owner < z) & (z < NZ - 1))
+        def _():
+            wo_hop(j, True, b, False).start()
+
+        @pl.when((owner > z) & (z > 0))
+        def _():
+            wo_hop(j, False, b, False).start()
+
+        @pl.when(owner == z)
+        def _():
+            wo_local(j, b).wait()
+
+    def wo_drain(j, b, owner):
+        @pl.when((owner <= z) & (z < NZ - 1))
+        def _():
+            wo_hop(j, True, b, False).wait_send()
+
+        @pl.when((owner >= z) & (z > 0))
+        def _():
+            wo_hop(j, False, b, False).wait_send()
+
+    wo_each(wo_start)
+    r.docs[8] = jnp.concatenate([r.doc[...].astype(f32), jnp.ones((7, length), f32)], axis=0)
+    spread_docs.start_z()
+    spread_docs.start_x()
     spread_x.relay_x()
     spread_docs.relay_x()
-    packed = p_ref[...].astype(f32)
+    spread_g.start_x()
+
+    for e in range(3):
+        for copy in load_raw(e):
+            copy.wait()
+        if e > 0:
+            store_cut(e - 1).wait()
+        unit = lax.broadcasted_iota(jnp.int32, (units, WIDE), 0)
+        slot = lax.broadcasted_iota(jnp.int32, (units, WIDE), 1)
+        for q in range(NZ):
+            pick = jnp.where((unit == slot + q * hidden_dev) & (slot < hidden_dev), 1.0, 0.0).astype(bf16)
+            for h in range(2):
+                r.cut[q, :, h * WIDE : (h + 1) * WIDE] = dot(raw(h)[...], pick).astype(bf16)
+        store_cut(e).start()
+        if e < 2:
+            for copy in load_raw(e + 1):
+                copy.start()
+    spread_g.relay_z()
+    packed = r.pown[...].astype(f32)
     for d in range(1, NZ):
         pcopy(d).wait_recv()
-        packed = packed + pall[d - 1].astype(f32)
-    psum_ref[...] = packed
+        packed = packed + r.pall[d - 1].astype(f32)
+    r.psum[...] = packed
     gain_one = packed[17:18]
     gain_two = packed[16:17]
     spread_x.arrive()
 
     def make_a(i, carry):
-        values = xall[i].astype(f32)
-        aall[rows_at(i * length, length)] = (values * norm_factor(values) * gain_one).astype(bf16)
+        values = r.pool[rows_at(i * length, length)].astype(f32)
+        r.bg[rows_at(i * length, length)] = (values * norm_factor(values) * gain_one).astype(bf16)
         return carry
 
     lax.fori_loop(0, 8, make_a, 0)
+    for d in range(2):
+        spread_g.relay_near(d)
     spread_h2.relay_z()
     spread_h2.relay_x()
     spread_h2.arrive()
     for d in range(1, NZ):
         h1wait(d)
-
-    def wgcopy(d):
+    wo_each(wo_relay)
+
+    def wgcopy(e, d):
         there = (z + d) % NZ
         return remote(
-            wsend_ref.at[there, 0:2], wgu.at[0:2, own_rows, :], wgs.at[d - 1], wgr.at[d - 1], c, there
+            r.wsend.at[there, e], r.wgu.at[e, own_rows, :], wgs.at[e, d - 1], wgr.at[e, d - 1], c, there
         )
 
-    def wgwait(d):
-        here = wgu.at[0:2, rows_at((z + NZ - d) % NZ * shard, shard), :]
-        remote(here, here, wgs.at[d - 1], wgr.at[d - 1], c, z).wait_recv()
-
-    wgown = pltpu.make_async_copy(wsend_ref.at[z, 0:2], wgu.at[0:2, own_rows, :], wgl)
-    spread_g.start_z()
-    spread_g.start_x()
+    def wgwait(e, d):
+        here = r.wgu.at[e, rows_at((z + NZ - d) % NZ * shard, shard), :]
+        remote(here, here, wgs.at[e, d - 1], wgr.at[e, d - 1], c, z).wait_recv()
+
+    wgown = pltpu.make_async_copy(r.wsend.at[z, 0:2], r.wgu.at[0:2, own_rows, :], wgl)
+    store_cut(2).wait()
     spread_s.start_z()
     spread_s.start_x()
     wgown.start()
     for d in range(1, NZ):
-        wgcopy(d).start()
-    step = 2 * length
+        wgcopy(0, d).start()
     for i in range(count // step):
         part = slice(i * step, (i + 1) * step)
-        values = dot(aall[part], wall[...])
-        cosine, sine = cos_ref[part], sin_ref[part]
-        q1[part] = turned(values[:, 0:128], cosine, sine).astype(bf16)
-        k1[part] = turned(values[:, 128:256], cosine, sine).astype(bf16)
-        v1[part] = values[:, 256:384].astype(bf16)
-        q2[part] = turned(values[:, 384:512], cosine, sine).astype(bf16)
-        k2[part] = turned(values[:, 512:640], cosine, sine).astype(bf16)
-        v2[part] = values[:, 640:768].astype(bf16)
+        values = dot(r.bg[part], r.wall[...])
+        cosine, sine = r.cos[part], r.sin[part]
+        r.q1[part] = turned(values[:, 0:128], cosine, sine).astype(bf16)
+        r.k1[part] = turned(values[:, 128:256], cosine, sine).astype(bf16)
+        r.v1[part] = values[:, 256:384].astype(bf16)
+        r.q2[part] = turned(values[:, 384:512], cosine, sine).astype(bf16)
+        r.k2[part] = turned(values[:, 512:640], cosine, sine).astype(bf16)
+        r.v2[part] = values[:, 640:768].astype(bf16)
+    for d in range(2, NZ):
+        spread_g.relay_near(d)
+    acopy = pltpu.make_async_copy(r.bg, r.aall, acsem)
+    acopy.start()
     spread_docs.arrive()
-    flags = jnp.where(docs[...] == 0.0, 1.0, 0.0)
+    flags = jnp.where(r.docs[0:8] == 0.0, 1.0, 0.0)
     boundary = jnp.sum(jnp.sum(flags, axis=0), axis=(0, 1), keepdims=True)
-    bound_ref[...] = jnp.broadcast_to(boundary, bound_ref.shape)
-    spread_g.relay_z()
-    spread_s.relay_z()
+    r.bound[...] = jnp.broadcast_to(boundary, r.bound.shape)
 
     def attend(queries, first, keys, values, n):
         scores = dot(queries, keys[0:n], NT) * (HEAD_DIM**-0.5)
@@ -436,67 +565,314 @@
         probs = (shares * (1.0 / total)).astype(bf16)
         return dot(probs, values[0:n]), jnp.broadcast_to(top + jnp.log(total), (step, 128))
 
-    mixed[...] = jnp.zeros_like(mixed)
+    r.mixed[...] = jnp.zeros_like(r.mixed)
     for i in range(count // step):
         part = slice(i * step, (i + 1) * step)
-        out, lse = attend(q1[part], i * step, k1, v1, (i + 1) * step)
-        att1[part] = out
-        lse1[part] = lse
-        mixed[part, 0:128] = out.astype(bf16)
+        out, lse = attend(r.q1[part], i * step, r.k1, r.v1, (i + 1) * step)
+        r.att1[part] = out
+        r.lse1[part] = lse
+        r.mixed[part, 0:128] = out.astype(bf16)
+        if i == 1:
+            spread_g.relay_far()
     mine = rows_at(quarter * step, step)
-    out, lse = attend(q2[mine], quarter * step, k2, v2, count)
-    att2[...] = out
-    lse2[...] = lse
-    mixed[mine, 128:256] = out.astype(bf16)
-    spread_s.relay_x()
-    for j, (_, owner) in enumerate(head_rows(c)):
-
-        @pl.when(owner == z)
-        def _(j=j):
-            wo_local(j).wait()
-            for d in range(1, NZ):
-                wo_remote(j, d).wait_send()
-
-        @pl.when(owner != z)
-        def _(j=j):
-            wo_remote(j, 1).wait_recv()
-
-    value = plane_reduce(lambda o: dot(mixed[rows_at(o * length, length)], woall[...]), c, z, reduce_refs)
-    hidden = x_ref[...].astype(f32) + value
-    hidden_ref[...] = hidden
+    out, lse = attend(r.q2[mine], quarter * step, r.k2, r.v2, count)
+    r.att2[...] = out
+    r.lse2[...] = lse
+    r.mixed[mine, 128:256] = out.astype(bf16)
+    spread_s.relay_z()
+
+    value = plane_reduce(
+        lambda o: dot(r.mixed[rows_at(o * length, length)], r.woall[...]), c, z, reduce_refs
+    )
+    hidden = r.x[...].astype(f32) + value
+    r.hidden[...] = hidden
     tokens = (hidden * norm_factor(hidden) * gain_two).astype(bf16)
-    b_ref[...] = tokens
+    r.tokens[...] = tokens
     logits = dot(packed[0:16].astype(bf16), tokens, NT)
     shifted = jnp.exp(logits - jnp.max(logits, axis=0, keepdims=True))
     gates = shifted / jnp.sum(shifted, axis=0, keepdims=True)
-    gates_ref[...] = gates
+    r.gates[...] = gates
     lane = lax.broadcasted_iota(jnp.int32, (length, 128), 1)
     named = jnp.zeros((length, 128), f32)
-    for k in range(routes_ref.shape[1]):
-        named = named + jnp.where(lane == routes_ref[:, k : k + 1], 1.0, 0.0)
+    for k in range(r.routes.shape[1]):
+        named = named + jnp.where(lane == r.routes[:, k : k + 1], 1.0, 0.0)
     named = named.T[0:16]
-    order = jnp.broadcast_to(prio_ref[...].astype(f32), (length, length))
+    order = jnp.broadcast_to(r.prio[...].astype(f32), (length, length))
     earlier = jnp.where(order.T < order, 1.0, 0.0).astype(bf16)
     rank = dot(named.astype(bf16), earlier)
     kept = (named > 0.0) & (rank < float(capacity))
-    table_ref[:, 0:length] = jnp.where(kept, rank, -1.0)
-    table_ref[:, length : 2 * length] = jnp.where(kept, gates, 0.0)
-    spread_g.relay_x()
+    r.table[:, 0:length] = jnp.where(kept, rank, -1.0)
+    r.table[:, length : 2 * length] = jnp.where(kept, gates, 0.0)
+    spread_b.start_z()
+    spread_b.start_x()
+    spread_t.start_z()
+    spread_t.start_x()
+    for d in range(1, NZ):
+        wgcopy(1, d).start()
+    r.acc[...] = jnp.zeros_like(r.acc)
+    r.ddn[...] = jnp.zeros_like(r.ddn)
+    r.st[group:final] = jnp.zeros((16, width), bf16)
+    r.zbuf[...] = jnp.zeros_like(r.zbuf)
+    for copy in down:
+        copy.wait()
+    r.wdn[:, hidden_dev:] = jnp.zeros((3, WIDE - hidden_dev, width), bf16)
+    for d in range(NZ):
+        spread_s.relay_near(d)
+    spread_s.relay_far()
+    spread_b.relay_z()
+    spread_t.relay_z()
+    for d in range(NZ):
+        spread_b.relay_near(d)
+        spread_t.relay_near(d)
+    spread_b.relay_far()
+    spread_t.relay_far()
+    spread_s.arrive()
     spread_g.arrive()
-    spread_s.arrive()
+    spread_b.arrive()
+    spread_t.arrive()
     wgown.wait()
     for d in range(1, NZ):
-        wgwait(d)
-        wgcopy(d).wait_send()
+        wgwait(0, d)
+        wgwait(1, d)
+    spread_x.drain()
+
+    def target(g):
+        left = 3 - g // 2
+        return flip(c, left % 2, left // 2, 1 - g % 2)
+
+    def loads(g):
+        slot = g % 2
+        there = target(g)
+        return (
+            pltpu.make_async_copy(r.ball.at[there], r.bg.at[rows_at(slot * group, group)], lsem.at[slot, 0]),
+            pltpu.make_async_copy(r.gall.at[there], r.gg.at[rows_at(slot * group, group)], lsem.at[slot, 1]),
+            pltpu.make_async_copy(r.tall.at[there], r.tg.at[slot], lsem.at[slot, 2]),
+        )
+
+    final = group + 16
+
+    def to_mate(s):
+        return remote(r.st, r.ld.at[s % 2], ms.at[s], mr.at[s], mate, z)
+
+    def to_chip(s, d):
+        left = 3 - s
+        there = flip(c, left % 2, left // 2, 0)
+        if d == NZ:
+            part = (slice(group, final), slice(0, group))
+        else:
+            part = (rows_at((z + d) % NZ * length, length), slice(None))
+        return remote(r.stc.at[(s,) + part], r.xrecv.at[(s,) + part], xs_s.at[s, d], xs_r.at[s, d], there, z)
+
+    def keep_y(s):
+        return pltpu.make_async_copy(r.sty, r.ypart.at[s], ysem)
+
+    slot_ids = lax.broadcasted_iota(jnp.int32, (SLOTS, length), 0).astype(f32)
+    row_ids = lax.broadcasted_iota(jnp.int32, (16, length), 0)
+    table_rows = lax.broadcasted_iota(jnp.int32, (16, 2 * length), 0)
+
+    acopy.wait()
+    for copy in loads(0):
+        copy.start()
+
+    def body(s, carry):
+        for par in range(2):
+            one_group(s, par)
+        return carry
+
+    def one_group(s, par):
+        g = 2 * s + par
+        slot = par
+        for copy in loads(g):
+            copy.wait()
+
+        @pl.when(g < 7)
+        def _():
+            for copy in loads(g + 1):
+                copy.start()
+
+        @pl.when(s > 0)
+        def _():
+            if par == 0:
+                to_mate(s - 1).wait_send()
+            else:
+                keep_y(s - 1).wait()
+
+        scales = [[], []]
+        for q in range(NZ):
+            hits = []
+            for e in range(2):
+                mine = jnp.sum(jnp.where(table_rows == 2 * c + e, r.tg[slot, q], 0.0), axis=0, keepdims=True)
+                rank = mine[:, :length]
+                share = mine[:, length:]
+                hit = slot_ids == rank
+                scales[e].append(jnp.sum(jnp.where(hit, share, 0.0), axis=1, keepdims=True))
+                hits.append(jnp.where(hit, 1.0, 0.0))
+            hot = jnp.concatenate(hits, axis=0).astype(bf16)
+            r.oh[q] = hot
+            for ref, at in ((r.bg, 0), (r.gg, group)):
+                first = slot * group + q * length
+                part = dot(hot, ref[first : first + length]).astype(bf16)
+                r.pool[at + q * SLOTS : at + (q + 1) * SLOTS] = part[:SLOTS]
+                r.pool[at + step + q * SLOTS : at + step + (q + 1) * SLOTS] = part[SLOTS:]
+        back = [0.0] * NZ
+        for e in range(2):
+            own = slice(step * e, step * (e + 1))
+            other = slice(group + step * e, group + step * (e + 1))
+            scale = jnp.concatenate(scales[e], axis=0)
+            both = dot(r.pool[own], r.wgu[e])
+            up = both[:, WIDE:]
+            silu, slope = swish(both[:, :WIDE])
+            inner = (silu * up).astype(bf16)
+            scaled = (inner.astype(f32) * scale).astype(bf16)
+            out = dot(scaled, r.wdn[e]).astype(bf16)
+            pull = dot(r.pool[other], r.wdn[e], NT)
+            gain = jnp.sum(inner.astype(f32) * pull, axis=1, keepdims=True)
+            pull = pull * scale
+            turn = jnp.concatenate([(pull * up * slope).astype(bf16), (pull * silu).astype(bf16)], axis=1)
+            r.ddn[e] += dot(scaled, r.pool[other], TN)
+            r.acc[e] += dot(r.pool[own], turn, TN)
+            into = dot(turn, r.wgu[e], NT).astype(bf16)
+            for q in range(NZ):
+                part = slice(q * SLOTS, (q + 1) * SLOTS)
+                r.ys[q, e * SLOTS : (e + 1) * SLOTS] = out[part]
+                r.ds[q, e * SLOTS : (e + 1) * SLOTS] = into[part]
+                hit = r.oh[q, e * SLOTS : (e + 1) * SLOTS].astype(f32)
+                line = jnp.sum(hit * gain[part], axis=0, keepdims=True)
+                back[q] = back[q] + jnp.where(row_ids == 2 * c + e, line, 0.0)
+        if par == 1:
+            to_mate(s).wait_recv()
+        for q in range(NZ):
+            part = slice(q * length, (q + 1) * length)
+            more = slice(final + q * length, final + (q + 1) * length)
+            pulled = dot(r.oh[q], r.ds[q], TN)
+            value = dot(r.oh[q], r.ys[q], TN)
+            if par == 0:
+                r.st[part] = pulled.astype(bf16)
+                r.st[more] = value.astype(bf16)
+                r.st[group:final, part] = back[q].astype(bf16)
+            else:
+                arrived = r.ld.at[s % 2]
+                r.stc[s, part] = (pulled + arrived[part].astype(f32)).astype(bf16)
+                r.sty[part] = (value + arrived[more].astype(f32)).astype(bf16)
+                r.stc[s, group:final, part] = (back[q] + arrived[group:final, part].astype(f32)).astype(bf16)
+
+        def own_column():
+            for h in range(2):
+                first = slot * group + h * step
+                tokens = r.bg[first : first + step]
+                upper = r.gg[first : first + step]
+                both = dot(tokens, r.wgu[2])
+                up = both[:, WIDE:]
+                silu, slope = swish(both[:, :WIDE])
+                inner = (silu * up).astype(bf16)
+                part = slice(step * h, step * (h + 1))
+                r.sty[part] = (r.sty[part].astype(f32) + dot(inner, r.wdn[2])).astype(bf16)
+                pull = dot(upper, r.wdn[2], NT)
+                turn = jnp.concatenate([(pull * up * slope).astype(bf16), (pull * silu).astype(bf16)], axis=1)
+                r.stc[3, part] = (r.stc[3, part].astype(f32) + dot(turn, r.wgu[2], NT)).astype(bf16)
+                if h == 0:
+                    r.dsdn[...] = dot(inner, upper, TN).astype(bf16)
+                    r.dsgu[...] = dot(tokens, turn, TN).astype(bf16)
+                else:
+                    r.dsdn[...] = (r.dsdn[...].astype(f32) + dot(inner, upper, TN)).astype(bf16)
+                    r.dsgu[...] = (r.dsgu[...].astype(f32) + dot(tokens, turn, TN)).astype(bf16)
+
+        if par == 0:
+            to_mate(s).start()
+        else:
+            pl.when(s == 3)(own_column)
+            keep_y(s).start()
+
+            @pl.when(s < 3)
+            def _():
+                for d in range(NZ + 1):
+                    to_chip(s, d).start()
+
+    lax.fori_loop(0, 4, body, 0)
+    for i in range(3):
+        to_chip(i, NZ).wait_recv()
+
+    def zcopy(d):
+        there = (z + d) % NZ
+        return remote(
+            r.zbuf.at[there, 0:length], r.zrecv.at[d - 1, 0:length], zs.at[d - 1, 0], zr.at[d - 1, 0], c, there
+        )
+
+    def zsmall(d):
+        there = (z + d) % NZ
+        lanes = (slice(length, length + 16), slice(0, length))
+        return remote(
+            r.zbuf.at[(there,) + lanes], r.zrecv.at[(d - 1,) + lanes], zs.at[d - 1, 1], zr.at[d - 1, 1], c, there
+        )
+
+    for d in (1, 2, 3, 0):
+        q = (z + d) % NZ
+        for i in range(3):
+            to_chip(i, d).wait_recv()
+
+        def add(i, carry):
+            part = rows_at(i * 16, 16)
+            there = rows_at(q * length + i * 16, 16)
+            total = r.stc[3, there].astype(f32)
+            for k in range(3):
+                total = total + r.xrecv[k, there].astype(f32)
+            r.zbuf[q, part] = total.astype(bf16)
+            return carry
+
+        lax.fori_loop(0, length // 16, add, 0)
+        total = r.stc[3, group:final, lanes_at(q * length, length)].astype(f32)
+        for k in range(3):
+            total = total + r.xrecv[k, group:final, lanes_at(q * length, length)].astype(f32)
+        r.zbuf[q, length : length + 16, 0:length] = total.astype(bf16)
+        if d:
+            zcopy(d).start()
+            zsmall(d).start()
+    r.wgu[0:2] = r.acc[...].astype(bf16)
+    acccopy = pltpu.make_async_copy(r.wgu.at[0:2], r.accout, accsem)
+    acccopy.start()
+    for d in range(1, NZ):
+        zcopy(d).wait_recv()
+        zsmall(d).wait_recv()
+
+    def settle(i, carry):
+        part = rows_at(i * 16, 16)
+        value = r.zbuf[z, part].astype(f32)
+        for d in range(3):
+            value = value + r.zrecv[d, part].astype(f32)
+        r.db[part] = value
+        return carry
+
+    lax.fori_loop(0, length // 16, settle, 0)
+    value = r.zbuf[z, length : length + 16, 0:length].astype(f32)
+    for d in range(3):
+        value = value + r.zrecv[d, length : length + 16, 0:length].astype(f32)
+    r.dg[...] = value
+    acccopy.wait()
+    to_mate(3).wait_send()
+    for i in range(3):
+        for d in range(NZ + 1):
+            to_chip(i, d).wait_send()
+    keep_y(3).wait()
+    wo_each(wo_drain)
+    for d in range(1, NZ):
+        zcopy(d).wait_send()
+        zsmall(d).wait_send()
+        wgcopy(0, d).wait_send()
+        wgcopy(1, d).wait_send()
         h1copy(d).wait_send()
         pcopy(d).wait_send()
-    for spread in (spread_x, spread_docs, spread_h2, spread_g, spread_s):
+    for spread in (spread_docs, spread_h2, spread_g, spread_s, spread_b, spread_t):
         spread.drain()
 
 
-def attention_stage(capacity, x, packed, docs, routes, prio, cosine, sine, upstream, wq, wk, wv, wo, wsend):
+def front_stage(capacity, *operands):
+    x, cosine = operands[0], operands[6]
     length, width = x.shape
     count = cosine.shape[0]
+    shard = width // NZ
+    group = NZ * length
+    final = group + 16
+    inner = 2 * WIDE
     dma = pltpu.SemaphoreType.DMA
     hbm = pl.BlockSpec(memory_space=pl.ANY)
     vmem = pl.BlockSpec(memory_space=pltpu.VMEM)
@@ -504,338 +880,54 @@
     shape = jax.ShapeDtypeStruct
     head = lambda rows, kind: shape((rows, HEAD_DIM), kind)
     return pl.pallas_call(
-        functools.partial(attention_kernel, capacity),
-        name="attention",
+        functools.partial(front_kernel, capacity),
+        name="front",
         out_shape=[
-            shape((length, width), f32), shape((length, width), bf16), shape((16, 2 * length), f32),
-            shape((16, length), f32), shape((32, width), f32), shape((8, 128), f32),
+            shape((length, width), f32), shape((length, width), bf16), shape((16, length), f32),
+            shape((32, width), f32), shape((8, 128), f32),
             shape((count, width), bf16), shape((width, 768), bf16), shape((256, width), bf16),
             head(count, bf16), head(count, bf16), head(count, bf16), head(count, bf16), head(count, bf16),
             head(count, bf16), head(count, f32), head(count, f32), head(2 * length, f32), head(2 * length, f32),
-            shape((count, 256), bf16), shape((8, NZ, length, width), bf16), shape((3, width, 2 * WIDE), bf16),
+            shape((count, 256), bf16), shape((length, width), f32), shape((16, length), f32),
+            shape((2, WIDE, width), f32), shape((width, inner), bf16), shape((WIDE, width), bf16),
+            shape((8, group, width), bf16), shape((NZ, 3, shard, inner), bf16), shape((8, group, width), bf16), shape((8, NZ, 16, 2 * length), f32),
+            shape((4, group, width), bf16), shape((2, width, inner), bf16),
         ],
-        in_specs=[vmem] * 7 + [hbm] * 6,
-        out_specs=[vmem] * 20 + [hbm] * 2,
+        in_specs=[vmem] * 8 + [hbm] * 11,
+        out_specs=[vmem] * 5 + [hbm] + [vmem] * 18 + [hbm] * 6,
         scratch_shapes=[
-            pltpu.VMEM((8, length, width), bf16), pltpu.VMEM((8, 8, 128), f32), pltpu.VMEM((3, 32, width), bf16),
+            pltpu.VMEM((2 * group, width), bf16), pltpu.VMEM((9, 8, 128), f32), pltpu.VMEM((32, width), bf16),
+            pltpu.VMEM((3, 32, width), bf16),
+            pltpu.VMEM((NZ, shard, inner), bf16), pltpu.VMEM((3, width, inner), bf16),
+            pltpu.VMEM((3, WIDE, width), bf16), pltpu.VMEM((16, 2 * length), f32), pltpu.VMEM((2, width, inner), f32),
+            pltpu.VMEM((2 * group, width), bf16), pltpu.VMEM((2 * group, width), bf16),
+            pltpu.VMEM((2, NZ, 16, 2 * length), f32), pltpu.VMEM((NZ, 2 * SLOTS, length), bf16),
+            pltpu.VMEM((NZ, 2 * SLOTS, width), bf16), pltpu.VMEM((NZ, 2 * SLOTS, width), bf16),
+            pltpu.VMEM((group + final, width), bf16), pltpu.VMEM((4, final, width), bf16),
+            pltpu.VMEM((group, width), bf16), pltpu.VMEM((2, group + final, width), bf16),
+            pltpu.VMEM((3, final, width), bf16), pltpu.VMEM((NZ, length + 16, width), bf16),
+            pltpu.VMEM((3, length + 16, width), bf16),
         ]
-        + spread_sems(1) + spread_sems(1) + spread_sems(NZ, 1) + spread_sems() + spread_sems()
+        + spread_sems(1) + spread_sems(1) + spread_sems(NZ, 1) + spread_sems() + spread_sems() + spread_sems()
+        + spread_sems()
         + [
-            dma((3,)), dma((3,)), dma((6,)), dma((3,)), dma((3,)), dma((4,)), dma((4, 3)), dma((4,)),
-            dma, dma((3,)), dma((3,)),
+            dma((3,)), dma((3,)), dma((6,)), dma((3,)), dma((3,)), dma((4,)), dma((4, 2)), dma((4,)),
+            dma, dma((2, 3)), dma((2, 3)), dma((2,)), dma, dma((3,)), dma,
+            dma((2, 3)), dma((4,)), dma((4,)), dma((3, NZ + 1)), dma((3, NZ + 1)), dma((3, 2)), dma((3, 2)), dma, dma,
         ]
-        + plane_scratch(length, width),
+        + plane_scratch(length, width)[3:],
         compiler_params=pltpu.CompilerParams(
-            collective_id=2, has_side_effects=True, vmem_limit_bytes=60 * MIB
+            collective_id=1, has_side_effects=True, vmem_limit_bytes=62 * MIB
         ),
-    )(x, packed, docs, routes, prio, cosine, sine, upstream, wq, wk, wv, wo, wsend)
-
-
-def expert_kernel(
-    b_ref, t_ref, gall, wgu, wdn_ref,
-    y_ref, db_ref, dg_ref, dgu_ref, ddn_ref, dsgu_ref, dsdn_ref, ball, tall, mrecv, xrecv,
-    acc, bg, gg, tg, oh, xs, gs, ys, ds, st, ld, zbuf, zrecv, gst,
-    sb0, sb1, sb2, sb3, sb4, sb5, sb6, st0, st1, st2, st3, st4, st5, st6,
-    lsem, ms, mr, xs_s, xs_r, ldsem, zs, zr, gl, gss, grs,
-):
-    c = lax.axis_index("ctx")
-    z = lax.axis_index("fsdp")
-    f32, bf16 = jnp.float32, jnp.bfloat16
-    mate = flip(c, 0, 0, 1)
-    length = b_ref.shape[0]
-    group = NZ * length
-    rows = wgu.shape[1] // NZ
-    greet(c, z)
-    spread_b = Spread(lambda _: b_ref, lambda o, q: ball.at[o, q], (sb0, sb1, sb2, sb3, sb4, sb5, sb6), c, z)
-    spread_t = Spread(lambda _: t_ref, lambda o, q: tall.at[o, q], (st0, st1, st2, st3, st4, st5, st6), c, z)
-    for spread in (spread_t, spread_b):
-        spread.start_z()
-        spread.start_x()
-    acc[...] = jnp.zeros_like(acc)
-    ddn_ref[...] = jnp.zeros_like(ddn_ref)
-    st[...] = jnp.zeros_like(st)
-    zbuf[...] = jnp.zeros_like(zbuf)
-    spread_t.relay_z()
-    spread_b.relay_z()
-    spread_t.relay_x()
-    spread_b.relay_x()
-    spread_t.arrive()
-    spread_b.arrive()
-
-    def target(g):
-        left = 3 - g // 2
-        return flip(c, left % 2, left // 2, 1 - g % 2)
-
-    def loads(g):
-        slot = g % 2
-        there = target(g)
-        return (
-            pltpu.make_async_copy(ball.at[there], bg.at[slot], lsem.at[slot, 0]),
-            pltpu.make_async_copy(gall.at[there], gg.at[slot], lsem.at[slot, 1]),
-            pltpu.make_async_copy(tall.at[there], tg.at[slot], lsem.at[slot, 2]),
-        )
-
-    def to_mate(s):
-        return remote(st.at[0], mrecv.at[s], ms.at[s], mr.at[s], mate, z)
-
-    def to_chip(s):
-        left = 3 - s
-        return remote(st.at[1], xrecv.at[s], xs_s.at[s], xs_r.at[s], flip(c, left % 2, left // 2, 0), z)
-
-    for copy in loads(0):
-        copy.start()
-    slot_ids = lax.broadcasted_iota(jnp.int32, (SLOTS, length), 0).astype(f32)
-    row_ids = lax.broadcasted_iota(jnp.int32, (16, length), 0)
-    table_rows = lax.broadcasted_iota(jnp.int32, (16, 2 * length), 0)
-
-    def step(g, carry):
-        slot = g % 2
-        s = g // 2
-        par = g % 2
-        for copy in loads(g):
-            copy.wait()
-
-        @pl.when(g < 7)
-        def _():
-            for copy in loads(g + 1):
-                copy.start()
-
-        @pl.when((s > 0) & (par == 0))
-        def _():
-            to_mate(s - 1).wait_send()
-
-        @pl.when((s > 0) & (par == 1))
-        def _():
-            to_chip(s - 1).wait_send()
-
-        scales = [[], []]
-        for q in range(NZ):
-            hits = []
-            for e in range(2):
-                mine = jnp.sum(jnp.where(table_rows == 2 * c + e, tg[slot, q], 0.0), axis=0, keepdims=True)
-                rank = mine[:, :length]
-                share = mine[:, length:]
-                hit = slot_ids == rank
-                scales[e].append(jnp.sum(jnp.where(hit, share, 0.0), axis=1, keepdims=True))
-                hits.append(jnp.where(hit, 1.0, 0.0))
-            hot = jnp.concatenate(hits, axis=0).astype(bf16)
-            oh[q] = hot
-            part = dot(hot, bg[slot, q]).astype(bf16)
-            xs[0, q * SLOTS : (q + 1) * SLOTS] = part[:SLOTS]
-            xs[1, q * SLOTS : (q + 1) * SLOTS] = part[SLOTS:]
-            part = dot(hot, gg[slot, q]).astype(bf16)
-            gs[0, q * SLOTS : (q + 1) * SLOTS] = part[:SLOTS]
-            gs[1, q * SLOTS : (q + 1) * SLOTS] = part[SLOTS:]
-        back = [0.0] * NZ
-        for e in range(2):
-            scale = jnp.concatenate(scales[e], axis=0)
-            both = dot(xs[e], wgu[e])
-            up = both[:, WIDE:]
-            silu, slope = swish(both[:, :WIDE])
-            inner = (silu * up).astype(bf16)
-            scaled = (inner.astype(f32) * scale).astype(bf16)
-            out = dot(scaled, wdn_ref[e]).astype(bf16)
-            pull = dot(gs[e], wdn_ref[e], NT)
-            gain = jnp.sum(inner.astype(f32) * pull, axis=1, keepdims=True)
-            pull = pull * scale
-            turn = jnp.concatenate([(pull * up * slope).astype(bf16), (pull * silu).astype(bf16)], axis=1)
-            ddn_ref[e] += dot(scaled, gs[e], TN)
-            acc[e] += dot(xs[e], turn, TN)
-            into = dot(turn, wgu[e], NT).astype(bf16)
-            for q in range(NZ):
-                part = slice(q * SLOTS, (q + 1) * SLOTS)
-                ys[q, e * SLOTS : (e + 1) * SLOTS] = out[part]
-                ds[q, e * SLOTS : (e + 1) * SLOTS] = into[part]
-                hit = oh[q, e * SLOTS : (e + 1) * SLOTS].astype(f32)
-                line = jnp.sum(hit * gain[part], axis=0, keepdims=True)
-                back[q] = back[q] + jnp.where(row_ids == 2 * c + e, line, 0.0)
-        for q in range(NZ):
-            st[par, q * length : (q + 1) * length] = dot(oh[q], ds[q], TN).astype(bf16)
-            st[par, group + q * length : group + (q + 1) * length] = dot(oh[q], ys[q], TN).astype(bf16)
-            st[par, 2 * group :, q * length : (q + 1) * length] = back[q].astype(bf16)
-
-        @pl.when(g == 7)
-        def _():
-            for h in range(2):
-                tokens = bg[slot, 2 * h : 2 * h + 2].reshape(2 * length, bg.shape[3])
-                upper = gg[slot, 2 * h : 2 * h + 2].reshape(2 * length, bg.shape[3])
-                both = dot(tokens, wgu[2])
-                up = both[:, WIDE:]
-                silu, slope = swish(both[:, :WIDE])
-                inner = (silu * up).astype(bf16)
-                part = slice(2 * h * length, 2 * (h + 1) * length)
-                more = slice(group + 2 * h * length, group + 2 * (h + 1) * length)
-                st[1, more] = (st[1, more].astype(f32) + dot(inner, wdn_ref[2])).astype(bf16)
-                pull = dot(upper, wdn_ref[2], NT)
-                turn = jnp.concatenate([(pull * up * slope).astype(bf16), (pull * silu).astype(bf16)], axis=1)
-                st[1, part] = (st[1, part].astype(f32) + dot(turn, wgu[2], NT)).astype(bf16)
-                if h == 0:
-                    dsdn_ref[...] = dot(inner, upper, TN)
-                    dsgu_ref[...] = dot(tokens, turn, TN)
-                else:
-                    dsdn_ref[...] += dot(inner, upper, TN)
-                    dsgu_ref[...] += dot(tokens, turn, TN)
-
-        @pl.when(par == 0)
-        def _():
-            to_mate(s).start()
-
-        @pl.when(par == 1)
-        def _():
-            to_mate(s).wait_recv()
-            copy = pltpu.make_async_copy(mrecv.at[s], ld.at[0], ldsem.at[0])
-            copy.start()
-            copy.wait()
-
-            def add(i, carry):
-                part = pl.ds(pl.multiple_of(i * 16, 16), 16)
-                st[1, part] = (st[1, part].astype(f32) + ld[0, part].astype(f32)).astype(bf16)
-                return carry
-
-            lax.fori_loop(0, st.shape[1] // 16, add, 0)
-
-            @pl.when(s < 3)
-            def _():
-                to_chip(s).start()
-
-        return carry
-
-    lax.fori_loop(0, 8, step, 0)
-    to_mate(3).wait_send()
-    for e in range(2):
-        gst[e] = acc[e].astype(bf16)
-
-    def gcopy(d):
-        there = (z + d) % NZ
-        return remote(
-            gst.at[:, pl.ds(pl.multiple_of(there * rows, rows), rows), :], dgu_ref.at[z],
-            gss.at[d - 1], grs.at[d - 1], c, there,
-        )
-
-    gown = pltpu.make_async_copy(gst.at[:, pl.ds(pl.multiple_of(z * rows, rows), rows), :], dgu_ref.at[z], gl)
-    gown.start()
-    for i in range(3):
-        to_chip(i).wait_recv()
-        pltpu.make_async_copy(xrecv.at[i], ld.at[i], ldsem.at[i]).start()
-    for i in range(3):
-        pltpu.make_async_copy(xrecv.at[i], ld.at[i], ldsem.at[i]).wait()
-
-    def total(part, lanes=slice(None)):
-        value = st[1, part, lanes].astype(f32)
-        for i in range(3):
-            value = value + ld[i, part, lanes].astype(f32)
-        return value.astype(bf16)
-
-    for q in range(NZ):
-
-        def add(i, carry):
-            base = pl.multiple_of(i * 16, 16)
-            zbuf[q, pl.ds(base, 16)] = total(pl.ds(pl.multiple_of(base + q * length, 16), 16))
-            zbuf[q, pl.ds(pl.multiple_of(base + length, 16), 16)] = total(
-                pl.ds(pl.multiple_of(base + group + q * length, 16), 16)
-            )
-            return carry
-
-        lax.fori_loop(0, length // 16, add, 0)
-        zbuf[q, 2 * length : 2 * length + 16, 0:length] = total(
-            slice(2 * group, 2 * group + 16), slice(q * length, (q + 1) * length)
-        )
-
-    def zcopy(d):
-        there = (z + d) % NZ
-        return remote(zbuf.at[there], zrecv.at[d - 1], zs.at[d - 1], zr.at[d - 1], c, there)
-
-    for d in range(1, NZ):
-        zcopy(d).start()
-    for d in range(1, NZ):
-        gcopy(d).start()
-    for d in range(1, NZ):
-        zcopy(d).wait_recv()
-
-    def settle(i, carry):
-        base = pl.multiple_of(i * 16, 16)
-        for ref, start in ((db_ref, 0), (y_ref, length)):
-            part = pl.ds(pl.multiple_of(base + start, 16), 16)
-            value = zbuf[z, part].astype(f32)
-            for d in range(3):
-                value = value + zrecv[d, part].astype(f32)
-            ref[pl.ds(base, 16)] = value
-        return carry
-
-    lax.fori_loop(0, length // 16, settle, 0)
-    last = slice(2 * length, 2 * length + 16)
-    value = zbuf[z, last, 0:length].astype(f32)
-    for d in range(3):
-        value = value + zrecv[d, last, 0:length].astype(f32)
-    dg_ref[...] = value
-    for d in range(1, NZ):
-        zcopy(d).wait_send()
-        gcopy(d).wait()
-    gown.wait()
-    spread_t.drain()
-    spread_b.drain()
-
-
-def expert_stage(moe_input, table, gall, wgu, wdn):
-    length, width = moe_input.shape
-    dma = pltpu.SemaphoreType.DMA
-    hbm = pl.BlockSpec(memory_space=pl.ANY)
-    vmem = pl.BlockSpec(memory_space=pltpu.VMEM)
-    f32, bf16 = jnp.float32, jnp.bfloat16
-    shape = jax.ShapeDtypeStruct
-    inner = 2 * WIDE
-    group = NZ * length
-    rows = width // NZ
-    return pl.pallas_call(
-        expert_kernel,
-        name="experts",
-        out_shape=[
-            shape((length, width), f32),
-            shape((length, width), f32),
-            shape((16, length), f32),
-            shape((NZ, 2, rows, inner), bf16),
-            shape((2, WIDE, width), f32),
-            shape((width, inner), f32),
-            shape((WIDE, width), f32),
-            shape((8, NZ, length, width), bf16),
-            shape((8, NZ, 16, 2 * length), f32),
-            shape((4, 2 * group + 16, width), bf16),
-            shape((3, 2 * group + 16, width), bf16),
-        ],
-        in_specs=[hbm, hbm, hbm, vmem, vmem],
-        out_specs=[vmem, vmem, vmem, hbm, vmem, vmem, vmem, hbm, hbm, hbm, hbm],
-        scratch_shapes=[
-            pltpu.VMEM((2, width, inner), f32),
-            pltpu.VMEM((2, NZ, length, width), bf16),
-            pltpu.VMEM((2, NZ, length, width), bf16),
-            pltpu.VMEM((2, NZ, 16, 2 * length), f32),
-            pltpu.VMEM((NZ, 2 * SLOTS, length), bf16),
-            pltpu.VMEM((2, NZ * SLOTS, width), bf16),
-            pltpu.VMEM((2, NZ * SLOTS, width), bf16),
-            pltpu.VMEM((NZ, 2 * SLOTS, width), bf16),
-            pltpu.VMEM((NZ, 2 * SLOTS, width), bf16),
-            pltpu.VMEM((2, 2 * group + 16, width), bf16),
-            pltpu.VMEM((3, 2 * group + 16, width), bf16),
-            pltpu.VMEM((NZ, 2 * length + 16, width), bf16),
-            pltpu.VMEM((3, 2 * length + 16, width), bf16),
-            pltpu.VMEM((2, width, inner), bf16),
-        ]
-        + spread_sems() + spread_sems()
-        + [
-            dma((2, 3)), dma((4,)), dma((4,)), dma((3,)), dma((3,)), dma((3,)),
-            dma((3,)), dma((3,)), dma, dma((3,)), dma((3,)),
-        ],
-        compiler_params=pltpu.CompilerParams(
-            collective_id=1, has_side_effects=True, vmem_limit_bytes=60 * MIB
-        ),
-    )(moe_input, table, gall, wgu, wdn)
+    )(*operands)
 
 
 def backward_kernel(
-    db_ref, dg_ref, g_ref, x_ref, hidden_ref, b_ref, gates_ref, psum_ref, bound_ref, cos_ref, sin_ref,
+    ypart, accout, dsgu, dsdn, db_ref, dg_ref, g_ref, x_ref, hidden_ref, b_ref, gates_ref, psum_ref, bound_ref, cos_ref, sin_ref,
     aall, wall, woall, q1, k1, v1, q2, k2, v2, att1, lse1, att2, lse2, mixed,
-    gtok_ref, small_ref, gwq_ref, gwk_ref, gwv_ref, gwo_ref,
-    dhb, dhall, dm, dk, dv, cat, wst, wrecv, wsum, wfinal, dwo, worecv, wosum, wofinal, small4, *sems,
+    out_ref, gtok_ref, small_ref, wfinal, wofinal, dgu, sfin, sdfin, yrecv,
+    dhb, dhall, dm, dk, dv, cat, wst, wrecv, wsum, dwo, worecv, wosum, small4,
+    sgm, sdm, sgs, sds, sgx, sdx, sgt, sgz, sdt, ybuf, ysend, yz, *sems,
 ):
     f32, bf16 = jnp.float32, jnp.bfloat16
     c = lax.axis_index("ctx")
@@ -848,15 +940,52 @@
     scale = HEAD_DIM**-0.5
     sems = list(sems)
 
-    def take(n):
-        taken = sems[:n]
-        del sems[:n]
-        return taken
-
-    spread_h = Spread(lambda _: dhb, lambda o, _: dhall.at[o], take(7), c, z, 1)
-    spread_w = Spread(lambda _: wsum, lambda o, _: wfinal.at[o], take(7), c, z, 1)
-    wzs, wzr, ozs, ozr, oxs, oxr, oms, omr, ss, sr = take(10)
-    reduce_refs = take(8)
+    spread_h = Spread(lambda _: dhb, lambda o, _: dhall.at[o], take(sems, 7), c, z, 1)
+    spread_w = Spread(lambda _: wsum, lambda o, _: wfinal.at[o], take(sems, 7), c, z, 1)
+    wzs, wzr, ozs, ozr, oxs, oxr, oms, omr, ss, sr = take(sems, 10)
+    yxs, yxr, yzs, yzr, gas, gar, gal, sms, smr, sxs, sxr, szs, szr, ylsem, olsem = take(sems, 15)
+    spread_s = Spread(lambda _: sgz, lambda o, _: sfin.at[o], take(sems, 7), c, z, 1)
+    spread_d = Spread(lambda _: sdt, lambda o, _: sdfin.at[o], take(sems, 7), c, z, 1)
+    reduce_refs = take(sems, 8)
+    core = c % 2
+    chip = c // 2
+    sub = shard // 4
+    part_rows = sdt.shape[0]
+
+    def ycopy(i):
+        return remote(
+            ypart.at[(1, 2, 0)[i]], yrecv.at[i], yxs.at[i], yxr.at[i], flip(c, PEERS[i][0], PEERS[i][1], 0), z
+        )
+
+    def yload(i):
+        src = ypart.at[3] if i == 3 else yrecv.at[i]
+        return pltpu.make_async_copy(src, ybuf.at[i], ylsem.at[i])
+
+    def yhop(d):
+        return remote(ysend.at[(z + d) % NZ], yz.at[d - 1], yzs.at[d - 1], yzr.at[d - 1], c, (z + d) % NZ)
+
+    def gcopy(d):
+        there = (z + d) % NZ
+        return remote(
+            accout.at[:, rows_at(there * shard, shard), :], dgu.at[z], gas.at[d - 1], gar.at[d - 1], c, there
+        )
+
+    gown = pltpu.make_async_copy(accout.at[:, rows_at(z * shard, shard), :], dgu.at[z], gal)
+
+    def smate(i):
+        if i == 0:
+            return remote(dsgu.at[:, lanes_at((1 - core) * WIDE, WIDE)], sgm, sms.at[0], smr.at[0], mate, z)
+        return remote(dsdn.at[rows_at((1 - core) * 4 * part_rows, 4 * part_rows)], sdm, sms.at[1], smr.at[1], mate, z)
+
+    def schip(i, kind):
+        there = flip(c, PEERS[i][0], PEERS[i][1], 0)
+        if kind == 0:
+            return remote(sgs.at[:, there // 2], sgx.at[i], sxs.at[i, 0], sxr.at[i, 0], there, z)
+        return remote(sds.at[there // 2], sdx.at[i], sxs.at[i, 1], sxr.at[i, 1], there, z)
+
+    def shop(d):
+        there = (z + d) % NZ
+        return remote(sgt.at[there], sgz.at[z], szs.at[d - 1], szr.at[d - 1], c, there)
     greet(c, z)
     packed = psum_ref[...]
     gain_one = packed[17:18]
@@ -879,10 +1008,17 @@
     dhb[...] = d_hidden.astype(bf16)
     spread_h.start_z()
     spread_h.start_x()
+    smate(0).start()
+    smate(1).start()
+    gown.start()
+    for d in range(1, NZ):
+        gcopy(d).start()
     dk[...] = jnp.zeros_like(dk)
     dv[...] = jnp.zeros_like(dv)
     cat[:, 384:512] = jnp.zeros((count, 128), bf16)
     spread_h.relay_x()
+    for i in range(3):
+        ycopy(i).start()
     spread_h.arrive()
     step = 2 * length
     for i in range(count // step):
@@ -908,6 +1044,19 @@
         def _(j=j, owner=owner):
             oz(j, owner).start()
 
+    smate(0).wait_recv()
+    smate(1).wait_recv()
+    for q in range(NZ):
+        for j in range(4):
+            part = slice(q * shard + j * sub, q * shard + (j + 1) * sub)
+            own = dsgu[part, lanes_at(core * WIDE, WIDE)].astype(f32)
+            sgs[q, j] = (own + sgm[part].astype(f32)).astype(bf16)
+    for j in range(4):
+        own = dsdn[rows_at(core * 4 * part_rows + j * part_rows, part_rows)].astype(f32)
+        sds[j] = (own + sdm[j * part_rows : (j + 1) * part_rows].astype(f32)).astype(bf16)
+    for i in range(3):
+        schip(i, 0).start()
+        schip(i, 1).start()
     boundary = bound_ref[0:1, 0:1]
 
     def pull_back(queries, first, keys, values, n, upper, out, lse, which):
@@ -944,6 +1093,23 @@
     for d in range(1, NZ):
         wz(d).start()
 
+    total_up = [sgs[q, chip].astype(f32) for q in range(NZ)]
+    total_down = sds[chip].astype(f32)
+    for i in range(3):
+        schip(i, 0).wait_recv()
+        schip(i, 1).wait_recv()
+        for q in range(NZ):
+            total_up[q] = total_up[q] + sgx[i, q].astype(f32)
+        total_down = total_down + sdx[i].astype(f32)
+    for q in range(NZ):
+        sgt[q] = total_up[q].astype(bf16)
+    sdt[...] = total_down.astype(bf16)
+    sgz[z] = sgt[z]
+    for d in range(1, NZ):
+        shop(d).start()
+    spread_d.start_z()
+    spread_d.start_x()
+
     def ox(j, i):
         there = flip(c, PEERS[i][0], PEERS[i][1], 0)
         return remote(wosum.at[j], wofinal.at[c, j], oxs.at[j, i], oxr.at[j, i], there, z)
@@ -953,6 +1119,9 @@
         origin = flip(c, fy, fx, 0)
         src = wosum.at[j] if i == 0 else wofinal.at[origin, j]
         return remote(src, wofinal.at[origin, j], oms.at[j, i], omr.at[j, i], mate, z)
+
+    def wo_keep(j):
+        return pltpu.make_async_copy(wosum.at[j], wofinal.at[c, j], olsem.at[j])
 
     for j, (_, owner) in enumerate(head_rows(c)):
 
@@ -964,7 +1133,7 @@
             for d in range(3):
                 total = total + worecv[j, d].astype(f32)
             wosum[j] = total.astype(bf16)
-            wofinal[c, j] = total.astype(bf16)
+            wo_keep(j).start()
             for i in range(3):
                 ox(j, i).start()
             om(j, 0).start()
@@ -981,14 +1150,6 @@
         d_hidden
         + factor_one * (pulled - normed_one * jnp.mean(pulled * normed_one, axis=1, keepdims=True))
     ).astype(bf16)
-
-    total = wst[rows_at(z * shard, shard)].astype(f32)
-    for d in range(1, NZ):
-        wz(d).wait_recv()
-        total = total + wrecv[d - 1].astype(f32)
-    wsum[...] = total.astype(bf16)
-    spread_w.start_z()
-    spread_w.start_x()
 
     def exchange(stage, slots, targets):
         copies = [
@@ -1010,9 +1171,43 @@
     value, more = exchange(2, (3, 4, 5), [(flip(c, fy, fx, 0), z) for fy, fx in PEERS])
     sent += more
     small4[6] = value
-    value, more = exchange(6, (7, 8, 9), [(c, (z + d) % NZ) for d in range(1, NZ)])
-    sent += more
-    small_ref[...] = value
+    last_hop = [
+        remote(small4.at[6], small4.at[6 + d], ss.at[6 + d], sr.at[6 + d], c, (z + d) % NZ) for d in range(1, NZ)
+    ]
+    for copy in last_hop:
+        copy.start()
+    for i in range(3):
+        ycopy(i).wait_recv()
+        yload(i).start()
+    yload(3).start()
+    for d in range(1, NZ):
+        shop_wait = sgz.at[(z + NZ - d) % NZ]
+        remote(shop_wait, shop_wait, szs.at[d - 1], szr.at[d - 1], c, z).wait_recv()
+    spread_s.start_z()
+    spread_s.start_x()
+    total = wst[rows_at(z * shard, shard)].astype(f32)
+    for d in range(1, NZ):
+        wz(d).wait_recv()
+        total = total + wrecv[d - 1].astype(f32)
+    wsum[...] = total.astype(bf16)
+    spread_w.start_z()
+    spread_w.start_x()
+
+    for i in range(4):
+        yload(i).wait()
+
+    def ysum(i, carry):
+        part = rows_at(i * 16, 16)
+        value = ybuf[0, part].astype(f32)
+        for k in range(1, 4):
+            value = value + ybuf[k, part].astype(f32)
+        ysend[i // (length // 16), rows_at(i % (length // 16) * 16, 16)] = value.astype(bf16)
+        return carry
+
+    lax.fori_loop(0, NZ * length // 16, ysum, 0)
+    for d in range(1, NZ):
+        yhop(d).start()
+
     for i in range(3):
         for j, (_, owner) in enumerate(head_rows(flip(c, PEERS[i][0], PEERS[i][1], 0))):
 
@@ -1033,23 +1228,118 @@
                 block = wofinal.at[flip(c, fy, fx, 1), j]
                 remote(block, block, oms.at[j, i], omr.at[j, i], c, z).wait_recv()
 
-    for i in range(5):
-        b = 5 * z + i
-
-        @pl.when(b < 16)
-        def _(b=b, i=i):
-            low = jnp.minimum(b, 15)
-            gwo_ref[64 * i : 64 * i + 64] = wofinal[low // 2, low % 2].astype(f32)
-
-        @pl.when(b >= 16)
-        def _(b=b, i=i):
-            high = jnp.maximum(b, 16) - 16
-            gwo_ref[64 * i : 64 * i + 64] = sum(
-                wofinal[4 * (high // 2) + k, 2 + high % 2].astype(f32) for k in range(4)
-            )
-
+    value = small4[6]
+    for d in range(1, NZ):
+        last_hop[d - 1].wait_recv()
+        value = value + small4[6 + d]
+    small_ref[...] = value
+    spread_s.relay_x()
+    spread_d.relay_x()
+    value = hidden + ysend[z].astype(f32)
+    for d in range(1, NZ):
+        yhop(d).wait_recv()
+        value = value + yz[d - 1].astype(f32)
+    out_ref[...] = value.astype(bf16)
     spread_w.arrive()
-    for n, ref in enumerate((gwq_ref, gwk_ref, gwv_ref)):
+    spread_s.arrive()
+    spread_d.arrive()
+    gown.wait()
+    for d in range(1, NZ):
+        gcopy(d).wait()
+        yhop(d).wait_send()
+        shop(d).wait_send()
+    for i in range(3):
+        ycopy(i).wait_send()
+        schip(i, 0).wait_send()
+        schip(i, 1).wait_send()
+    smate(0).wait_send()
+    smate(1).wait_send()
+    for copy in sent + last_hop:
+        copy.wait_send()
+    for j, (_, owner) in enumerate(head_rows(c)):
+
+        @pl.when(owner != z)
+        def _(j=j, owner=owner):
+            oz(j, owner).wait_send()
+
+        @pl.when(owner == z)
+        def _(j=j):
+            for i in range(3):
+                ox(j, i).wait_send()
+            om(j, 0).wait_send()
+            wo_keep(j).wait()
+
+    for i in range(3):
+        for j, (_, owner) in enumerate(head_rows(flip(c, PEERS[i][0], PEERS[i][1], 0))):
+
+            @pl.when(owner == z)
+            def _(j=j, i=i):
+                om(j, i + 1).wait_send()
+
+    for d in range(1, NZ):
+        wz(d).wait_send()
+    for spread in (spread_h, spread_w, spread_s, spread_d):
+        spread.drain()
+
+
+def backward_stage(*operands):
+    x, aall, dsdn = operands[7], operands[15], operands[3]
+    length, width = x.shape
+    count = aall.shape[0]
+    shard = width // NZ
+    sub = shard // 4
+    part_rows = dsdn.shape[0] // 8
+    dma = pltpu.SemaphoreType.DMA
+    hbm = pl.BlockSpec(memory_space=pl.ANY)
+    vmem = pl.BlockSpec(memory_space=pltpu.VMEM)
+    f32, bf16 = jnp.float32, jnp.bfloat16
+    shape = jax.ShapeDtypeStruct
+    return pl.pallas_call(
+        backward_kernel,
+        name="backward",
+        out_shape=[
+            shape((length, width), bf16), shape((length, width), bf16), shape((32, width), f32),
+            shape((8, shard, 768), bf16), shape((8, 4, 64, width), bf16), shape((NZ, 2, shard, 2 * WIDE), bf16),
+            shape((8, NZ, sub, WIDE), bf16), shape((8, part_rows, width), bf16), shape((3, NZ * length, width), bf16),
+        ],
+        in_specs=[hbm] * 2 + [vmem] * (len(operands) - 2),
+        out_specs=[vmem] * 3 + [hbm] * 6,
+        scratch_shapes=[
+            pltpu.VMEM((length, width), bf16), pltpu.VMEM((8, length, width), bf16), pltpu.VMEM((count, 256), bf16),
+            pltpu.VMEM((2, count, 128), f32), pltpu.VMEM((2, count, 128), f32), pltpu.VMEM((count, 768), bf16),
+            pltpu.VMEM((width, 768), bf16), pltpu.VMEM((3, shard, 768), bf16), pltpu.VMEM((shard, 768), bf16),
+            pltpu.VMEM((256, width), f32), pltpu.VMEM((4, 3, 64, width), bf16),
+            pltpu.VMEM((4, 64, width), bf16), pltpu.VMEM((10, 32, width), f32),
+            pltpu.VMEM((width, WIDE), bf16), pltpu.VMEM((4 * part_rows, width), bf16),
+            pltpu.VMEM((NZ, 4, sub, WIDE), bf16), pltpu.VMEM((4, part_rows, width), bf16),
+            pltpu.VMEM((3, NZ, sub, WIDE), bf16), pltpu.VMEM((3, part_rows, width), bf16),
+            pltpu.VMEM((NZ, sub, WIDE), bf16), pltpu.VMEM((NZ, sub, WIDE), bf16), pltpu.VMEM((part_rows, width), bf16),
+            pltpu.VMEM((4, NZ * length, width), bf16), pltpu.VMEM((NZ, length, width), bf16),
+            pltpu.VMEM((3, length, width), bf16),
+        ]
+        + spread_sems(1) + spread_sems(1)
+        + [
+            dma((3,)), dma((3,)), dma((4,)), dma((4, 3)), dma((4, 3)), dma((4, 3)), dma((4, 4)), dma((4, 4)),
+            dma((10,)), dma((10,)),
+            dma((3,)), dma((3,)), dma((3,)), dma((3,)), dma((3,)), dma((3,)), dma, dma((2,)), dma((2,)),
+            dma((3, 2)), dma((3, 2)), dma((3,)), dma((3,)), dma((4,)), dma((4,)),
+        ]
+        + spread_sems(1) + spread_sems(1)
+        + plane_scratch(length, width),
+        compiler_params=pltpu.CompilerParams(
+            collective_id=3, has_side_effects=True, vmem_limit_bytes=62 * MIB
+        ),
+    )(*operands)
+
+
+def gather_kernel(
+    wfinal, wofinal, dgu, sfin, sdfin, ddn, gwq, gwk, gwv, gwo, gsg, gsu, gsd, geg, geu, ged,
+):
+    f32, bf16 = jnp.float32, jnp.bfloat16
+    z = lax.axis_index("fsdp")
+    hidden_dev = gsd.shape[0]
+    sub = sfin.shape[2]
+    for n, ref in enumerate((gwq, gwk, gwv)):
         for o in range(8):
             ref[:, 128 * o : 128 * o + 128] = wfinal[o, :, 128 * n : 128 * n + 128].astype(f32)
         for y in range(2):
@@ -1057,68 +1347,68 @@
             ref[:, 1024 + 128 * y : 1152 + 128 * y] = sum(
                 wfinal[4 * y + k, :, lanes].astype(f32) for k in range(4)
             )
-    for copy in sent:
-        copy.wait_send()
-    for j, (_, owner) in enumerate(head_rows(c)):
-
-        @pl.when(owner != z)
-        def _(j=j, owner=owner):
-            oz(j, owner).wait_send()
-
-        @pl.when(owner == z)
-        def _(j=j):
-            for i in range(3):
-                ox(j, i).wait_send()
-            om(j, 0).wait_send()
-
-    for i in range(3):
-        for j, (_, owner) in enumerate(head_rows(flip(c, PEERS[i][0], PEERS[i][1], 0))):
-
-            @pl.when(owner == z)
-            def _(j=j, i=i):
-                om(j, i + 1).wait_send()
-
-    for d in range(1, NZ):
-        wz(d).wait_send()
-    spread_h.drain()
-    spread_w.drain()
-
-
-def backward_stage(*operands):
-    x, aall = operands[3], operands[11]
-    length, width = x.shape
-    count = aall.shape[0]
-    shard = width // NZ
-    dma = pltpu.SemaphoreType.DMA
+    for i in range(5):
+        b = 5 * z + i
+
+        @pl.when(b < 16)
+        def _(b=b, i=i):
+            low = jnp.minimum(b, 15)
+            gwo[64 * i : 64 * i + 64] = wofinal[low // 2, low % 2].astype(f32)
+
+        @pl.when(b >= 16)
+        def _(b=b, i=i):
+            high = jnp.maximum(b, 16) - 16
+            gwo[64 * i : 64 * i + 64] = sum(
+                wofinal[4 * (high // 2) + k, 2 + high % 2].astype(f32) for k in range(4)
+            )
+
+    units = geg.shape[2]
+    for e in range(2):
+        ged[e] = ddn[e, 0:hidden_dev]
+    for o in range(8):
+        start = 128 * (o % 2) + 32 * (o // 2)
+        size = min(32, hidden_dev - start)
+        if size > 0:
+            gsd[start : start + size] = sdfin[o, 0:size].astype(f32)
+    slot = lax.broadcasted_iota(jnp.int32, (WIDE, units), 0)
+    unit = lax.broadcasted_iota(jnp.int32, (WIDE, units), 1)
+    for q in range(NZ):
+        put = jnp.where((unit == slot + q * hidden_dev) & (slot < hidden_dev), 1.0, 0.0).astype(bf16)
+        for h, (ref, shared) in enumerate(((geg, gsg), (geu, gsu))):
+            for e in range(2):
+                part = dot(dgu[q, e, :, h * WIDE : (h + 1) * WIDE], put)
+                if q == 0:
+                    ref[e] = part
+                else:
+                    ref[e] += part
+            for j in range(4):
+                part = dot(sfin[2 * j + h, q], put)
+                if q == 0:
+                    shared[sub * j : sub * j + sub] = part
+                else:
+                    shared[sub * j : sub * j + sub] += part
+
+
+def gather_stage(wfinal, wofinal, dgu, sfin, sdfin, ddn, hidden_dev):
+    width = wofinal.shape[3]
+    shard = wfinal.shape[1]
+    units = NZ * hidden_dev
+    f32 = jnp.float32
+    shape = jax.ShapeDtypeStruct
     vmem = pl.BlockSpec(memory_space=pltpu.VMEM)
-    f32, bf16 = jnp.float32, jnp.bfloat16
-    shape = jax.ShapeDtypeStruct
+    square = shape((shard, width), f32)
     return pl.pallas_call(
-        backward_kernel,
-        name="backward",
+        gather_kernel,
+        name="assemble",
         out_shape=[
-            shape((length, width), bf16), shape((32, width), f32), shape((shard, width), f32),
-            shape((shard, width), f32), shape((shard, width), f32), shape((shard, width), f32),
+            square, square, square, square, shape((shard, units), f32), shape((shard, units), f32),
+            shape((hidden_dev, width), f32), shape((2, shard, units), f32), shape((2, shard, units), f32),
+            shape((2, hidden_dev, width), f32),
         ],
-        in_specs=[vmem] * len(operands),
-        out_specs=[vmem] * 6,
-        scratch_shapes=[
-            pltpu.VMEM((length, width), bf16), pltpu.VMEM((8, length, width), bf16), pltpu.VMEM((count, 256), bf16),
-            pltpu.VMEM((2, count, 128), f32), pltpu.VMEM((2, count, 128), f32), pltpu.VMEM((count, 768), bf16),
-            pltpu.VMEM((width, 768), bf16), pltpu.VMEM((3, shard, 768), bf16), pltpu.VMEM((shard, 768), bf16),
-            pltpu.VMEM((8, shard, 768), bf16), pltpu.VMEM((256, width), f32), pltpu.VMEM((4, 3, 64, width), bf16),
-            pltpu.VMEM((4, 64, width), bf16), pltpu.VMEM((8, 4, 64, width), bf16), pltpu.VMEM((10, 32, width), f32),
-        ]
-        + spread_sems(1) + spread_sems(1)
-        + [
-            dma((3,)), dma((3,)), dma((4,)), dma((4, 3)), dma((4, 3)), dma((4, 3)), dma((4, 4)), dma((4, 4)),
-            dma((10,)), dma((10,)),
-        ]
-        + plane_scratch(length, width),
-        compiler_params=pltpu.CompilerParams(
-            collective_id=3, has_side_effects=True, vmem_limit_bytes=60 * MIB
-        ),
-    )(*operands)
+        in_specs=[vmem] * 6,
+        out_specs=[vmem] * 10,
+        compiler_params=pltpu.CompilerParams(vmem_limit_bytes=60 * MIB),
+    )(wfinal, wofinal, dgu, sfin, sdfin, ddn)
 
 
 def per_device_fast(
@@ -1149,71 +1439,35 @@
     capacity = 9 * length * TOPK // (8 * experts)
     shard = query_weight.shape[0]
     hidden_dev = expert_gate.shape[2] // NZ
-    cosine, sine = rotary_tables(jnp.arange(row_length, dtype=jnp.int32), HEAD_DIM // 2)
-    cosine, sine = cosine[:, 0], sine[:, 0]
-    cosine_wide = jnp.concatenate([cosine, cosine], axis=1)
-    sine_wide = jnp.concatenate([-sine, sine], axis=1)
-    small = jnp.concatenate(
-        [router_weight.T, feedforward_gain[None], attention_gain[None], jnp.zeros((14, shard), bf16)], axis=0
-    )
-    packed = lax.dynamic_update_slice(jnp.zeros((32, NZ * shard), bf16), small, (0, z * shard))
-    docs = jnp.concatenate([documents.astype(f32), jnp.ones((7, length), f32)], axis=0)
-
-    def slices(weights):
-        parts = weights.reshape(weights.shape[0], weights.shape[1], NZ, hidden_dev)
-        parts = jnp.pad(parts, ((0, 0), (0, 0), (0, 0), (0, WIDE - hidden_dev)))
-        return jnp.transpose(parts, (2, 0, 1, 3))
-
-    wsend = jnp.concatenate(
-        [
-            jnp.concatenate([slices(expert_gate), slices(shared_gate[None])], axis=1),
-            jnp.concatenate([slices(expert_up), slices(shared_up[None])], axis=1),
-        ],
-        axis=3,
-    )
-    wdn = jnp.pad(
-        jnp.concatenate([expert_down, shared_down[None]], axis=0), ((0, 0), (0, WIDE - hidden_dev), (0, 0))
-    )
-    front = attention_stage(
-        capacity, tokens[0], packed, docs, routes[0], priority[0], cosine_wide, sine_wide, cotangent[0],
-        query_weight, key_weight, value_weight, output_weight, wsend,
-    )
-    hidden, moe_input, table, gates, packed_sum, bound = front[:6]
-    kept = front[6:20]
-    (routed, grad_moe, grad_table, gu_back, grad_down, shared_gu, shared_dn) = expert_stage(
-        moe_input, table, front[20], front[21], wdn
-    )[:7]
-    output_rows = (hidden + routed).astype(bf16)
-
-    def joined(parts, at):
-        return jnp.concatenate([parts[i][..., at : at + hidden_dev] for i in range(NZ)], axis=-1).astype(f32)
-
-    shared_sum = lax.psum(shared_gu.astype(bf16), "ctx")
-    shared_down_sum = lax.psum(shared_dn[:hidden_dev].astype(bf16), "ctx")
-    grad_tokens, small, grad_wq, grad_wk, grad_wv, grad_wo = backward_stage(
-        grad_moe, grad_table, cotangent[0], tokens[0], hidden, moe_input, gates, packed_sum, bound, cosine_wide,
-        sine_wide, *kept
-    )
-    shared_back = lax.all_to_all(
-        shared_sum.reshape(NZ, shard, 2 * WIDE), "fsdp", split_axis=0, concat_axis=0, tiled=True
+    frequency = theta_base ** (-np.arange(HEAD_DIM // 2, dtype=np.float32) / (HEAD_DIM // 2))
+    angles = np.arange(row_length, dtype=np.float32)[:, None] * frequency.astype(np.float32)[None, :]
+    cosine, sine = np.cos(angles), np.sin(angles)
+    cosine_wide = jnp.asarray(np.concatenate([cosine, cosine], axis=1), f32)
+    sine_wide = jnp.asarray(np.concatenate([-sine, sine], axis=1), f32)
+    gains = jnp.concatenate([feedforward_gain[None], attention_gain[None], jnp.zeros((14, shard), bf16)], axis=0)
+    front = dict(
+        zip(
+            FRONT_OUT,
+            front_stage(
+                capacity, tokens[0], router_weight, gains, documents, routes[0], priority[0], cosine_wide, sine_wide,
+                cotangent[0], query_weight, key_weight, value_weight, output_weight, expert_gate, expert_up,
+                shared_gate, shared_up, expert_down, shared_down,
+            ),
+        )
+    )
+    kept = FRONT_OUT[5:19]
+    output_rows, grad_tokens, small, wfinal, wofinal, dgu, sfin, sdfin = backward_stage(
+        *[front[n] for n in ("ypart", "accout", "dsgu", "dsdn", "db", "dg")], cotangent[0], tokens[0],
+        *[front[n] for n in ("hidden", "tokens", "gates", "psum", "bound")], cosine_wide, sine_wide,
+        *[front[n] for n in kept]
+    )[:8]
+    gwq, gwk, gwv, gwo, gsg, gsu, gsd, geg, geu, ged = gather_stage(
+        wfinal, wofinal, dgu, sfin, sdfin, front["ddn"], hidden_dev
     )
     mine = lax.dynamic_slice_in_dim(small, z * shard, shard, 1)
     return (
-        output_rows[None],
-        grad_tokens[None],
-        mine[17],
-        grad_wq,
-        grad_wk,
-        grad_wv,
-        grad_wo,
-        mine[16],
-        mine[:16].T,
-        joined(shared_back, 0),
-        joined(shared_back, WIDE),
-        shared_down_sum.astype(f32),
-        joined(gu_back, 0),
-        joined(gu_back, WIDE),
-        grad_down[:, :hidden_dev],
+        output_rows[None], grad_tokens[None], mine[17], gwq, gwk, gwv, gwo, mine[16], mine[:16].T, gsg, gsu, gsd, geg,
+        geu, ged,
     )
 
 

time: 901 us -> 537 us (0.60)
  Pallas kernels: 751 us -> 521 us
  waiting for transfers between devices: 60.4 us -> 0 us
  local copies, waits for them, and re-layouts: 43.9 us -> 8.67 us
  other arithmetic: 20 us -> 0.68 us
  between operations: 14.6 us -> 0.87 us
    pallas_call x2, Pallas kernels: 598 us -> 326 us  [the longest x1 311 us: front_stage(): pl.pallas_call(functools.partial(front_kernel, capacity), name='front', o...]
    psum x1 -> x0, waiting for transfers between devices: 60.4 us -> none  [per_device_fast(): shared_sum = lax.psum(shared_gu.astype(bf16), 'ctx')]
    pallas_call x1, Pallas kernels: 153 us -> 195 us  [backward_stage(): pl.pallas_call(backward_kernel, name='backward', out_shape=[shape((length...]
    convert_element_type x8 -> x0, other arithmetic: 10.2 us -> none  [the longest x4 6.19 us: joined(): jnp.concatenate([parts[i][..., at:at + hidden_dev] for i in range(NZ)], a...]
    reshape x4 -> x0, local copies, waits for them, and re-layouts: 9.51 us -> none  [slices(): parts = weights.reshape(weights.shape[0], weights.shape[1], NZ, hidden_dev)]
  transfers between devices with their start and end apart: 2 -> 0, of which waited for: 1 -> 0; matrix products, arithmetic and copies ran while one was open for 2% -> 0% of each run, Pallas kernels for 17% -> 0%
where the time goes in v3:
time: 537 us; the launch traced here: 531 us
  Pallas kernels  521 us (97%)
  local copies, waits for them, and re-layouts  8.67 us (2%)
    pallas_call x1, Pallas kernels, front_stage(): pl.pallas_call(functools.partial(front_kernel, capacity), name='front', o...  311 us
    pallas_call x1, Pallas kernels, backward_stage(): pl.pallas_call(backward_kernel, name='backward', out_shape=[shape((length...  195 us
    pallas_call x1, Pallas kernels, gather_stage(): pl.pallas_call(gather_kernel, name='assemble', out_shape=[square, square,...  14.7 us

profile of v3, /device:TPU:21, one launch (start us, length us, event | category | flops | bytes accessed | tf_op | source)
XLA Modules:
  0.0 531.4 jit_solution(15692913707407452500)
XLA Ops:
  0.6 1.4 copy.36.refs_1_
  2.1 1.4 copy.35
  3.5 0.7 broadcast_in_dim.15
  4.2 0.7 broadcast_in_dim.16
  4.9 0.1 pad.2.clone
  5.0 0.7 maximum_maximum_fusion.refs_2_
  5.6 311.0 %front.1 = (f32[128,1280]{1,0:T(8,128)}, bf16[128,1280]{1,0:T(8,128)(2,1)}, f32[16,128]{1,0:T(8,128)}, f32[32,1280]{1,0:T(8,128)}, f32[8,128]{1,0:T(8,128)}, /*i...) custom-call(bf16[128,1280]{1,0:T(8,128)(2,1)} %bitcast.8, ...), custom_call_target="tpu_custom_call" | custom-call | tf_op jit(solution)/shard_map/front/pallas_call | solution.py:882
  316.7 195.5 %backward.1 = (bf16[128,1280]{1,0:T(8,128)(2,1)}, bf16[128,1280]{1,0:T(8,128)(2,1)}, f32[32,1280]{1,0:T(8,128)}, bf16[8,320,768]{2,1,0:T(8,128)(2,1)}, bf16[8,4,...) custom-call(bf16[4,512,1280]{2,1,0:T(8,128)(2,1)} %get-tuple-element, ...), custom_call_target="tpu_custom_call" | custom-call | tf_op jit(solution)/shard_map/backward/pallas_call | solution.py:1297
  512.1 0.0 copy-start.1
  512.2 0.0 copy-start
  512.2 14.7 %assemble.1 = (f32[320,1280]{1,0:T(8,128)}, f32[320,1280]{1,0:T(8,128)}, f32[320,1280]{1,0:T(8,128)}, f32[320,1280]{1,0:T(8,128)}, f32[320,896]{1,0:T(8,128)}, /...) custom-call(bf16[8,320,768]{2,1,0:T(8,128)(2,1)} %get-tuple-element., ...), custom_call_target="tpu_custom_call" | custom-call | tf_op jit(solution)/shard_map/assemble/pallas_call | solution.py:1400
  526.9 1.4 dynamic-slice_bitcast_fusion
  528.3 1.5 dynamic-slice_reduce_fusion
  529.8 0.0 copy-done.1
  529.8 0.7 copy.39
  530.5 0.0 copy-done
  530.5 0.7 copy.40
  (1 shorter events, 0.0 us)
Async XLA Ops:
  512.1 17.7 %copy-start.1 = (bf16[128,1280]{1,0:T(8,128)(2,1)S(1)}, bf16[128,1280]{1,0:T(8,128)(2,1)}, u32[]{:S(2)}) copy-start(bf16[128,1280]{1,0:T(8,128)(2,1)} %get-tuple-element.84) | copy-start | bytes 983044
  512.2 18.4 %copy-start = (bf16[128,1280]{1,0:T(8,128)(2,1)S(1)}, bf16[128,1280]{1,0:T(8,128)(2,1)}, u32[]{:S(2)}) copy-start(bf16[128,1280]{1,0:T(8,128)(2,1)} %get-tuple-element.85) | copy-start | bytes 983044

commit v4 on v3

--- a/solution.py
+++ b/solution.py
@@ -123,29 +123,65 @@
 
 
 class Spread:
-    def __init__(self, src, block, sems, c, z, hops=NZ, peers=PEERS, copy_own=True):
+    def __init__(self, src, block, sems, c, z, hops=NZ, peers=PEERS, copy_own=True, plane=None, chain=False, relays=True):
         self.src, self.block, self.c, self.z = src, block, c, z
         self.hops, self.peers, self.all = hops, peers, ((0, 0),) + peers
         self.local, self.zs, self.zr, self.xs, self.xr, self.ms, self.mr = sems
-        self.forwards = hops == NZ and len(peers) == 3
+        self.plane = plane is not None
+        self.chain, self.relays = chain, relays
+        self.forwards = (hops == NZ or self.plane) and len(peers) == 3
+        self.zhops = 1 if self.plane else hops
         self.direct = 2 if self.forwards else len(peers)
-        self.own = pltpu.make_async_copy(src(z), block(c, z), self.local) if copy_own else None
+        pair = plane if self.plane else (src(z), block(c, z)) if copy_own else None
+        self.own = pltpu.make_async_copy(*pair, self.local) if pair is not None else None
 
     def at(self, c, d):
-        return self.block(c, (self.z + NZ - d) % NZ)
+        return self.block(c, d if self.plane else (self.z + NZ - d) % NZ)
 
     def mine(self, c, d):
+        if self.plane:
+            return self.src(d)
         return self.src(self.z) if d == 0 else self.at(c, d)
 
     def zcopy(self, d):
         there = (self.z + d) % NZ
         return remote(
-            self.src(there), self.block(self.c, self.z), self.zs.at[d - 1], self.zr.at[d - 1], self.c, there
+            self.src(there), self.block(self.c, self.z), self.zs.at[0, d - 1], self.zr.at[d - 1], self.c, there
         )
+
+    def hop(self, up, k):
+        origin = self.z - k if up else self.z + k
+        there = self.z + 1 if up else self.z - 1
+        block = self.block(self.c, origin)
+        src = self.src(self.z) if k == 0 else block
+        return remote(src, block, self.zs.at[int(up), k], self.zr.at[k if up else 2 - k], self.c, there)
+
+    def hops_of(self, k):
+        return (True, (self.z >= k) & (self.z < NZ - 1)), (False, (self.z + k < NZ) & (self.z > 0))
+
+    def onward(self, d):
+        if self.relays:
+            for i in range(self.direct):
+                self.xcopy(i, d).start()
+            self.mcopy(0, d).start()
+
+    def chain_stage(self, k):
+        for up, here, d in ((True, self.z >= k, k), (False, self.z + k < NZ, NZ - k)):
+
+            @pl.when(here)
+            def _(up=up, d=d):
+                self.zwait(d)
+                if k < NZ - 1:
+
+                    @pl.when((self.z < NZ - 1) if up else (self.z > 0))
+                    def _():
+                        self.hop(up, k).start()
+
+                self.onward(d)
 
     def zwait(self, d):
         block = self.at(self.c, d)
-        remote(block, block, self.zs.at[d - 1], self.zr.at[d - 1], self.c, self.z).wait_recv()
+        remote(block, block, self.zs.at[0, d - 1], self.zr.at[d - 1], self.c, self.z).wait_recv()
 
     def xcopy(self, i, d):
         there = flip(self.c, self.peers[i][0], self.peers[i][1], 0)
@@ -173,20 +209,26 @@
     def start_z(self):
         if self.own is not None:
             self.own.start()
-        for d in range(1, self.hops):
+        if self.chain:
+            for up, edge in self.hops_of(0):
+                pl.when(edge)(self.hop(up, 0).start)
+            return
+        for d in range(1, self.zhops):
             self.zcopy(d).start()
 
     def start_x(self):
-        for i in range(self.direct):
-            self.xcopy(i, 0).start()
-        self.mcopy(0, 0).start()
-
-    def relay_z(self):
-        for d in range(1, self.hops):
-            self.zwait(d)
+        for d in range(self.hops if self.plane else 1):
             for i in range(self.direct):
                 self.xcopy(i, d).start()
             self.mcopy(0, d).start()
+
+    def relay_z(self):
+        for d in range(1, self.zhops):
+            if self.chain:
+                self.chain_stage(d)
+            else:
+                self.zwait(d)
+                self.onward(d)
 
     def relay_x(self):
         for d in range(self.hops):
@@ -197,7 +239,7 @@
         for i in range(min(2, len(self.peers))):
             self.xwait(i, d)
             self.mcopy(i + 1, d).start()
-            if self.forwards and i == (d >= 2):
+            if self.forwards and i == (d >= self.hops // 2):
                 self.fcopy(i, d).start()
 
     def relay_far(self):
@@ -217,21 +259,36 @@
                 self.mwait(i, d)
 
     def drain(self):
-        for d in range(1, self.hops):
-            self.zcopy(d).wait_send()
+        for d in range(1, self.zhops):
+            if self.chain:
+                for up, edge in self.hops_of(d - 1):
+                    pl.when(edge)(self.hop(up, d - 1).wait_send)
+            else:
+                self.zcopy(d).wait_send()
+        if not self.relays:
+            return
         for d in range(self.hops):
             for i in range(self.direct):
                 self.xcopy(i, d).wait_send()
             if self.forwards:
-                self.fcopy(int(d >= 2), d).wait_send()
+                self.fcopy(int(d >= self.hops // 2), d).wait_send()
             for i in range(len(self.all)):
                 self.mcopy(i, d).wait_send()
+
+
+def halves(src, dst, sems, c, z):
+    count = src.shape[0] // 2
+    return Spread(
+        lambda d: src.at[d * count : (d + 1) * count],
+        lambda o, d: dst(o).at[d * count : (d + 1) * count],
+        sems, c, z, 2, plane=(src, dst(c)),
+    )
 
 
 def spread_sems(hops=NZ, peers=3):
     dma = pltpu.SemaphoreType.DMA
     return [
-        dma, dma((3,)), dma((3,)), dma((peers, hops)), dma((peers, hops)), dma((peers + 1, hops)), dma((peers + 1, hops)),
+        dma, dma((2, 3)), dma((3,)), dma((peers, hops)), dma((peers, hops)), dma((peers + 1, hops)), dma((peers + 1, hops)),
     ]
 
 
@@ -342,17 +399,20 @@
     )
     spread_docs = Spread(lambda _: r.docs.at[8], lambda o, _: r.docs.at[o], take(sems, 7), c, z, 1)
     second = lambda o, s: r.wall.at[rows_at(s * shard + (o % 4) * sub, sub), 384:768]
-    spread_h2 = Spread(lambda _: second(c, z), second, take(sems, 7), c, z, NZ, ((0, 1),), False)
+    spread_h2 = Spread(lambda _: second(c, z), second, take(sems, 7), c, z, NZ, ((0, 1),), False, chain=True)
+    first = lambda _, s: r.wall.at[rows_at(s * shard, shard), 0:384]
+    spread_h1 = Spread(lambda _: first(c, z), first, take(sems, 7), c, z, copy_own=False, chain=True, relays=False)
     spread_g = Spread(lambda _: r.g, lambda o, s: r.gall.at[o, rows_at(s * length, length)], take(sems, 7), c, z)
     shared_in = lambda s: r.wsend.at[s, 2, rows_at((c // 2) * sub, sub), lanes_at(c % 2 * WIDE, WIDE)]
     shared_to = lambda o, s: r.wgu.at[2, rows_at(s * shard + (o // 2) * sub, sub), lanes_at(o % 2 * WIDE, WIDE)]
     spread_s = Spread(shared_in, shared_to, take(sems, 7), c, z)
-    spread_b = Spread(lambda _: r.tokens, lambda o, s: r.ball.at[o, rows_at(s * length, length)], take(sems, 7), c, z)
+    spread_b = Spread(lambda _: r.tokens, lambda o, s: r.ball.at[o, rows_at(s * length, length)], take(sems, 7), c, z, chain=True)
     spread_t = Spread(lambda _: r.table, lambda o, s: r.tall.at[o, s], take(sems, 7), c, z)
-    ps, pr, wl, w1s, w1r, wol, wos, wor, wgl, wgs, wgr, rawsem, cutsem, dnsem, acsem = take(sems, 15)
+    ps, pr, wl, wol, wos, wor, wgl, wgs, wgr, rawsem, cutsem, dnsem, acsem = take(sems, 13)
     lsem, ms, mr, xs_s, xs_r, zs, zr, ysem, accsem = take(sems, 9)
     reduce_refs = [r.ys, r.ds, r.zbuf.at[0:3, 0:length]] + take(sems, 5)
 
+    r.pall[...] = jnp.zeros_like(r.pall)
     greet(c, z)
     own_rows = rows_at(z * shard, shard)
     sub_rows = rows_at(z * shard + quarter * sub, sub)
@@ -398,26 +458,22 @@
     r.pown[16:32] = dot(r.gains[...], place).astype(bf16)
 
     def pcopy(d):
-        return remote(r.pown, r.pall.at[d - 1], ps.at[d - 1], pr.at[d - 1], c, (z + d) % NZ)
+        lanes = lanes_at(5 * z // 2 * 128, 384)
+        return remote(
+            r.pown.at[:, lanes], r.pall.at[d - 1, :, lanes], ps.at[d - 1], pr.at[d - 1], c, (z + d) % NZ
+        )
+
+    def pwait(d):
+        here = r.pall.at[d - 1, :, lanes_at(5 * ((z + NZ - d) % NZ) // 2 * 128, 384)]
+        remote(here, here, ps.at[d - 1], pr.at[d - 1], c, z).wait_recv()
 
     for d in range(1, NZ):
         pcopy(d).start()
-    spread_g.start_z()
     for copy in copies:
         copy.wait()
 
-    def h1copy(d):
-        return remote(
-            r.wall.at[own_rows, 0:384], r.wall.at[own_rows, 0:384], w1s.at[d - 1], w1r.at[d - 1], c, (z + d) % NZ
-        )
-
-    def h1wait(d):
-        here = r.wall.at[rows_at((z + NZ - d) % NZ * shard, shard), 0:384]
-        remote(here, here, w1s.at[d - 1], w1r.at[d - 1], c, z).wait_recv()
-
     spread_h2.start_z()
-    for d in range(1, NZ):
-        h1copy(d).start()
+    spread_h1.start_z()
     spread_h2.start_x()
     def wo_local(j, b):
         return pltpu.make_async_copy(
@@ -473,12 +529,13 @@
             wo_hop(j, False, b, False).wait_send()
 
     wo_each(wo_start)
+    spread_g.start_z()
+    spread_g.start_x()
     r.docs[8] = jnp.concatenate([r.doc[...].astype(f32), jnp.ones((7, length), f32)], axis=0)
     spread_docs.start_z()
     spread_docs.start_x()
     spread_x.relay_x()
     spread_docs.relay_x()
-    spread_g.start_x()
 
     for e in range(3):
         for copy in load_raw(e):
@@ -495,10 +552,9 @@
         if e < 2:
             for copy in load_raw(e + 1):
                 copy.start()
-    spread_g.relay_z()
     packed = r.pown[...].astype(f32)
     for d in range(1, NZ):
-        pcopy(d).wait_recv()
+        pwait(d)
         packed = packed + r.pall[d - 1].astype(f32)
     r.psum[...] = packed
     gain_one = packed[17:18]
@@ -511,13 +567,11 @@
         return carry
 
     lax.fori_loop(0, 8, make_a, 0)
-    for d in range(2):
-        spread_g.relay_near(d)
-    spread_h2.relay_z()
+    for d in range(1, NZ):
+        spread_h2.chain_stage(d)
+        spread_h1.chain_stage(d)
     spread_h2.relay_x()
     spread_h2.arrive()
-    for d in range(1, NZ):
-        h1wait(d)
     wo_each(wo_relay)
 
     def wgcopy(e, d):
@@ -547,8 +601,6 @@
         r.q2[part] = turned(values[:, 384:512], cosine, sine).astype(bf16)
         r.k2[part] = turned(values[:, 512:640], cosine, sine).astype(bf16)
         r.v2[part] = values[:, 640:768].astype(bf16)
-    for d in range(2, NZ):
-        spread_g.relay_near(d)
     acopy = pltpu.make_async_copy(r.bg, r.aall, acsem)
     acopy.start()
     spread_docs.arrive()
@@ -572,8 +624,8 @@
         r.att1[part] = out
         r.lse1[part] = lse
         r.mixed[part, 0:128] = out.astype(bf16)
-        if i == 1:
-            spread_g.relay_far()
+        if i == 2:
+            spread_g.relay_z()
     mine = rows_at(quarter * step, step)
     out, lse = attend(r.q2[mine], quarter * step, r.k2, r.v2, count)
     r.att2[...] = out
@@ -607,8 +659,6 @@
     spread_b.start_x()
     spread_t.start_z()
     spread_t.start_x()
-    for d in range(1, NZ):
-        wgcopy(1, d).start()
     r.acc[...] = jnp.zeros_like(r.acc)
     r.ddn[...] = jnp.zeros_like(r.ddn)
     r.st[group:final] = jnp.zeros((16, width), bf16)
@@ -617,13 +667,19 @@
         copy.wait()
     r.wdn[:, hidden_dev:] = jnp.zeros((3, WIDE - hidden_dev, width), bf16)
     for d in range(NZ):
-        spread_s.relay_near(d)
-    spread_s.relay_far()
-    spread_b.relay_z()
+        spread_g.relay_near(d)
+    for d in range(1, NZ):
+        spread_b.chain_stage(d)
+    for d in range(1, NZ):
+        wgcopy(1, d).start()
     spread_t.relay_z()
     for d in range(NZ):
         spread_b.relay_near(d)
         spread_t.relay_near(d)
+    for d in range(NZ):
+        spread_s.relay_near(d)
+    spread_g.relay_far()
+    spread_s.relay_far()
     spread_b.relay_far()
     spread_t.relay_far()
     spread_s.arrive()
@@ -859,9 +915,8 @@
         zsmall(d).wait_send()
         wgcopy(0, d).wait_send()
         wgcopy(1, d).wait_send()
-        h1copy(d).wait_send()
         pcopy(d).wait_send()
-    for spread in (spread_docs, spread_h2, spread_g, spread_s, spread_b, spread_t):
+    for spread in (spread_docs, spread_h1, spread_h2, spread_g, spread_s, spread_b, spread_t):
         spread.drain()
 
 
@@ -908,10 +963,10 @@
             pltpu.VMEM((3, final, width), bf16), pltpu.VMEM((NZ, length + 16, width), bf16),
             pltpu.VMEM((3, length + 16, width), bf16),
         ]
-        + spread_sems(1) + spread_sems(1) + spread_sems(NZ, 1) + spread_sems() + spread_sems() + spread_sems()
+        + spread_sems(1) + spread_sems(1) + spread_sems(NZ, 1) + spread_sems() + spread_sems() + spread_sems() + spread_sems()
         + spread_sems()
         + [
-            dma((3,)), dma((3,)), dma((6,)), dma((3,)), dma((3,)), dma((4,)), dma((4, 2)), dma((4,)),
+            dma((3,)), dma((3,)), dma((6,)), dma((4,)), dma((4, 2)), dma((4,)),
             dma, dma((2, 3)), dma((2, 3)), dma((2,)), dma, dma((3,)), dma,
             dma((2, 3)), dma((4,)), dma((4,)), dma((3, NZ + 1)), dma((3, NZ + 1)), dma((3, 2)), dma((3, 2)), dma, dma,
         ]
@@ -925,9 +980,9 @@
 def backward_kernel(
     ypart, accout, dsgu, dsdn, db_ref, dg_ref, g_ref, x_ref, hidden_ref, b_ref, gates_ref, psum_ref, bound_ref, cos_ref, sin_ref,
     aall, wall, woall, q1, k1, v1, q2, k2, v2, att1, lse1, att2, lse2, mixed,
-    out_ref, gtok_ref, small_ref, wfinal, wofinal, dgu, sfin, sdfin, yrecv,
+    out_ref, gtok_ref, small_ref, wfinal, wfinal2, wofinal, dgu, sfin, sdfin, yrecv,
     dhb, dhall, dm, dk, dv, cat, wst, wrecv, wsum, dwo, worecv, wosum, small4,
-    sgm, sdm, sgs, sds, sgx, sdx, sgt, sgz, sdt, ybuf, ysend, yz, *sems,
+    sgm, sdm, sgs, sds, sgx, sdx, sgt, sgz, sdt, ybuf, ysend, yz, yhalf, yadd, wm, wpair, wrecv2, wsum2, *sems,
 ):
     f32, bf16 = jnp.float32, jnp.bfloat16
     c = lax.axis_index("ctx")
@@ -940,25 +995,40 @@
     scale = HEAD_DIM**-0.5
     sems = list(sems)
 
-    spread_h = Spread(lambda _: dhb, lambda o, _: dhall.at[o], take(sems, 7), c, z, 1)
-    spread_w = Spread(lambda _: wsum, lambda o, _: wfinal.at[o], take(sems, 7), c, z, 1)
-    wzs, wzr, ozs, ozr, oxs, oxr, oms, omr, ss, sr = take(sems, 10)
-    yxs, yxr, yzs, yzr, gas, gar, gal, sms, smr, sxs, sxr, szs, szr, ylsem, olsem = take(sems, 15)
-    spread_s = Spread(lambda _: sgz, lambda o, _: sfin.at[o], take(sems, 7), c, z, 1)
-    spread_d = Spread(lambda _: sdt, lambda o, _: sdfin.at[o], take(sems, 7), c, z, 1)
+    spread_h = halves(dhb, lambda o: dhall.at[o], take(sems, 7), c, z)
+    spread_w = halves(wsum, lambda o: wfinal.at[o], take(sems, 7), c, z)
+    spread_v = halves(wsum2, lambda o: wfinal2.at[o], take(sems, 7), c, z)
+    wzs, wzr, wms, wmr, ozs, ozr, oxs, oxr, oms, omr, ss, sr = take(sems, 12)
+    yxs, yxr, yzs, yzr, gas, gar, gal, sms, smr, sxs, sxr, szs, szr, ylsem, olsem, yasem = take(sems, 16)
+    spread_s = halves(sgz, lambda o: sfin.at[o], take(sems, 7), c, z)
+    spread_d = halves(sdt, lambda o: sdfin.at[o], take(sems, 7), c, z)
     reduce_refs = take(sems, 8)
     core = c % 2
     chip = c // 2
     sub = shard // 4
     part_rows = sdt.shape[0]
 
+    half = ypart.shape[1] // 2
+    upper, lower = slice(0, half), slice(half, 2 * half)
+    x_chip, y_chip = flip(c, 0, 1, 0), flip(c, 1, 0, 0)
+
     def ycopy(i):
-        return remote(
-            ypart.at[(1, 2, 0)[i]], yrecv.at[i], yxs.at[i], yxr.at[i], flip(c, PEERS[i][0], PEERS[i][1], 0), z
-        )
+        src, dst, there = (
+            (ypart.at[0, upper], yhalf.at[0], x_chip),
+            (ypart.at[0, lower], yhalf.at[1], y_chip),
+            (ypart.at[1, upper], yrecv.at[0, upper], x_chip),
+            (ypart.at[2, lower], yrecv.at[1, lower], y_chip),
+            (yadd.at[0], yrecv.at[1, upper], y_chip),
+            (yadd.at[1], yrecv.at[0, lower], x_chip),
+        )[i]
+        return remote(src, dst, yxs.at[i], yxr.at[i], there, z)
+
+    def ytake(i):
+        src = (ypart.at[2, upper], ypart.at[1, lower])[i]
+        return pltpu.make_async_copy(src, yadd.at[i], yasem.at[i])
 
     def yload(i):
-        src = ypart.at[3] if i == 3 else yrecv.at[i]
+        src = ypart.at[3] if i == 2 else yrecv.at[i]
         return pltpu.make_async_copy(src, ybuf.at[i], ylsem.at[i])
 
     def yhop(d):
@@ -1017,8 +1087,10 @@
     dv[...] = jnp.zeros_like(dv)
     cat[:, 384:512] = jnp.zeros((count, 128), bf16)
     spread_h.relay_x()
-    for i in range(3):
+    for i in range(4):
         ycopy(i).start()
+    for i in range(2):
+        ytake(i).start()
     spread_h.arrive()
     step = 2 * length
     for i in range(count // step):
@@ -1044,6 +1116,17 @@
         def _(j=j, owner=owner):
             oz(j, owner).start()
 
+    for i in range(2):
+        ycopy(i).wait_recv()
+        ytake(i).wait()
+
+        def yjoin(n, carry):
+            part = rows_at(n * 16, 16)
+            yadd[i, part] = (yadd[i, part].astype(f32) + yhalf[i, part].astype(f32)).astype(bf16)
+            return carry
+
+        lax.fori_loop(0, half // 16, yjoin, 0)
+        ycopy(4 + i).start()
     smate(0).wait_recv()
     smate(1).wait_recv()
     for q in range(NZ):
@@ -1084,14 +1167,26 @@
     for i in range(width // 256):
         wst[256 * i : 256 * i + 256] = dot(aall[:, 256 * i : 256 * i + 256], cat[...], TN).astype(bf16)
 
-    def wz(d):
+    def wz(d, second):
         there = (z + d) % NZ
-        return remote(
-            wst.at[rows_at(there * shard, shard)], wrecv.at[d - 1], wzs.at[d - 1], wzr.at[d - 1], c, there
-        )
-
+        src = wpair.at[there] if second else wst.at[rows_at(there * shard, shard), 0:384]
+        dst = wrecv2 if second else wrecv
+        return remote(src, dst.at[d - 1], wzs.at[d - 1, second], wzr.at[d - 1, second], c, there)
+
+    def wmate(q):
+        rows = rows_at(q * shard + (1 - core) * (shard // 2), shard // 2)
+        return remote(wst.at[rows, 384:768], wm.at[q], wms.at[q], wmr.at[q], mate, z)
+
+    for q in range(NZ):
+        wmate(q).start()
     for d in range(1, NZ):
-        wz(d).start()
+        wz(d, 0).start()
+    for q in range(NZ):
+        wmate(q).wait_recv()
+        own = wst[rows_at(q * shard + core * (shard // 2), shard // 2), 384:768].astype(f32)
+        wpair[q] = (own + wm[q].astype(f32)).astype(bf16)
+    for d in range(1, NZ):
+        wz(d, 1).start()
 
     total_up = [sgs[q, chip].astype(f32) for q in range(NZ)]
     total_down = sds[chip].astype(f32)
@@ -1171,35 +1266,54 @@
     value, more = exchange(2, (3, 4, 5), [(flip(c, fy, fx, 0), z) for fy, fx in PEERS])
     sent += more
     small4[6] = value
+    window = lambda s: lanes_at(5 * s // 2 * 128, 384)
     last_hop = [
-        remote(small4.at[6], small4.at[6 + d], ss.at[6 + d], sr.at[6 + d], c, (z + d) % NZ) for d in range(1, NZ)
+        remote(
+            small4.at[6, :, window((z + d) % NZ)], small4.at[6 + d, :, window((z + d) % NZ)],
+            ss.at[6 + d], sr.at[6 + d], c, (z + d) % NZ,
+        )
+        for d in range(1, NZ)
+    ]
+    last_wait = [
+        remote(
+            small4.at[6 + d, :, window(z)], small4.at[6 + d, :, window(z)], ss.at[6 + d], sr.at[6 + d], c, z
+        )
+        for d in range(1, NZ)
     ]
     for copy in last_hop:
         copy.start()
-    for i in range(3):
-        ycopy(i).wait_recv()
+    yload(2).start()
+    for i in range(2):
+        ycopy(2 + i).wait_recv()
+        ycopy(5 - i).wait_recv()
         yload(i).start()
-    yload(3).start()
     for d in range(1, NZ):
         shop_wait = sgz.at[(z + NZ - d) % NZ]
         remote(shop_wait, shop_wait, szs.at[d - 1], szr.at[d - 1], c, z).wait_recv()
     spread_s.start_z()
     spread_s.start_x()
-    total = wst[rows_at(z * shard, shard)].astype(f32)
+    total = wst[rows_at(z * shard, shard), 0:384].astype(f32)
     for d in range(1, NZ):
-        wz(d).wait_recv()
+        wz(d, 0).wait_recv()
         total = total + wrecv[d - 1].astype(f32)
     wsum[...] = total.astype(bf16)
     spread_w.start_z()
     spread_w.start_x()
-
-    for i in range(4):
+    total = wpair[z].astype(f32)
+    for d in range(1, NZ):
+        wz(d, 1).wait_recv()
+        total = total + wrecv2[d - 1].astype(f32)
+    wsum2[...] = total.astype(bf16)
+    spread_v.start_z()
+    spread_v.start_x()
+
+    for i in range(3):
         yload(i).wait()
 
     def ysum(i, carry):
         part = rows_at(i * 16, 16)
         value = ybuf[0, part].astype(f32)
-        for k in range(1, 4):
+        for k in range(1, 3):
             value = value + ybuf[k, part].astype(f32)
         ysend[i // (length // 16), rows_at(i % (length // 16) * 16, 16)] = value.astype(bf16)
         return carry
@@ -1219,6 +1333,7 @@
                 om(j, i + 1).start()
 
     spread_w.relay_x()
+    spread_v.relay_x()
     for i in range(4):
         fy, fx = (((0, 0),) + PEERS)[i]
         for j, (_, owner) in enumerate(head_rows(flip(c, fy, fx, 1))):
@@ -1228,11 +1343,11 @@
                 block = wofinal.at[flip(c, fy, fx, 1), j]
                 remote(block, block, oms.at[j, i], omr.at[j, i], c, z).wait_recv()
 
-    value = small4[6]
+    value = small4[6, :, window(z)]
     for d in range(1, NZ):
-        last_hop[d - 1].wait_recv()
-        value = value + small4[6 + d]
-    small_ref[...] = value
+        last_wait[d - 1].wait_recv()
+        value = value + small4[6 + d, :, window(z)]
+    small_ref[:, window(z)] = value
     spread_s.relay_x()
     spread_d.relay_x()
     value = hidden + ysend[z].astype(f32)
@@ -1241,6 +1356,7 @@
         value = value + yz[d - 1].astype(f32)
     out_ref[...] = value.astype(bf16)
     spread_w.arrive()
+    spread_v.arrive()
     spread_s.arrive()
     spread_d.arrive()
     gown.wait()
@@ -1248,8 +1364,9 @@
         gcopy(d).wait()
         yhop(d).wait_send()
         shop(d).wait_send()
+    for i in range(6):
+        ycopy(i).wait_send()
     for i in range(3):
-        ycopy(i).wait_send()
         schip(i, 0).wait_send()
         schip(i, 1).wait_send()
     smate(0).wait_send()
@@ -1277,8 +1394,11 @@
                 om(j, i + 1).wait_send()
 
     for d in range(1, NZ):
-        wz(d).wait_send()
-    for spread in (spread_h, spread_w, spread_s, spread_d):
+        wz(d, 0).wait_send()
+        wz(d, 1).wait_send()
+    for q in range(NZ):
+        wmate(q).wait_send()
+    for spread in (spread_h, spread_w, spread_v, spread_s, spread_d):
         spread.drain()
 
 
@@ -1299,32 +1419,35 @@
         name="backward",
         out_shape=[
             shape((length, width), bf16), shape((length, width), bf16), shape((32, width), f32),
-            shape((8, shard, 768), bf16), shape((8, 4, 64, width), bf16), shape((NZ, 2, shard, 2 * WIDE), bf16),
-            shape((8, NZ, sub, WIDE), bf16), shape((8, part_rows, width), bf16), shape((3, NZ * length, width), bf16),
+            shape((8, shard, 384), bf16), shape((8, shard // 2, 384), bf16), shape((8, 4, 64, width), bf16), shape((NZ, 2, shard, 2 * WIDE), bf16),
+            shape((8, NZ, sub, WIDE), bf16), shape((8, part_rows, width), bf16), shape((2, NZ * length, width), bf16),
         ],
         in_specs=[hbm] * 2 + [vmem] * (len(operands) - 2),
-        out_specs=[vmem] * 3 + [hbm] * 6,
+        out_specs=[vmem] * 3 + [hbm] * 7,
         scratch_shapes=[
             pltpu.VMEM((length, width), bf16), pltpu.VMEM((8, length, width), bf16), pltpu.VMEM((count, 256), bf16),
             pltpu.VMEM((2, count, 128), f32), pltpu.VMEM((2, count, 128), f32), pltpu.VMEM((count, 768), bf16),
-            pltpu.VMEM((width, 768), bf16), pltpu.VMEM((3, shard, 768), bf16), pltpu.VMEM((shard, 768), bf16),
+            pltpu.VMEM((width, 768), bf16), pltpu.VMEM((3, shard, 384), bf16), pltpu.VMEM((shard, 384), bf16),
             pltpu.VMEM((256, width), f32), pltpu.VMEM((4, 3, 64, width), bf16),
             pltpu.VMEM((4, 64, width), bf16), pltpu.VMEM((10, 32, width), f32),
             pltpu.VMEM((width, WIDE), bf16), pltpu.VMEM((4 * part_rows, width), bf16),
             pltpu.VMEM((NZ, 4, sub, WIDE), bf16), pltpu.VMEM((4, part_rows, width), bf16),
             pltpu.VMEM((3, NZ, sub, WIDE), bf16), pltpu.VMEM((3, part_rows, width), bf16),
             pltpu.VMEM((NZ, sub, WIDE), bf16), pltpu.VMEM((NZ, sub, WIDE), bf16), pltpu.VMEM((part_rows, width), bf16),
-            pltpu.VMEM((4, NZ * length, width), bf16), pltpu.VMEM((NZ, length, width), bf16),
-            pltpu.VMEM((3, length, width), bf16),
+            pltpu.VMEM((3, NZ * length, width), bf16), pltpu.VMEM((NZ, length, width), bf16),
+            pltpu.VMEM((3, length, width), bf16), pltpu.VMEM((2, 2 * length, width), bf16),
+            pltpu.VMEM((2, 2 * length, width), bf16), pltpu.VMEM((NZ, shard // 2, 384), bf16),
+            pltpu.VMEM((NZ, shard // 2, 384), bf16), pltpu.VMEM((3, shard // 2, 384), bf16),
+            pltpu.VMEM((shard // 2, 384), bf16),
         ]
-        + spread_sems(1) + spread_sems(1)
+        + spread_sems(2) + spread_sems(2) + spread_sems(2)
         + [
-            dma((3,)), dma((3,)), dma((4,)), dma((4, 3)), dma((4, 3)), dma((4, 3)), dma((4, 4)), dma((4, 4)),
+            dma((3, 2)), dma((3, 2)), dma((4,)), dma((4,)), dma((4,)), dma((4, 3)), dma((4, 3)), dma((4, 3)), dma((4, 4)), dma((4, 4)),
             dma((10,)), dma((10,)),
-            dma((3,)), dma((3,)), dma((3,)), dma((3,)), dma((3,)), dma((3,)), dma, dma((2,)), dma((2,)),
-            dma((3, 2)), dma((3, 2)), dma((3,)), dma((3,)), dma((4,)), dma((4,)),
+            dma((6,)), dma((6,)), dma((3,)), dma((3,)), dma((3,)), dma((3,)), dma, dma((2,)), dma((2,)),
+            dma((3, 2)), dma((3, 2)), dma((3,)), dma((3,)), dma((4,)), dma((4,)), dma((2,)),
         ]
-        + spread_sems(1) + spread_sems(1)
+        + spread_sems(2) + spread_sems(2)
         + plane_scratch(length, width),
         compiler_params=pltpu.CompilerParams(
             collective_id=3, has_side_effects=True, vmem_limit_bytes=62 * MIB
@@ -1333,35 +1456,14 @@
 
 
 def gather_kernel(
-    wfinal, wofinal, dgu, sfin, sdfin, ddn, gwq, gwk, gwv, gwo, gsg, gsu, gsd, geg, geu, ged,
+    wfinal, wfinal2, wofinal, dgu, sfin, sdfin, ddn, *refs
 ):
+    gwq, gwk, gwv, gwo, gsg, gsu, gsd, geg, geu, ged = refs
+
+    z = lax.axis_index("fsdp")
     f32, bf16 = jnp.float32, jnp.bfloat16
-    z = lax.axis_index("fsdp")
     hidden_dev = gsd.shape[0]
     sub = sfin.shape[2]
-    for n, ref in enumerate((gwq, gwk, gwv)):
-        for o in range(8):
-            ref[:, 128 * o : 128 * o + 128] = wfinal[o, :, 128 * n : 128 * n + 128].astype(f32)
-        for y in range(2):
-            lanes = slice(384 + 128 * n, 512 + 128 * n)
-            ref[:, 1024 + 128 * y : 1152 + 128 * y] = sum(
-                wfinal[4 * y + k, :, lanes].astype(f32) for k in range(4)
-            )
-    for i in range(5):
-        b = 5 * z + i
-
-        @pl.when(b < 16)
-        def _(b=b, i=i):
-            low = jnp.minimum(b, 15)
-            gwo[64 * i : 64 * i + 64] = wofinal[low // 2, low % 2].astype(f32)
-
-        @pl.when(b >= 16)
-        def _(b=b, i=i):
-            high = jnp.maximum(b, 16) - 16
-            gwo[64 * i : 64 * i + 64] = sum(
-                wofinal[4 * (high // 2) + k, 2 + high % 2].astype(f32) for k in range(4)
-            )
-
     units = geg.shape[2]
     for e in range(2):
         ged[e] = ddn[e, 0:hidden_dev]
@@ -1387,9 +1489,33 @@
                     shared[sub * j : sub * j + sub] = part
                 else:
                     shared[sub * j : sub * j + sub] += part
-
-
-def gather_stage(wfinal, wofinal, dgu, sfin, sdfin, ddn, hidden_dev):
+    for n, ref in enumerate((gwq, gwk, gwv)):
+        for o in range(8):
+            ref[:, 128 * o : 128 * o + 128] = wfinal[o, :, 128 * n : 128 * n + 128].astype(f32)
+        half = wfinal2.shape[1]
+        lanes = slice(128 * n, 128 * n + 128)
+        for y in range(2):
+            for k in range(2):
+                ref[half * k : half * k + half, 1024 + 128 * y : 1152 + 128 * y] = (
+                    wfinal2[4 * y + k, :, lanes].astype(f32) + wfinal2[4 * y + 2 + k, :, lanes].astype(f32)
+                )
+    for i in range(5):
+        b = 5 * z + i
+
+        @pl.when(b < 16)
+        def _(b=b, i=i):
+            low = jnp.minimum(b, 15)
+            gwo[64 * i : 64 * i + 64] = wofinal[low // 2, low % 2].astype(f32)
+
+        @pl.when(b >= 16)
+        def _(b=b, i=i):
+            high = jnp.maximum(b, 16) - 16
+            gwo[64 * i : 64 * i + 64] = sum(
+                wofinal[4 * (high // 2) + k, 2 + high % 2].astype(f32) for k in range(4)
+            )
+
+
+def gather_stage(wfinal, wfinal2, wofinal, dgu, sfin, sdfin, ddn, hidden_dev):
     width = wofinal.shape[3]
     shard = wfinal.shape[1]
     units = NZ * hidden_dev
@@ -1397,18 +1523,19 @@
     shape = jax.ShapeDtypeStruct
     vmem = pl.BlockSpec(memory_space=pltpu.VMEM)
     square = shape((shard, width), f32)
+    outs = [
+        square, square, square, square, shape((shard, units), f32), shape((shard, units), f32),
+        shape((hidden_dev, width), f32), shape((2, shard, units), f32), shape((2, shard, units), f32),
+        shape((2, hidden_dev, width), f32),
+    ]
     return pl.pallas_call(
         gather_kernel,
         name="assemble",
-        out_shape=[
-            square, square, square, square, shape((shard, units), f32), shape((shard, units), f32),
-            shape((hidden_dev, width), f32), shape((2, shard, units), f32), shape((2, shard, units), f32),
-            shape((2, hidden_dev, width), f32),
-        ],
-        in_specs=[vmem] * 6,
+        out_shape=outs,
+        in_specs=[vmem] * 7,
         out_specs=[vmem] * 10,
         compiler_params=pltpu.CompilerParams(vmem_limit_bytes=60 * MIB),
-    )(wfinal, wofinal, dgu, sfin, sdfin, ddn)
+    )(wfinal, wfinal2, wofinal, dgu, sfin, sdfin, ddn)
 
 
 def per_device_fast(
@@ -1456,13 +1583,13 @@
         )
     )
     kept = FRONT_OUT[5:19]
-    output_rows, grad_tokens, small, wfinal, wofinal, dgu, sfin, sdfin = backward_stage(
+    output_rows, grad_tokens, small, wfinal, wfinal2, wofinal, dgu, sfin, sdfin = backward_stage(
         *[front[n] for n in ("ypart", "accout", "dsgu", "dsdn", "db", "dg")], cotangent[0], tokens[0],
         *[front[n] for n in ("hidden", "tokens", "gates", "psum", "bound")], cosine_wide, sine_wide,
         *[front[n] for n in kept]
-    )[:8]
+    )[:9]
     gwq, gwk, gwv, gwo, gsg, gsu, gsd, geg, geu, ged = gather_stage(
-        wfinal, wofinal, dgu, sfin, sdfin, front["ddn"], hidden_dev
+        wfinal, wfinal2, wofinal, dgu, sfin, sdfin, front["ddn"], hidden_dev
     )
     mine = lax.dynamic_slice_in_dim(small, z * shard, shard, 1)
     return (

time: 537 us -> 517 us (0.963)
  Pallas kernels: 521 us -> 500 us
    pallas_call x1, Pallas kernels: 311 us -> 297 us  [front_stage(): pl.pallas_call(functools.partial(front_kernel, capacity), name='front', o...]
    pallas_call x1, Pallas kernels: 195 us -> 186 us  [backward_stage(): pl.pallas_call(backward_kernel, name='backward', out_shape=[shape((length...]
where the time goes in v4:
time: 517 us; the launch traced here: 510 us
  Pallas kernels  500 us (97%)
  local copies, waits for them, and re-layouts  8.67 us (2%)
    pallas_call x1, Pallas kernels, front_stage(): pl.pallas_call(functools.partial(front_kernel, capacity), name='front', o...  297 us
    pallas_call x1, Pallas kernels, backward_stage(): pl.pallas_call(backward_kernel, name='backward', out_shape=[shape((length...  186 us
    pallas_call x1, Pallas kernels, gather_stage(): pl.pallas_call(gather_kernel, name='assemble', out_shape=outs, in_specs=[...  16.5 us

profile of v4, /device:TPU:21, one launch (start us, length us, event | category | flops | bytes accessed | tf_op | source)
XLA Modules:
  0.0 510.1 jit_solution(14923190055819949505)
XLA Ops:
  0.6 1.4 copy.36.refs_1_
  2.1 1.4 copy.35
  3.5 0.7 broadcast_in_dim.15
  4.2 0.7 broadcast_in_dim.16
  4.9 0.1 pad.2.clone
  5.0 0.7 maximum_maximum_fusion.refs_2_
  5.6 297.0 %front.1 = (f32[128,1280]{1,0:T(8,128)}, bf16[128,1280]{1,0:T(8,128)(2,1)}, f32[16,128]{1,0:T(8,128)}, f32[32,1280]{1,0:T(8,128)}, f32[8,128]{1,0:T(8,128)}, /*i...) custom-call(bf16[128,1280]{1,0:T(8,128)(2,1)} %bitcast.8, ...), custom_call_target="tpu_custom_call" | custom-call | tf_op jit(solution)/shard_map/front/pallas_call | solution.py:937
  302.6 186.4 %backward.1 = (bf16[128,1280]{1,0:T(8,128)(2,1)}, bf16[128,1280]{1,0:T(8,128)(2,1)}, f32[32,1280]{1,0:T(8,128)}, bf16[8,320,384]{2,1,0:T(8,128)(2,1)}, bf16[8,16...) custom-call(bf16[4,512,1280]{2,1,0:T(8,128)(2,1)} %get-tuple-element, ...), custom_call_target="tpu_custom_call" | custom-call | tf_op jit(solution)/shard_map/backward/pallas_call | solution.py:1417
  489.0 0.0 copy-start.1
  489.1 0.0 copy-start
  489.1 16.5 %assemble.1 = (f32[320,1280]{1,0:T(8,128)}, f32[320,1280]{1,0:T(8,128)}, f32[320,1280]{1,0:T(8,128)}, f32[320,1280]{1,0:T(8,128)}, f32[320,896]{1,0:T(8,128)}, /...) custom-call(bf16[8,320,384]{2,1,0:T(8,128)(2,1)} %get-tuple-element., ...), custom_call_target="tpu_custom_call" | custom-call | tf_op jit(solution)/shard_map/assemble/pallas_call | solution.py:1531
  505.6 1.4 dynamic-slice_bitcast_fusion
  507.0 1.5 dynamic-slice_reduce_fusion
  508.5 0.0 copy-done.1
  508.5 0.7 copy.39
  509.2 0.0 copy-done
  509.2 0.7 copy.40
  (1 shorter events, 0.0 us)
Async XLA Ops:
  489.0 19.4 %copy-start.1 = (bf16[128,1280]{1,0:T(8,128)(2,1)S(1)}, bf16[128,1280]{1,0:T(8,128)(2,1)}, u32[]{:S(2)}) copy-start(bf16[128,1280]{1,0:T(8,128)(2,1)} %get-tuple-element.85) | copy-start | bytes 983044
  489.1 20.2 %copy-start = (bf16[128,1280]{1,0:T(8,128)(2,1)S(1)}, bf16[128,1280]{1,0:T(8,128)(2,1)}, u32[]{:S(2)}) copy-start(bf16[128,1280]{1,0:T(8,128)(2,1)} %get-tuple-element.86) | copy-start | bytes 983044
